TPU v7x, 128 devices: a whole 4x4x4 slice. The times are simulated.
128 devices in a mesh: gz: 8 (over y, z_hi), gy: 4 (over z_lo, core), gx: 4 (over x).
Axes of the slice: x: 4, y: 4, z: 4 (z_hi: 2, z_lo: 2; z = z_hi * 2 + z_lo), core: 2. Of those that a mesh axis runs over, the one named last changes fastest.
Arguments:
- e_start: float32 [3, 64, 128, 512], P(None, 'gz', 'gy', 'gx'), may hold values from -6 to 6
- h_start: float32 [3, 64, 128, 512], P(None, 'gz', 'gy', 'gx'), may hold values from -6 to 6
- adjoint_e: float32 [3, 64, 128, 512], P(None, 'gz', 'gy', 'gx'), may hold values from -6 to 6
- adjoint_h: float32 [3, 64, 128, 512], P(None, 'gz', 'gy', 'gx'), may hold values from -6 to 6
- permittivity: float32 [64, 128, 512], P('gz', 'gy', 'gx'), may hold values from 1 to 4
- current: float32 [64, 128, 512], P('gz', 'gy', 'gx'), may hold values from -6 to 6
- layer_of_cell: int32 [64], P('gz'), may hold values from 0 to 15, as said below
- pml_cells: int32 [3], replicated, may hold values from 4 to 8
- start_step: int32 [1], replicated, may hold values from 0 to 99999
Outputs:
- gradient: float32 [16, 128, 512], P('gz', 'gy', 'gx')
- adjoint_e_out: float32 [3, 64, 128, 512], P(None, 'gz', 'gy', 'gx')
- adjoint_h_out: float32 [3, 64, 128, 512], P(None, 'gz', 'gy', 'gx')
Inputs may be any that keep to these rules, and one draw needn't show every extreme that they name: `layer_of_cell`: every aligned block of 16 consecutive z planes holds each layer exactly once.
All inputs are finite; a program needn't handle non-finite values.
Results may differ from a plain program's by a relative error of at most 0.00011.
Values sent between devices are 32-bit elements; how exact they have to be, the bound alone decides.
No kernel may reach another device: no remote copies, remote signals or barrier semaphores. Data moves between devices by JAX's collectives and lax.ppermute only.
A program may use at most 128 MiB of HBM per device.

v0:
```python
import math

import jax
import jax.numpy as jnp
from jax import lax
from jax.sharding import PartitionSpec as P

LAY_DEV = 2


time_step = 0.5
sigma_peak = 0.8
period_steps = 64


def with_halo(value, sides, width):
    for axis, dim in sides:
        count, length = (lax.axis_size(axis), value.shape[dim])
        up = [(i, (i + 1) % count) for i in range(count - 1)]
        down = [(j, i) for i, j in up]
        last = lax.slice_in_dim(value, length - width, length, axis=dim)
        leading = lax.slice_in_dim(value, 0, width, axis=dim)
        before = lax.ppermute(last, axis, up)
        after = lax.ppermute(leading, axis, down)
        value = jnp.concatenate([before, value, after], axis=dim)
    return value


def profile(positions, extent, thickness):
    distance = jnp.minimum(positions, extent - 1 - positions)
    depth = jnp.maximum(thickness - distance, 0).astype(jnp.float32) / thickness.astype(jnp.float32)
    return sigma_peak * depth * depth


def magnetic_coeffs(sigma):
    half_loss = sigma * (time_step * 0.5)
    return ((1.0 - half_loss) / (1.0 + half_loss), time_step / (1.0 + half_loss))


def electric_coeffs(sigma, permittivity):
    half_loss = sigma * time_step / (2.0 * permittivity)
    return ((1.0 - half_loss) / (1.0 + half_loss), time_step / (permittivity * (1.0 + half_loss)))


def plain_diff(values, along):
    extent = values.shape[along]
    return lax.slice_in_dim(values, 1, extent, axis=along) - lax.slice_in_dim(
        values, 0, extent - 1, axis=along
    )


def next_with_rim(values, along):
    result = plain_diff(values, along)
    for other in range(3):
        if other != along:
            result = lax.slice_in_dim(result, 0, result.shape[other] - 1, axis=other)
    return result


def prev_on_block(values, along):
    result = plain_diff(values, along)
    for other in range(3):
        if other != along:
            result = lax.slice_in_dim(result, 1, result.shape[other], axis=other)
    return result


def local_update(padded, coeffs, drive):
    mag_keep, mag_scale, ele_keep, ele_scale = coeffs
    e_padded = padded[:3]
    h_padded = padded[3:]
    curl_e = jnp.stack(
        [
            next_with_rim(e_padded[2], 1) - next_with_rim(e_padded[1], 0),
            next_with_rim(e_padded[0], 0) - next_with_rim(e_padded[2], 2),
            next_with_rim(e_padded[1], 2) - next_with_rim(e_padded[0], 1),
        ]
    )
    h_next = mag_keep * h_padded[:, :-1, :-1, :-1] - mag_scale * curl_e
    curl_h = jnp.stack(
        [
            prev_on_block(h_next[2], 1) - prev_on_block(h_next[1], 0),
            prev_on_block(h_next[0], 0) - prev_on_block(h_next[2], 2),
            prev_on_block(h_next[1], 2) - prev_on_block(h_next[0], 1),
        ]
    )
    curl_h = jnp.stack([curl_h[0], curl_h[1], curl_h[2] - drive])
    e_next = ele_keep * e_padded[:, 1:-1, 1:-1, 1:-1] + ele_scale * curl_h
    return (e_next, h_next[:, 1:, 1:, 1:])


def inner(first_field, second_field):
    return (
        first_field[0] * second_field[0]
        + first_field[1] * second_field[1]
        + first_field[2] * second_field[2]
    )


def lower_guard(cells, index_now):
    return jnp.where(
        (jnp.arange(cells + 1, dtype=jnp.int32) == 0) & (index_now == 0), 0.0, 1.0
    ).astype(jnp.float32)


def local(
    e_start,
    h_start,
    adjoint_e,
    adjoint_h,
    permittivity,
    current,
    layer_of_cell,
    pml_cells,
    start_step,
):
    depth_z, rows_y, cols_x = permittivity.shape
    index_z = lax.axis_index("gz")
    index_y = lax.axis_index("gy")
    index_x = lax.axis_index("gx")
    extent_z = depth_z * lax.axis_size("gz")
    extent_y = rows_y * lax.axis_size("gy")
    extent_x = cols_x * lax.axis_size("gx")
    own_z = index_z * depth_z + jnp.arange(depth_z, dtype=jnp.int32)
    own_y = index_y * rows_y + jnp.arange(rows_y, dtype=jnp.int32)
    own_x = index_x * cols_x + jnp.arange(cols_x, dtype=jnp.int32)
    sigma_own = (
        profile(own_z, extent_z, pml_cells[0])[:, None, None]
        + profile(own_y, extent_y, pml_cells[1])[None, :, None]
        + profile(own_x, extent_x, pml_cells[2])[None, None, :]
    )
    ele_keep, ele_scale = electric_coeffs(sigma_own, permittivity)
    drives = []
    for offset in (1, 2):
        phase = ((start_step[0] + offset) % period_steps).astype(jnp.float32) * (
            2.0 * math.pi / period_steps
        )
        drives.append(current * jnp.sin(phase))
    no_drive = jnp.zeros_like(current)
    rim_z = index_z * depth_z - 1 + jnp.arange(depth_z + 1, dtype=jnp.int32)
    rim_y = index_y * rows_y - 1 + jnp.arange(rows_y + 1, dtype=jnp.int32)
    rim_x = index_x * cols_x - 1 + jnp.arange(cols_x + 1, dtype=jnp.int32)
    sigma_rim = (
        profile(rim_z, extent_z, pml_cells[0])[:, None, None]
        + profile(rim_y, extent_y, pml_cells[1])[None, :, None]
        + profile(rim_x, extent_x, pml_cells[2])[None, None, :]
    )
    guard = (
        lower_guard(depth_z, index_z)[:, None, None]
        * lower_guard(rows_y, index_y)[None, :, None]
        * lower_guard(cols_x, index_x)[None, None, :]
    )
    rim_keep, rim_scale = magnetic_coeffs(sigma_rim)
    coeffs = (rim_keep * guard, rim_scale * guard, ele_keep, ele_scale)

    def step_runs(e_runs, h_runs, drive_runs):
        padded = with_halo(
            jnp.concatenate((e_runs, h_runs), axis=1), (("gz", 2), ("gy", 3), ("gx", 4)), 1
        )
        e_next, h_next = local_update(padded[0], coeffs, drive_runs[0])
        e_list = [e_next]
        h_list = [h_next]
        return (jnp.stack(e_list), jnp.stack(h_list))

    e_runs, h_runs = step_runs(e_start[None], h_start[None], drives[0][None])
    e_one = e_runs[0]
    e_runs, h_runs = step_runs(e_runs, h_runs, drives[1][None])
    e_two = e_runs[0]
    lam_runs, lam_h_runs = step_runs(adjoint_e[None], adjoint_h[None], no_drive[None])
    lam_e_one = lam_runs[0]
    lam_runs, lam_h_runs = step_runs(lam_runs, lam_h_runs, no_drive[None])
    lam_e_zero, lam_h_zero = (lam_runs[0], lam_h_runs[0])
    density = inner(e_start, lam_e_zero) + inner(e_one, lam_e_one) + inner(e_two, adjoint_e)
    flat_density = density.reshape(depth_z, rows_y * cols_x)
    layer_rows = lax.iota(jnp.int32, LAY_DEV * lax.axis_size("gz"))
    onehot = (layer_rows[:, None] == layer_of_cell[None, :]).astype(jnp.float32)
    summed = jnp.dot(onehot, flat_density, precision=lax.Precision.HIGHEST)
    gradient = lax.psum_scatter(
        summed.reshape(LAY_DEV * lax.axis_size("gz"), rows_y, cols_x),
        "gz",
        scatter_dimension=0,
        tiled=True,
    )
    return (gradient, lam_e_zero, lam_h_zero)


def solution(mesh):
    return jax.shard_map(
        local,
        mesh=mesh,
        in_specs=(
            P(None, "gz", "gy", "gx"),
            P(None, "gz", "gy", "gx"),
            P(None, "gz", "gy", "gx"),
            P(None, "gz", "gy", "gx"),
            P("gz", "gy", "gx"),
            P("gz", "gy", "gx"),
            P("gz"),
            P(),
            P(),
        ),
        out_specs=(P("gz", "gy", "gx"), P(None, "gz", "gy", "gx"), P(None, "gz", "gy", "gx")),
        check_vma=False,
    )
```

profile of v0, /device:TPU:0, one launch (start us, length us, event | category | flops | bytes accessed | tf_op | source)
XLA Modules:
  0.0 324.0 jit_solution(6975959987397547904)
XLA Ops:
  8.8 6.5 %collective-permute-start.12 = (f32[1,6,1,32,128]{4,3,2,1,0:T(8,128)}, f32[1,6,1,32,128]{4,3,2,1,0:T(8,128)}, u32[]{:S(2)}, u32[]{:S(2)}) collective-permute-start(f32[1,6,1,32,128]{4,3,2,1,0:T(8,128)} %get-tuple-element.92), channel_id=1, source_target_pairs={{0,16},{16,32},{32,48},{48,64},{64,80},{80,96},{96,112},{1,17},{17... | collective-permute-start | bytes 294920 | tf_op jit(solution)/shard_map/ppermute | solution.py:23
  18.2 6.7 %collective-permute-start = (f32[1,6,1,32,128]{4,3,2,1,0:T(8,128)}, f32[1,6,1,32,128]{4,3,2,1,0:T(8,128)}, u32[]{:S(2)}, u32[]{:S(2)}) collective-permute-start(f32[1,6,1,32,128]{4,3,2,1,0:T(8,128)} %get-tuple-element.88), channel_id=1, source_target_pairs={{0,16},{16,32},{32,48},{48,64},{64,80},{80,96},{96,112},{1,17},{17... | collective-permute-start | bytes 294920 | tf_op jit(solution)/shard_map/ppermute | solution.py:23
  36.6 2.0 copy.150
  45.4 3.6 %copy.148 = f32[1,6,10,32,128]{3,4,2,1,0:T(8,128)} copy(f32[1,6,10,32,128]{4,3,2,1,0:T(8,128)} %copy-done.37) | data formatting | bytes 1966080 | tf_op jit(solution)/shard_map/concatenate | solution.py:25
  49.0 3.6 %copy.137 = f32[1,6,10,32,128]{3,4,2,1,0:T(8,128)} copy(f32[1,6,10,32,128]{4,3,2,1,0:T(8,128)} %copy-done.36) | data formatting | bytes 1966080 | tf_op jit(solution)/shard_map/concatenate | solution.py:25
  52.6 4.3 %collective-permute-start.14 = (f32[1,6,10,1,128]{4,3,2,1,0:T(1,128)S(1)}, f32[1,6,10,1,128]{4,3,2,1,0:T(1,128)S(1)}, u32[]{:S(2)}, u32[]{:S(2)}) collective-permute-start(f32[1,6,10,1,128]{4,3,2,1,0:T(1,128)S(1)} %get-tuple-element.84), channel_id=1, source_target_pairs={{0,4},{4,8},{8,12},{1,5},{5,9},{9,13},{2,6},{6,10},{10,14},{3,7},{... | collective-permute-start | bytes 92168 | tf_op jit(solution)/shard_map/ppermute | solution.py:23
  58.2 2.6 copy.136
  60.8 2.5 copy.138
  65.1 3.4 %collective-permute-start.4 = (f32[1,6,10,34,1]{3,4,2,1,0:T(1,128)S(1)}, f32[1,6,10,34,1]{3,4,2,1,0:T(1,128)S(1)}, u32[]{:S(2)}, u32[]{:S(2)}) collective-permute-start(f32[1,6,10,34,1]{3,4,2,1,0:T(1,128)S(1)} %get-tuple-element.20), channel_id=1, source_target_pairs={{0,1},{1,2},{2,3},{4,5},{5,6},{6,7},{8,9},{9,10},{10,11},{12,13},{... | collective-permute-start | bytes 24488 | tf_op jit(solution)/shard_map/ppermute | solution.py:23
  69.8 2.6 copy.147
  72.4 2.5 copy.149
  74.9 1.9 pad_maximum_fusion.21
  76.9 4.8 %collective-permute-start.16 = (f32[1,6,10,34,1]{3,4,2,1,0:T(1,128)S(1)}, f32[1,6,10,34,1]{3,4,2,1,0:T(1,128)S(1)}, u32[]{:S(2)}, u32[]{:S(2)}) collective-permute-start(f32[1,6,10,34,1]{3,4,2,1,0:T(1,128)S(1)} %get-tuple-element.24), channel_id=1, source_target_pairs={{0,1},{1,2},{2,3},{4,5},{5,6},{6,7},{8,9},{9,10},{10,11},{12,13},{... | collective-permute-start | bytes 24488 | tf_op jit(solution)/shard_map/ppermute | solution.py:23
  83.5 2.5 pad_maximum_fusion
  93.1 2.4 pad_maximum_fusion.2
  97.6 2.4 slice_bitcast_fusion.3
  100.0 2.0 fusion.120
  107.5 2.0 copy.140
  111.5 6.7 %collective-permute-start.6 = (f32[1,6,1,32,128]{4,3,2,1,0:T(8,128)S(1)}, f32[1,6,1,32,128]{4,3,2,1,0:T(8,128)S(1)}, u32[]{:S(2)}, u32[]{:S(2)}) collective-permute-start(f32[1,6,1,32,128]{4,3,2,1,0:T(8,128)S(1)} %get-tuple-element.86), channel_id=1, source_target_pairs={{0,16},{16,32},{32,48},{48,64},{64,80},{80,96},{96,112},{1,17},{17... | collective-permute-start | bytes 294920 | tf_op jit(solution)/shard_map/ppermute | solution.py:23
  119.5 2.6 fusion.16
  122.1 2.7 fusion.21
  124.8 2.2 collective-permute-done.7
  127.1 2.0 collective-permute-start.8
  131.4 2.6 copy.143
  134.0 2.6 copy.142
  136.6 2.6 copy.144
  139.2 1.9 pad_maximum_fusion.24
  141.2 5.1 %collective-permute-start.10 = (f32[1,6,10,34,1]{3,4,2,1,0:T(1,128)S(1)}, f32[1,6,10,34,1]{3,4,2,1,0:T(1,128)S(1)}, u32[]{:S(2)}, u32[]{:S(2)}) collective-permute-start(f32[1,6,10,34,1]{3,4,2,1,0:T(1,128)S(1)} %get-tuple-element.18), channel_id=1, source_target_pairs={{0,1},{1,2},{2,3},{4,5},{5,6},{6,7},{8,9},{9,10},{10,11},{12,13},{... | collective-permute-start | bytes 24488 | tf_op jit(solution)/shard_map/ppermute | solution.py:23
  149.0 3.1 collective-permute-done.11
  152.1 2.5 pad_maximum_fusion.1
  165.6 2.1 fusion.6
  167.7 2.6 copy.151
  170.3 2.6 copy.152
  173.9 4.5 %collective-permute-start.18 = (f32[1,6,1,32,128]{4,3,2,1,0:T(8,128)S(1)}, f32[1,6,1,32,128]{4,3,2,1,0:T(8,128)S(1)}, u32[]{:S(2)}, u32[]{:S(2)}) collective-permute-start(f32[1,6,1,32,128]{4,3,2,1,0:T(8,128)S(1)} %get-tuple-element.90), channel_id=1, source_target_pairs={{0,16},{16,32},{32,48},{48,64},{64,80},{80,96},{96,112},{1,17},{17... | collective-permute-start | bytes 294920 | tf_op jit(solution)/shard_map/ppermute | solution.py:23
  181.4 4.9 %collective-permute-done.19 = f32[1,6,1,32,128]{4,3,2,1,0:T(8,128)S(1)} collective-permute-done((f32[1,6,1,32,128]{4,3,2,1,0:T(8,128)S(1)}, f32[1,6,1,32,128]{4,3,2,1,0:T(8,128)S(1)}, u32[]{:S(2)}, u32[]{:S(2)}) %collective-permute-start.19) | collective-permute-done | bytes 98336 | tf_op jit(solution)/shard_map/ppermute | solution.py:24
  188.0 3.1 collective-permute-start.20
  193.3 1.9 copy.164
  197.1 1.9 copy.166
  199.0 1.9 copy.167
  200.9 1.9 copy.168
  204.7 3.6 %copy.154 = f32[1,6,10,32,128]{3,4,2,1,0:T(8,128)} copy(f32[1,6,10,32,128]{4,3,2,1,0:T(8,128)} %copy-done.35) | data formatting | bytes 1966080 | tf_op jit(solution)/shard_map/concatenate | solution.py:25
  208.3 2.6 copy.153
  210.9 2.6 copy.155
  213.5 1.9 pad_maximum_fusion.18
  215.4 3.7 %collective-permute-start.22 = (f32[1,6,10,34,1]{3,4,2,1,0:T(1,128)S(1)}, f32[1,6,10,34,1]{3,4,2,1,0:T(1,128)S(1)}, u32[]{:S(2)}, u32[]{:S(2)}) collective-permute-start(f32[1,6,10,34,1]{3,4,2,1,0:T(1,128)S(1)} %get-tuple-element.22), channel_id=1, source_target_pairs={{0,1},{1,2},{2,3},{4,5},{5,6},{6,7},{8,9},{9,10},{10,11},{12,13},{... | collective-permute-start | bytes 24488 | tf_op jit(solution)/shard_map/ppermute | solution.py:23
  222.6 2.5 collective-permute-done.23
  225.2 2.5 pad_maximum_fusion.3
  243.9 73.0 %reduce-scatter.2.cloned.1.call-done = f32[2,32,128]{2,1,0:T(8,128)} async-done(((f32[16,32,128]{2,1,0:T(8,128)}), f32[2,32,128]{2,1,0:T(8,128)}) %reduce-scatter.2.cloned.1.call-update) | async-done | bytes 32784 | tf_op jit(solution)/shard_map/reduce_scatter | solution.py:178
  (273 shorter events, 91.2 us)
Async XLA Ops:
  7.2 19.0 %copy-start.59 = (s32[3]{0:T(128)S(1)}, s32[3]{0:T(128)}, u32[]{:S(2)}) copy-start(s32[3]{0:T(128)} %param.16) | copy-start | bytes 40
  7.2 26.2 %copy-start.58 = (f32[8,32,128]{2,1,0:T(8,128)S(1)}, f32[8,32,128]{2,1,0:T(8,128)}, u32[]{:S(2)}) copy-start(f32[8,32,128]{2,1,0:T(8,128)} %param.13) | copy-start | bytes 393220
  7.2 309.7 %reduce-scatter.2.cloned.1.call-start = ((), (), s32[]{:S(2)}) async-start(), calls=%async_computation.1 | async-start | bytes 294912 | tf_op jit(solution)/shard_map/reduce_scatter | solution.py:178
  8.8 34.5 %collective-permute-start.12 = (f32[1,6,1,32,128]{4,3,2,1,0:T(8,128)}, f32[1,6,1,32,128]{4,3,2,1,0:T(8,128)}, u32[]{:S(2)}, u32[]{:S(2)}) collective-permute-start(f32[1,6,1,32,128]{4,3,2,1,0:T(8,128)} %get-tuple-element.92), channel_id=1, source_target_pairs={{0,16},{16,32},{32,48},{48,64},{64,80},{80,96},{96,112},{1,17},{17... | collective-permute-start | bytes 294920 | tf_op jit(solution)/shard_map/ppermute | solution.py:23
  15.3 28.0 %collective-permute-start.13 = (f32[1,6,1,32,128]{4,3,2,1,0:T(8,128)}, f32[1,6,1,32,128]{4,3,2,1,0:T(8,128)}, u32[]{:S(2)}, u32[]{:S(2)}) collective-permute-start(f32[1,6,1,32,128]{4,3,2,1,0:T(8,128)} %get-tuple-element.93), channel_id=1, source_target_pairs={{16,0},{32,16},{48,32},{64,48},{80,64},{96,80},{112,96},{17,1},{33... | collective-permute-start | bytes 294920 | tf_op jit(solution)/shard_map/ppermute | solution.py:24
  18.2 20.4 %collective-permute-start = (f32[1,6,1,32,128]{4,3,2,1,0:T(8,128)}, f32[1,6,1,32,128]{4,3,2,1,0:T(8,128)}, u32[]{:S(2)}, u32[]{:S(2)}) collective-permute-start(f32[1,6,1,32,128]{4,3,2,1,0:T(8,128)} %get-tuple-element.88), channel_id=1, source_target_pairs={{0,16},{16,32},{32,48},{48,64},{64,80},{80,96},{96,112},{1,17},{17... | collective-permute-start | bytes 294920 | tf_op jit(solution)/shard_map/ppermute | solution.py:23
  24.9 13.8 %collective-permute-start.1 = (f32[1,6,1,32,128]{4,3,2,1,0:T(8,128)}, f32[1,6,1,32,128]{4,3,2,1,0:T(8,128)}, u32[]{:S(2)}, u32[]{:S(2)}) collective-permute-start(f32[1,6,1,32,128]{4,3,2,1,0:T(8,128)} %get-tuple-element.89), channel_id=1, source_target_pairs={{16,0},{32,16},{48,32},{64,48},{80,64},{96,80},{112,96},{17,1},{33... | collective-permute-start | bytes 294920 | tf_op jit(solution)/shard_map/ppermute | solution.py:24
  27.5 11.1 %copy-start.39 = (f32[3,8,32,128]{3,2,1,0:T(8,128)S(1)}, f32[3,8,32,128]{3,2,1,0:T(8,128)}, u32[]{:S(2)}) copy-start(f32[3,8,32,128]{3,2,1,0:T(8,128)} %param.11) | copy-start | bytes 1179652
  27.5 11.1 %copy-start.56 = (f32[3,8,32,128]{3,2,1,0:T(8,128)S(1)}, f32[3,8,32,128]{3,2,1,0:T(8,128)}, u32[]{:S(2)}) copy-start(f32[3,8,32,128]{3,2,1,0:T(8,128)} %param.12) | copy-start | bytes 1179652
  33.4 122.8 %copy-start.22 = (f32[9,33,129]{1,2,0:T(8,128)}, f32[9,33,129]{1,2,0:T(8,128)S(1)}, u32[]{:S(2)}) copy-start(f32[9,33,129]{1,2,0:T(8,128)S(1)} %get-tuple-element.166) | copy-start | bytes 459760
  33.4 122.8 %copy-start.24 = (f32[9,33,129]{1,2,0:T(8,128)}, f32[9,33,129]{1,2,0:T(8,128)S(1)}, u32[]{:S(2)}) copy-start(f32[9,33,129]{1,2,0:T(8,128)S(1)} %get-tuple-element.167) | copy-start | bytes 459760
  35.0 8.4 %copy-start.38 = (f32[3,8,32,128]{3,2,1,0:T(8,128)S(1)}, f32[3,8,32,128]{3,2,1,0:T(8,128)}, u32[]{:S(2)}) copy-start(f32[3,8,32,128]{3,2,1,0:T(8,128)} %param.9) | copy-start | bytes 1179652
  35.2 69.8 %copy-start.16 = (f32[8,32,128]{1,2,0:T(8,128)}, f32[8,32,128]{1,2,0:T(8,128)S(1)}, u32[]{:S(2)}) copy-start(f32[8,32,128]{1,2,0:T(8,128)S(1)} %copy.135) | copy-start | bytes 393220
  36.5 68.6 %copy-start.19 = (f32[8,32,128]{1,2,0:T(8,128)}, f32[8,32,128]{1,2,0:T(8,128)S(1)}, u32[]{:S(2)}) copy-start(f32[8,32,128]{1,2,0:T(8,128)S(1)} %copy.139) | copy-start | bytes 393220
  40.8 17.4 %collective-permute-start.2 = (f32[1,6,10,1,128]{4,3,2,1,0:T(1,128)S(1)}, f32[1,6,10,1,128]{4,3,2,1,0:T(1,128)S(1)}, u32[]{:S(2)}, u32[]{:S(2)}) collective-permute-start(f32[1,6,10,1,128]{4,3,2,1,0:T(1,128)S(1)} %get-tuple-element.80), channel_id=1, source_target_pairs={{0,4},{4,8},{8,12},{1,5},{5,9},{9,13},{2,6},{6,10},{10,14},{3,7},{... | collective-permute-start | bytes 92168 | tf_op jit(solution)/shard_map/ppermute | solution.py:23
  42.1 18.7 %collective-permute-start.3 = (f32[1,6,10,1,128]{4,3,2,1,0:T(1,128)S(1)}, f32[1,6,10,1,128]{4,3,2,1,0:T(1,128)S(1)}, u32[]{:S(2)}, u32[]{:S(2)}) collective-permute-start(f32[1,6,10,1,128]{4,3,2,1,0:T(1,128)S(1)} %get-tuple-element.81), channel_id=1, source_target_pairs={{4,0},{8,4},{12,8},{5,1},{9,5},{13,9},{6,2},{10,6},{14,10},{7,3},{... | collective-permute-start | bytes 92168 | tf_op jit(solution)/shard_map/ppermute | solution.py:24
  52.6 17.2 %collective-permute-start.14 = (f32[1,6,10,1,128]{4,3,2,1,0:T(1,128)S(1)}, f32[1,6,10,1,128]{4,3,2,1,0:T(1,128)S(1)}, u32[]{:S(2)}, u32[]{:S(2)}) collective-permute-start(f32[1,6,10,1,128]{4,3,2,1,0:T(1,128)S(1)} %get-tuple-element.84), channel_id=1, source_target_pairs={{0,4},{4,8},{8,12},{1,5},{5,9},{9,13},{2,6},{6,10},{10,14},{3,7},{... | collective-permute-start | bytes 92168 | tf_op jit(solution)/shard_map/ppermute | solution.py:23
  56.9 15.5 %collective-permute-start.15 = (f32[1,6,10,1,128]{4,3,2,1,0:T(1,128)S(1)}, f32[1,6,10,1,128]{4,3,2,1,0:T(1,128)S(1)}, u32[]{:S(2)}, u32[]{:S(2)}) collective-permute-start(f32[1,6,10,1,128]{4,3,2,1,0:T(1,128)S(1)} %get-tuple-element.85), channel_id=1, source_target_pairs={{4,0},{8,4},{12,8},{5,1},{9,5},{13,9},{6,2},{10,6},{14,10},{7,3},{... | collective-permute-start | bytes 92168 | tf_op jit(solution)/shard_map/ppermute | solution.py:24
  65.1 18.4 %collective-permute-start.4 = (f32[1,6,10,34,1]{3,4,2,1,0:T(1,128)S(1)}, f32[1,6,10,34,1]{3,4,2,1,0:T(1,128)S(1)}, u32[]{:S(2)}, u32[]{:S(2)}) collective-permute-start(f32[1,6,10,34,1]{3,4,2,1,0:T(1,128)S(1)} %get-tuple-element.20), channel_id=1, source_target_pairs={{0,1},{1,2},{2,3},{4,5},{5,6},{6,7},{8,9},{9,10},{10,11},{12,13},{... | collective-permute-start | bytes 24488 | tf_op jit(solution)/shard_map/ppermute | solution.py:23
  68.5 15.0 %collective-permute-start.5 = (f32[1,6,10,34,1]{3,4,2,1,0:T(1,128)S(1)}, f32[1,6,10,34,1]{3,4,2,1,0:T(1,128)S(1)}, u32[]{:S(2)}, u32[]{:S(2)}) collective-permute-start(f32[1,6,10,34,1]{3,4,2,1,0:T(1,128)S(1)} %get-tuple-element.21), channel_id=1, source_target_pairs={{1,0},{2,1},{3,2},{5,4},{6,5},{7,6},{9,8},{10,9},{11,10},{13,12},{... | collective-permute-start | bytes 24488 | tf_op jit(solution)/shard_map/ppermute | solution.py:24
  74.9 8.6 %copy-start.4 = (f32[1,6,10,32,128]{3,4,2,1,0:T(8,128)S(1)}, f32[1,6,10,32,128]{3,4,2,1,0:T(8,128)}, u32[]{:S(2)}) copy-start(f32[1,6,10,32,128]{3,4,2,1,0:T(8,128)} %copy.137) | copy-start | bytes 2949124
  74.9 8.6 %copy-start.5 = (f32[1,6,10,1,128]{3,4,2,1,0:T(8,128)S(1)}, f32[1,6,10,1,128]{3,4,2,1,0:T(8,128)}, u32[]{:S(2)}) copy-start(f32[1,6,10,1,128]{3,4,2,1,0:T(8,128)} %copy.136) | copy-start | bytes 92164
  74.9 8.6 %copy-start.6 = (f32[1,6,10,1,128]{3,4,2,1,0:T(8,128)S(1)}, f32[1,6,10,1,128]{3,4,2,1,0:T(8,128)}, u32[]{:S(2)}) copy-start(f32[1,6,10,1,128]{3,4,2,1,0:T(8,128)} %copy.138) | copy-start | bytes 92164
  76.9 13.3 %collective-permute-start.16 = (f32[1,6,10,34,1]{3,4,2,1,0:T(1,128)S(1)}, f32[1,6,10,34,1]{3,4,2,1,0:T(1,128)S(1)}, u32[]{:S(2)}, u32[]{:S(2)}) collective-permute-start(f32[1,6,10,34,1]{3,4,2,1,0:T(1,128)S(1)} %get-tuple-element.24), channel_id=1, source_target_pairs={{0,1},{1,2},{2,3},{4,5},{5,6},{6,7},{8,9},{9,10},{10,11},{12,13},{... | collective-permute-start | bytes 24488 | tf_op jit(solution)/shard_map/ppermute | solution.py:23
  81.7 8.5 %collective-permute-start.17 = (f32[1,6,10,34,1]{3,4,2,1,0:T(1,128)S(1)}, f32[1,6,10,34,1]{3,4,2,1,0:T(1,128)S(1)}, u32[]{:S(2)}, u32[]{:S(2)}) collective-permute-start(f32[1,6,10,34,1]{3,4,2,1,0:T(1,128)S(1)} %get-tuple-element.25), channel_id=1, source_target_pairs={{1,0},{2,1},{3,2},{5,4},{6,5},{7,6},{9,8},{10,9},{11,10},{13,12},{... | collective-permute-start | bytes 24488 | tf_op jit(solution)/shard_map/ppermute | solution.py:24
  86.5 18.5 %copy-start.14 = (f32[3,10,34,130]{2,3,1,0:T(8,128)}, f32[3,10,34,130]{2,3,1,0:T(8,128)S(1)}, u32[]{:S(2)}) copy-start(f32[3,10,34,130]{2,3,1,0:T(8,128)S(1)} %get-tuple-element.39) | copy-start | bytes 1591204
  111.5 13.2 %collective-permute-start.6 = (f32[1,6,1,32,128]{4,3,2,1,0:T(8,128)S(1)}, f32[1,6,1,32,128]{4,3,2,1,0:T(8,128)S(1)}, u32[]{:S(2)}, u32[]{:S(2)}) collective-permute-start(f32[1,6,1,32,128]{4,3,2,1,0:T(8,128)S(1)} %get-tuple-element.86), channel_id=1, source_target_pairs={{0,16},{16,32},{32,48},{48,64},{64,80},{80,96},{96,112},{1,17},{17... | collective-permute-start | bytes 294920 | tf_op jit(solution)/shard_map/ppermute | solution.py:23
  118.2 8.8 %collective-permute-start.7 = (f32[1,6,1,32,128]{4,3,2,1,0:T(8,128)S(1)}, f32[1,6,1,32,128]{4,3,2,1,0:T(8,128)S(1)}, u32[]{:S(2)}, u32[]{:S(2)}) collective-permute-start(f32[1,6,1,32,128]{4,3,2,1,0:T(8,128)S(1)} %get-tuple-element.87), channel_id=1, source_target_pairs={{16,0},{32,16},{48,32},{64,48},{80,64},{96,80},{112,96},{17,1},{33... | collective-permute-start | bytes 294920 | tf_op jit(solution)/shard_map/ppermute | solution.py:24
  127.1 6.9 %collective-permute-start.8 = (f32[1,6,10,1,128]{4,3,2,1,0:T(1,128)S(1)}, f32[1,6,10,1,128]{4,3,2,1,0:T(1,128)S(1)}, u32[]{:S(2)}, u32[]{:S(2)}) collective-permute-start(f32[1,6,10,1,128]{4,3,2,1,0:T(1,128)S(1)} %get-tuple-element.78), channel_id=1, source_target_pairs={{0,4},{4,8},{8,12},{1,5},{5,9},{9,13},{2,6},{6,10},{10,14},{3,7},{... | collective-permute-start | bytes 92168 | tf_op jit(solution)/shard_map/ppermute | solution.py:23
  129.2 7.5 %collective-permute-start.9 = (f32[1,6,10,1,128]{4,3,2,1,0:T(1,128)S(1)}, f32[1,6,10,1,128]{4,3,2,1,0:T(1,128)S(1)}, u32[]{:S(2)}, u32[]{:S(2)}) collective-permute-start(f32[1,6,10,1,128]{4,3,2,1,0:T(1,128)S(1)} %get-tuple-element.79), channel_id=1, source_target_pairs={{4,0},{8,4},{12,8},{5,1},{9,5},{13,9},{6,2},{10,6},{14,10},{7,3},{... | collective-permute-start | bytes 92168 | tf_op jit(solution)/shard_map/ppermute | solution.py:24
  136.6 11.1 %copy-start.44 = (f32[10,34,129]{1,2,0:T(8,128)S(1)}, f32[10,34,129]{1,2,0:T(8,128)}, u32[]{:S(2)}) copy-start(f32[10,34,129]{1,2,0:T(8,128)} %get-tuple-element.120) | copy-start | bytes 526324
  136.6 11.1 %copy-start.45 = (f32[10,34,129]{1,2,0:T(8,128)S(1)}, f32[10,34,129]{1,2,0:T(8,128)}, u32[]{:S(2)}) copy-start(f32[10,34,129]{1,2,0:T(8,128)} %get-tuple-element.121) | copy-start | bytes 526324
  139.2 12.8 %copy-start.7 = (f32[1,6,10,32,128]{3,4,2,1,0:T(8,128)S(1)}, f32[1,6,10,32,128]{3,4,2,1,0:T(8,128)}, u32[]{:S(2)}) copy-start(f32[1,6,10,32,128]{3,4,2,1,0:T(8,128)} %copy.143) | copy-start | bytes 2949124
  139.2 12.8 %copy-start.9 = (f32[1,6,10,1,128]{3,4,2,1,0:T(8,128)S(1)}, f32[1,6,10,1,128]{3,4,2,1,0:T(8,128)}, u32[]{:S(2)}) copy-start(f32[1,6,10,1,128]{3,4,2,1,0:T(8,128)} %copy.142) | copy-start | bytes 92164
  139.2 12.8 %copy-start.11 = (f32[1,6,10,1,128]{3,4,2,1,0:T(8,128)S(1)}, f32[1,6,10,1,128]{3,4,2,1,0:T(8,128)}, u32[]{:S(2)}) copy-start(f32[1,6,10,1,128]{3,4,2,1,0:T(8,128)} %copy.144) | copy-start | bytes 92164
  141.2 7.8 %collective-permute-start.10 = (f32[1,6,10,34,1]{3,4,2,1,0:T(1,128)S(1)}, f32[1,6,10,34,1]{3,4,2,1,0:T(1,128)S(1)}, u32[]{:S(2)}, u32[]{:S(2)}) collective-permute-start(f32[1,6,10,34,1]{3,4,2,1,0:T(1,128)S(1)} %get-tuple-element.18), channel_id=1, source_target_pairs={{0,1},{1,2},{2,3},{4,5},{5,6},{6,7},{8,9},{9,10},{10,11},{12,13},{... | collective-permute-start | bytes 24488 | tf_op jit(solution)/shard_map/ppermute | solution.py:23
  146.3 5.8 %collective-permute-start.11 = (f32[1,6,10,34,1]{3,4,2,1,0:T(1,128)S(1)}, f32[1,6,10,34,1]{3,4,2,1,0:T(1,128)S(1)}, u32[]{:S(2)}, u32[]{:S(2)}) collective-permute-start(f32[1,6,10,34,1]{3,4,2,1,0:T(1,128)S(1)} %get-tuple-element.19), channel_id=1, source_target_pairs={{1,0},{2,1},{3,2},{5,4},{6,5},{7,6},{9,8},{10,9},{11,10},{13,12},{... | collective-permute-start | bytes 24488 | tf_op jit(solution)/shard_map/ppermute | solution.py:24
  172.9 13.5 %copy-start.42 = (f32[1,3,8,32,128]{4,3,2,1,0:T(8,128)S(1)}, f32[1,3,8,32,128]{4,3,2,1,0:T(8,128)}, u32[]{:S(2)}) copy-start(f32[1,3,8,32,128]{4,3,2,1,0:T(8,128)} %copy.151) | copy-start | bytes 1179652
  172.9 13.5 %copy-start.43 = (f32[1,3,8,32,128]{4,3,2,1,0:T(8,128)S(1)}, f32[1,3,8,32,128]{4,3,2,1,0:T(8,128)}, u32[]{:S(2)}) copy-start(f32[1,3,8,32,128]{4,3,2,1,0:T(8,128)} %copy.152) | copy-start | bytes 1179652
  172.9 19.6 %copy-start.40 = (f32[3,8,32,128]{3,2,1,0:T(8,128)S(1)}, f32[3,8,32,128]{3,2,1,0:T(8,128)}, u32[]{:S(2)}) copy-start(f32[3,8,32,128]{3,2,1,0:T(8,128)} %param.11) | copy-start | bytes 1179652
  173.9 7.5 %collective-permute-start.18 = (f32[1,6,1,32,128]{4,3,2,1,0:T(8,128)S(1)}, f32[1,6,1,32,128]{4,3,2,1,0:T(8,128)S(1)}, u32[]{:S(2)}, u32[]{:S(2)}) collective-permute-start(f32[1,6,1,32,128]{4,3,2,1,0:T(8,128)S(1)} %get-tuple-element.90), channel_id=1, source_target_pairs={{0,16},{16,32},{32,48},{48,64},{64,80},{80,96},{96,112},{1,17},{17... | collective-permute-start | bytes 294920 | tf_op jit(solution)/shard_map/ppermute | solution.py:23
  178.3 8.0 %collective-permute-start.19 = (f32[1,6,1,32,128]{4,3,2,1,0:T(8,128)S(1)}, f32[1,6,1,32,128]{4,3,2,1,0:T(8,128)S(1)}, u32[]{:S(2)}, u32[]{:S(2)}) collective-permute-start(f32[1,6,1,32,128]{4,3,2,1,0:T(8,128)S(1)} %get-tuple-element.91), channel_id=1, source_target_pairs={{16,0},{32,16},{48,32},{64,48},{80,64},{96,80},{112,96},{17,1},{33... | collective-permute-start | bytes 294920 | tf_op jit(solution)/shard_map/ppermute | solution.py:24
  188.0 20.2 %collective-permute-start.20 = (f32[1,6,10,1,128]{4,3,2,1,0:T(1,128)}, f32[1,6,10,1,128]{4,3,2,1,0:T(1,128)S(1)}, u32[]{:S(2)}, u32[]{:S(2)}) collective-permute-start(f32[1,6,10,1,128]{4,3,2,1,0:T(1,128)} %get-tuple-element.82), channel_id=1, source_target_pairs={{0,4},{4,8},{8,12},{1,5},{5,9},{9,13},{2,6},{6,10},{10,14},{3,7},{... | collective-permute-start | bytes 92168 | tf_op jit(solution)/shard_map/ppermute | solution.py:23
  191.1 19.8 %collective-permute-start.21 = (f32[1,6,10,1,128]{4,3,2,1,0:T(1,128)S(1)}, f32[1,6,10,1,128]{4,3,2,1,0:T(1,128)S(1)}, u32[]{:S(2)}, u32[]{:S(2)}) collective-permute-start(f32[1,6,10,1,128]{4,3,2,1,0:T(1,128)S(1)} %get-tuple-element.83), channel_id=1, source_target_pairs={{4,0},{8,4},{12,8},{5,1},{9,5},{13,9},{6,2},{10,6},{14,10},{7,3},{... | collective-permute-start | bytes 92168 | tf_op jit(solution)/shard_map/ppermute | solution.py:24
  213.4 11.7 %copy-start.10 = (f32[1,6,10,1,128]{3,4,2,1,0:T(8,128)S(1)}, f32[1,6,10,1,128]{3,4,2,1,0:T(8,128)}, u32[]{:S(2)}) copy-start(f32[1,6,10,1,128]{3,4,2,1,0:T(8,128)} %copy.153) | copy-start | bytes 92164
  213.4 11.7 %copy-start.12 = (f32[1,6,10,1,128]{3,4,2,1,0:T(8,128)S(1)}, f32[1,6,10,1,128]{3,4,2,1,0:T(8,128)}, u32[]{:S(2)}) copy-start(f32[1,6,10,1,128]{3,4,2,1,0:T(8,128)} %copy.155) | copy-start | bytes 92164
  215.4 7.2 %collective-permute-start.22 = (f32[1,6,10,34,1]{3,4,2,1,0:T(1,128)S(1)}, f32[1,6,10,34,1]{3,4,2,1,0:T(1,128)S(1)}, u32[]{:S(2)}, u32[]{:S(2)}) collective-permute-start(f32[1,6,10,34,1]{3,4,2,1,0:T(1,128)S(1)} %get-tuple-element.22), channel_id=1, source_target_pairs={{0,1},{1,2},{2,3},{4,5},{5,6},{6,7},{8,9},{9,10},{10,11},{12,13},{... | collective-permute-start | bytes 24488 | tf_op jit(solution)/shard_map/ppermute | solution.py:23
  219.1 6.0 %collective-permute-start.23 = (f32[1,6,10,34,1]{3,4,2,1,0:T(1,128)S(1)}, f32[1,6,10,34,1]{3,4,2,1,0:T(1,128)S(1)}, u32[]{:S(2)}, u32[]{:S(2)}) collective-permute-start(f32[1,6,10,34,1]{3,4,2,1,0:T(1,128)S(1)} %get-tuple-element.23), channel_id=1, source_target_pairs={{1,0},{2,1},{3,2},{5,4},{6,5},{7,6},{9,8},{10,9},{11,10},{13,12},{... | collective-permute-start | bytes 24488 | tf_op jit(solution)/shard_map/ppermute | solution.py:24
  (38 other events, 106.8 us)
Sparse Core Ops, SparseCore 0:
  241.2 75.6 reduce-scatter.1
where the time goes:
time: 330 us; the launch traced here: 324 us
  local copies, waits for them, and re-layouts  97.3 us (29%)
  waiting for transfers between devices  85.8 us (26%)
  starting transfers between devices  68.6 us (21%)
  other arithmetic  52.7 us (16%)
  between operations  18.4 us (6%)
    reduce_scatter x1, waiting for transfers between devices, local(): lax.psum_scatter(summed.reshape(LAY_DEV * lax.axis_size('gz'), rows_y, co...  73 us
    ppermute x12, starting transfers between devices, with_halo(): before = lax.ppermute(last, axis, up)  51.9 us
    unnamed x131, local copies, waits for them, and re-layouts  30.8 us
    ppermute x12, starting transfers between devices, with_halo(): after = lax.ppermute(leading, axis, down)  16.6 us
    concatenate x4, local copies, waits for them, and re-layouts, with_halo(): value = jnp.concatenate([before, value, after], axis=dim)  13.3 us
    ppermute x12, waiting for transfers between devices, with_halo(): after = lax.ppermute(leading, axis, down)  12.7 us
    slice x8, other arithmetic, with_halo(): last = lax.slice_in_dim(value, length - width, length, axis=dim)  12.6 us
    concatenate x8, other arithmetic, with_halo(): value = jnp.concatenate([before, value, after], axis=dim)  12 us
  transfers between devices with their start and end apart: 25, of which 5 were waited for; matrix products, arithmetic and copies ran while one was open for 24% of the time, Pallas kernels for 0%

commit v1 on v0

v1 whole, which is shorter than its diff:
```python
import functools
import math

import jax
import jax.numpy as jnp
from jax import lax
from jax.experimental import pallas as pl
from jax.experimental.pallas import tpu as pltpu
from jax.sharding import PartitionSpec as P

F32 = jnp.float32
PLANES, ROWS, COLS = 8, 32, 128
DEEP, TALL = PLANES + 4, ROWS + 8
LAYERS = 16
PERIOD = 64
COMPS = 14
BELOW = [(k, 1) for k in range(14)] + [(k, 2) for k in (0, 1, 2, 3, 4, 6, 7, 8, 9, 10)]
ABOVE = [(k, 0) for k in range(13)] + [(k, 1) for k in (0, 1, 6, 7)]
BELOW_TILES, ABOVE_TILES = (len(BELOW) + 1) // 2, (len(ABOVE) + 1) // 2


def lanes(rows=8):
    return lax.broadcasted_iota(jnp.int32, (rows, COLS), 1)


def subs(rows=8):
    return lax.broadcasted_iota(jnp.int32, (rows, COLS), 0)


def turn(value, shift, axis):
    shift = shift % value.shape[axis]
    return value if shift == 0 else pltpu.roll(value, shift, axis)


def slot(k):
    return k // 8, (k % 8) // 4, k % 4


def slot_mask(k, rows):
    _, half, pair = slot(k)
    lane = lanes(rows)
    inside = ((lane - 16 - 64 * half) & 127) < 64
    return inside & (((lane & 7) >> 1) == pair)


def window(p, rows):
    lane = lanes(rows)
    return (lane >= 8 * (p + 2)) & (lane < 8 * (p + 2) + 4)


def parity(axis):
    return lax.rem(lax.axis_index(axis), 2) == 0


def strip(planes, rows):
    out = jnp.zeros((rows, COLS), F32)
    for p, plane in enumerate(planes):
        out = jnp.where(window(p, rows), turn(plane, 8 * (p + 2) + 2, 1), out)
    return out


def face_pack(strips, rows):
    right = [jnp.zeros((rows, COLS), F32) for _ in range(2)]
    left = [jnp.zeros((rows, COLS), F32) for _ in range(2)]
    for k, value in enumerate(strips):
        array, half, pair = slot(k)
        mask = slot_mask(k, rows)
        right[array] = jnp.where(mask, turn(value, 2 * pair + 64 * half, 1), right[array])
        left[array] = jnp.where(mask, turn(value, 2 * pair - 2 + 64 * half, 1), left[array])
    return right, left


def first_kernel(e, h, ae, ah, eps, cur, zu, zd, ya, yb, strips, right_out, left_out):
    def plane(k, p):
        if k < 12:
            return (e, h, ae, ah)[k // 3][k % 3, p]
        return (eps, cur)[k - 12][p]

    even = parity("gy")
    sub = subs()
    for k in range(COMPS):
        for half in range(2):
            up = jnp.zeros((8, COLS), F32)
            down = jnp.zeros((8, COLS), F32)
            for j in range(4):
                block = plane(k, 4 * half + j)
                mask = (sub >> 1) == j
                up = jnp.where(mask, turn(block[24:32], 2 * j - 6, 0), up)
                down = jnp.where(mask, turn(block[0:8], 2 * j, 0), down)
            at = 8 * (2 * k + half)
            ya[at : at + 8] = jnp.where(even, up, down)
            yb[at : at + 8] = jnp.where(even, down, up)
    for i, (k, below) in enumerate(BELOW):
        zu[i] = plane(k, PLANES - below)
    for i, (k, above) in enumerate(ABOVE):
        zd[i] = plane(k, above)
    values = []
    for k in range(COMPS):
        value = strip([plane(k, p) for p in range(PLANES)], ROWS)
        strips[k] = value
        values.append(value)
    right, left = face_pack(values, ROWS)
    for a in range(2):
        right_out[a] = right[a]
        left_out[a] = left[a]


def second_kernel(ya, yb, right_in, left_in, tiles, strips, xa, xb):
    index = lax.axis_index("gy")
    even = parity("gy")
    has_after = (index < lax.axis_size("gy") - 1).astype(F32)
    has_before = (index > 0).astype(F32)
    sub = subs()
    values = []
    for k in range(COMPS):
        planes = []
        for half in range(2):
            at = 8 * (2 * k + half)
            got_a, got_b = ya[at : at + 8], yb[at : at + 8]
            after = jnp.where(even, got_a, got_b) * has_after
            before = jnp.where(even, got_b, got_a) * has_before
            for j in range(4):
                tile = jnp.where(sub < 2, turn(after, -2 * j, 0), jnp.where(sub >= 6, turn(before, 6 - 2 * j, 0), 0.0))
                tiles[k, 4 * half + j] = tile
                planes.append(tile)
        value = strip(planes, 8)
        strips[k] = value
        values.append(value)
    right, left = face_pack(values, 8)
    even = parity("gx")
    for a in range(2):
        xa[a, 0:ROWS] = jnp.where(even, right_in[a], left_in[a])
        xb[a, 0:ROWS] = jnp.where(even, left_in[a], right_in[a])
        xa[a, ROWS:TALL] = jnp.where(even, right[a], left[a])
        xb[a, ROWS:TALL] = jnp.where(even, left[a], right[a])


def rim_pack(out, items, plane_of, tiles, side, first_lane):
    sub = subs()
    kept = (sub < 2) | (sub >= 6)
    count = (len(items) + 1) // 2
    for i in range(count):
        k, at = items[2 * i]
        tile = tiles[k, plane_of(at)]
        if 2 * i + 1 < len(items):
            k, at = items[2 * i + 1]
            tile = jnp.where(kept, tile, turn(tiles[k, plane_of(at)], 4, 0))
        out[8 * i : 8 * i + 8] = tile
    lane = lanes(TALL)
    for a in range(2):
        packed = jnp.zeros((TALL, COLS), F32)
        for k in range(8 * a, min(8 * a + 8, COMPS)):
            packed = jnp.where((lane >> 4) == k % 8, turn(side[k], 16 * (k % 8) - first_lane, 1), packed)
        at = 8 * count + TALL * a
        out[at : at + TALL] = packed


def third_kernel(xa, xb, strips, strips_rim, tiles, sides, rim_up, rim_down):
    index = lax.axis_index("gx")
    even = parity("gx")
    has_after = (index < lax.axis_size("gx") - 1).astype(F32)
    has_before = (index > 0).astype(F32)
    lane = lanes(TALL)
    pair_of = (lane & 7) >> 1
    own = (lane >= 16) & (lane < 80)
    after = [jnp.where(even, xa[a], xb[a]) * has_after for a in range(2)]
    before = [jnp.where(even, xb[a], xa[a]) * has_before for a in range(2)]
    side = []
    for k in range(COMPS):
        array, half, pair = slot(k)
        mine = jnp.concatenate([strips[k], strips_rim[k]], axis=0)
        value = jnp.where(pair_of == 0, mine, turn(mine, 4, 1))
        value = jnp.where(pair_of == 1, turn(after[array], 2 - 2 * pair - 64 * half, 1), value)
        value = jnp.where(pair_of == 2, turn(before[array], 4 - 2 * pair - 64 * half, 1), value)
        value = jnp.where(own, value, 0.0)
        sides[k] = value
        side.append(value)
    rim_pack(rim_up, BELOW, lambda below: PLANES - below, tiles, side, 64)
    rim_pack(rim_down, ABOVE, lambda above: above, tiles, side, 16)


def profile(position, extent, thickness):
    distance = jnp.minimum(position, extent - 1 - position)
    depth = jnp.maximum(thickness - distance, 0).astype(F32) / thickness.astype(F32)
    return 0.8 * depth * depth


def magnetic(ex, ey, ez, ex_up, ey_up, hx, hy, hz, r, next_x, next_y, at=(0, 1, 2)):
    cx = (next_y(ez, 2) - ez) - (ey_up - ey)
    cy = (ex_up - ex) - (next_x(ez, 2) - ez)
    cz = (next_x(ey, 1) - ey) - (next_y(ex, 0) - ex)
    return [r * (h + h - 0.5 * c) - h for h, c in ((hx, cx), (hy, cy), (hz, cz))]


def electric(hx, hy, hz, hx_down, hy_down, ex, ey, ez, q, g, drive, prev_x, prev_y):
    cx = (hz - prev_y(hz, 2)) - (hy - hy_down)
    cy = (hx - hx_down) - (hz - prev_x(hz, 2))
    cz = (hy - prev_x(hy, 1)) - (hx - prev_y(hx, 0))
    if drive is not None:
        cz = cz - drive
    return [q * (g * e + c) for e, c in ((ex, cx), (ey, cy), (ez, cz))]


def main_kernel(
    layer, pml, start, e, h, ae, ah, eps, cur, zu, zd, tiles, sides, rim_up, rim_down,
    sums, e_out, h_out,
    f, one, rr, qq, gg, xf, xone, xr, xq, xg,
):
    iz, iy, ix = (lax.axis_index(a) for a in ("gz", "gy", "gx"))
    nz, ny, nx = (PLANES * lax.axis_size("gz"), ROWS * lax.axis_size("gy"), COLS * lax.axis_size("gx"))
    has_above = (iz < lax.axis_size("gz") - 1).astype(F32)
    has_below = (iz > 0).astype(F32)
    for k in range(COMPS):
        for p in range(PLANES):
            if k < 12:
                f[k, p + 2, 0:ROWS] = (e, h, ae, ah)[k // 3][k % 3, p]
            else:
                f[k, p + 2, 0:ROWS] = (eps, cur)[k - 12][p]
            f[k, p + 2, ROWS:TALL] = tiles[k, p]
    sent = set()
    for items, faces, rim, place, keep in (
        (BELOW, zu, rim_up, lambda below: 2 - below, has_below),
        (ABOVE, zd, rim_down, lambda above: PLANES + 2 + above, has_above),
    ):
        for i, (k, at) in enumerate(items):
            idx = place(at)
            sent.add((k, idx))
            tile = rim[8 * (i // 2) : 8 * (i // 2) + 8]
            f[k, idx, 0:ROWS] = faces[i] * keep
            f[k, idx, ROWS:TALL] = turn(tile, 4 * (i % 2), 0) * keep
    for k in range(COMPS):
        for idx in (0, 1, PLANES + 2, PLANES + 3):
            if (k, idx) not in sent:
                f[k, idx] = jnp.zeros((TALL, COLS), F32)
    lane = lanes(TALL)
    row = subs(TALL)
    for k in range(COMPS):
        at = 8 * BELOW_TILES + TALL * (k // 8)
        low = turn(rim_up[at : at + TALL], -16 * (k % 8), 1) * has_below
        at = 8 * ABOVE_TILES + TALL * (k // 8)
        high = turn(rim_down[at : at + TALL], 80 - 16 * (k % 8), 1) * has_above
        value = jnp.where(lane < 16, low, sides[k])
        xf[k] = jnp.where((lane >= 80) & (lane < 96), high, value)
    y_at = ROWS * iy + jnp.where(row >= 36, row - TALL, row)
    x_at = COLS * ix + lane
    y_in = (y_at >= 0) & (y_at < ny)
    profile_y = profile(y_at, ny, pml[1])
    profile_yx = profile_y + profile(x_at, nx, pml[2])

    def coefficients(sigma, inside, permittivity):
        permittivity = jnp.maximum(permittivity, 1.0)
        r = jnp.where(inside, 1.0 / (1.0 + 0.25 * sigma), 0.0)
        q = jnp.where(inside, 1.0 / (2.0 * permittivity + 0.5 * sigma), 0.0)
        return r, q, 2.0 * permittivity - 0.5 * sigma

    def plane_coefficients(idx, carry):
        z_at = jnp.full((TALL, COLS), PLANES * iz + idx - 2, jnp.int32)
        inside = y_in & (z_at >= 0) & (z_at < nz)
        sigma = profile(z_at[0:8], nz, pml[0])
        sigma = jnp.concatenate([sigma] * (TALL // 8), axis=0) + profile_yx
        rr[idx], qq[idx], gg[idx] = coefficients(sigma, inside, f[12, idx])
        return carry

    lax.fori_loop(0, DEEP, plane_coefficients, 0)
    column = lane & 7
    x_at = COLS * ix + jnp.where(column < 4, COLS - 2 + column, column - 6)
    z_at = PLANES * iz + (lane >> 3) - 2
    inside = y_in & (z_at >= 0) & (z_at < nz) & (x_at >= 0) & (x_at < nx)
    sigma = profile(z_at, nz, pml[0]) + profile_y + profile(x_at, nx, pml[2])
    xr[...], xq[...], xg[...] = coefficients(sigma, inside, xf[12])
    factors = []
    for k in (1, 2):
        phase = jnp.full((8, COLS), lax.rem(start[0] + k, PERIOD), jnp.int32).astype(F32)
        factor = jnp.sin(phase * (2.0 * math.pi / PERIOD))
        factors.append(jnp.concatenate([factor] * (TALL // 8), axis=0))
    first_lane, last_lane = lane == 0, lane == COLS - 1

    def up_row(value, _):
        return pltpu.roll(value, TALL - 1, 0)

    def down_row(value, _):
        return pltpu.roll(value, 1, 0)

    def side_magnetic(e_ref, e_base, h_base):
        got = [e_ref[e_base + c] for c in range(3)]
        new = magnetic(
            *got, pltpu.roll(got[0], 120, 1), pltpu.roll(got[1], 120, 1), *[xf[h_base + c] for c in range(3)], xr[...],
            lambda v, _: pltpu.roll(v, 127, 1), up_row,
        )
        for c in range(3):
            xf[h_base + c] = new[c]

    def side_electric(e_base, h_base, out_base, factor):
        got = [xf[h_base + c] for c in range(3)]
        drive = None if factor is None else xf[13] * factor
        new = electric(
            *got, pltpu.roll(got[0], 8, 1), pltpu.roll(got[1], 8, 1), *[xf[e_base + c] for c in range(3)], xq[...], xg[...], drive,
            lambda v, _: pltpu.roll(v, 1, 1), down_row,
        )
        for c in range(3):
            xone[out_base + c] = new[c]

    def plane_magnetic(idx, e_ref, x_ref, e_base, h_base):
        def next_x(value, c):
            halo = pltpu.roll(x_ref[e_base + c], 125 - 8 * idx, 1)
            return jnp.where(last_lane, halo, pltpu.roll(value, COLS - 1, 1))

        new = magnetic(
            *[e_ref[e_base + c, idx] for c in range(3)], e_ref[e_base, idx + 1], e_ref[e_base + 1, idx + 1],
            *[f[h_base + c, idx] for c in range(3)], rr[idx], next_x, up_row,
        )
        for c in range(3):
            f[h_base + c, idx] = new[c]

    def plane_electric(idx, e_ref, e_base, h_base, factor):
        def prev_x(value, c):
            halo = pltpu.roll(xf[h_base + c], 123 - 8 * idx, 1)
            return jnp.where(first_lane, halo, pltpu.roll(value, 1, 1))

        drive = None if factor is None else f[13, idx] * factor
        return electric(
            *[f[h_base + c, idx] for c in range(3)], f[h_base, idx - 1], f[h_base + 1, idx - 1],
            *[e_ref[e_base + c, idx] for c in range(3)], qq[idx], gg[idx], drive, prev_x, down_row,
        )

    def body(idx, carry):
        plane_magnetic(idx, f, xf, 0, 3)
        plane_magnetic(idx, f, xf, 6, 9)
        return carry

    lax.fori_loop(0, PLANES + 3, body, 0)
    side_magnetic(xf, 0, 3)
    side_magnetic(xf, 6, 9)

    def body(idx, carry):
        for base, out, factor in ((0, 0, factors[0]), (6, 3, None)):
            new = plane_electric(idx, f, base, base + 3, factor)
            for c in range(3):
                one[out + c, idx] = new[c]
        return carry

    lax.fori_loop(1, PLANES + 3, body, 0)
    side_electric(0, 3, 0, factors[0])
    side_electric(6, 9, 3, None)

    def body(idx, carry):
        plane_magnetic(idx, one, xone, 0, 3)
        plane_magnetic(idx, one, xone, 3, 9)
        return carry

    lax.fori_loop(1, PLANES + 2, body, 0)
    side_magnetic(xone, 0, 3)
    side_magnetic(xone, 3, 9)
    sums[...] = jnp.zeros((LAYERS, ROWS, COLS), F32)

    def body(p, carry):
        idx = p + 2
        two = plane_electric(idx, one, 0, 3, factors[1])
        zero = plane_electric(idx, one, 3, 9, None)
        density = jnp.zeros((ROWS, COLS), F32)
        for c in range(3):
            last = zero[c][0:ROWS]
            e_out[c, p] = last
            h_out[c, p] = f[9 + c, idx, 0:ROWS]
            density = density + f[c, idx, 0:ROWS] * last + one[c, idx, 0:ROWS] * one[3 + c, idx, 0:ROWS]
            density = density + two[c][0:ROWS] * f[6 + c, idx, 0:ROWS]
        sums[layer[p]] = density
        return carry

    lax.fori_loop(0, PLANES, body, 0)


def sum_kernel(got, out):
    total = got[0]
    for i in range(1, got.shape[0]):
        total = total + got[i]
    out[...] = total


def call(kernel, outs, scratch=(), scalars=0, flops=1000000):
    def run(*args):
        specs = [pl.BlockSpec(memory_space=pltpu.SMEM)] * scalars
        specs += [pl.BlockSpec(memory_space=pltpu.VMEM)] * (len(args) - scalars)
        size = sum(4 * math.prod(s) for s in outs) + sum(4 * math.prod(a.shape) for a in args)
        return pl.pallas_call(
            kernel,
            out_shape=[jax.ShapeDtypeStruct(s, F32) for s in outs],
            in_specs=specs,
            out_specs=[pl.BlockSpec(memory_space=pltpu.VMEM)] * len(outs),
            scratch_shapes=[pltpu.VMEM(s, F32) for s in scratch],
            compiler_params=pltpu.CompilerParams(vmem_limit_bytes=24 * 2**20),
            cost_estimate=pl.CostEstimate(flops=flops, bytes_accessed=size, transcendentals=0),
        )(*args)

    return run


def ring(axis, step):
    count = lax.axis_size(axis)
    return [(i, (i + step) % count) for i in range(count)]


def swaps(axis, first):
    count = lax.axis_size(axis)
    pairs = [(i % count, (i + 1) % count) for i in range(first, count, 2)]
    return pairs + [(b, a) for a, b in pairs]


def local(e_start, h_start, adjoint_e, adjoint_h, permittivity, current, layer_of_cell, pml_cells, start_step):
    raw = (e_start, h_start, adjoint_e, adjoint_h, permittivity, current)
    block = (ROWS, COLS)
    zu, zd, ya, yb, strips, right, left = call(
        first_kernel,
        [(len(BELOW),) + block, (len(ABOVE),) + block, (16 * COMPS, COLS), (16 * COMPS, COLS), (COMPS,) + block, (2,) + block, (2,) + block],
    )(*raw)
    ya = lax.ppermute(ya, "gy", swaps("gy", 0))
    yb = lax.ppermute(yb, "gy", swaps("gy", 1))
    zu = lax.ppermute(zu, "gz", ring("gz", 1))
    zd = lax.ppermute(zd, "gz", ring("gz", -1))
    tiles, strips_rim, xa, xb = call(
        second_kernel, [(COMPS, PLANES, 8, COLS), (COMPS, 8, COLS), (2, TALL, COLS), (2, TALL, COLS)]
    )(ya, yb, right, left)
    xa = lax.ppermute(xa, "gx", swaps("gx", 0))
    xb = lax.ppermute(xb, "gx", swaps("gx", 1))
    sides, rim_up, rim_down = call(
        third_kernel,
        [(COMPS, TALL, COLS), (8 * BELOW_TILES + 2 * TALL, COLS), (8 * ABOVE_TILES + 2 * TALL, COLS)],
    )(xa, xb, strips, strips_rim, tiles)
    rim_up = lax.ppermute(rim_up, "gz", ring("gz", 1))
    rim_down = lax.ppermute(rim_down, "gz", ring("gz", -1))
    deep, tall = (DEEP, TALL, COLS), (TALL, COLS)
    sums, e_out, h_out = call(
        main_kernel,
        [(LAYERS,) + block, (3, PLANES) + block, (3, PLANES) + block],
        [(COMPS,) + deep, (6,) + deep, deep, deep, deep, (COMPS,) + tall, (6,) + tall, tall, tall, tall],
        scalars=3,
    )(layer_of_cell, pml_cells, start_step, *raw, zu, zd, tiles, sides, rim_up, rim_down)
    count = lax.axis_size("gz")
    got = lax.all_to_all(sums, "gz", 0, 0, tiled=True)
    (gradient,) = call(sum_kernel, [(LAYERS // count,) + block])(got.reshape((count, LAYERS // count) + block))
    return gradient, e_out, h_out


def solution(mesh):
    fields = P(None, "gz", "gy", "gx")
    cells = P("gz", "gy", "gx")
    return jax.shard_map(
        local,
        mesh=mesh,
        in_specs=(fields, fields, fields, fields, cells, cells, P("gz"), P(), P()),
        out_specs=(cells, fields, fields),
        check_vma=False,
    )
```

time: 330 us -> 67.1 us (0.20); the launches traced: 324 us -> 66.7 us
  local copies, waits for them, and re-layouts: 97.3 us -> 5.81 us
  waiting for transfers between devices: 85.8 us -> 20.4 us
  other arithmetic: 52.7 us -> 0 us
  starting transfers between devices: 68.6 us -> 17.2 us
  between operations: 18.4 us -> 1.39 us
  blocking collectives: 0 us -> 13 us
  Pallas kernels: 0 us -> 8.83 us
    reduce_scatter x1 -> x0, waiting for transfers between devices: 73 us -> none  [local(): lax.psum_scatter(summed.reshape(LAY_DEV * lax.axis_size('gz'), rows_y, co...]
    ppermute x24 -> x8, starting transfers between devices: 68.5 us -> 17.2 us  [the longest x1 4.3 us: local(): rim_up = lax.ppermute(rim_up, 'gz', ring('gz', 1))]
    unnamed x131 -> x24, local copies, waits for them, and re-layouts: 30.8 us -> 5.81 us
    ppermute x8 -> x0, local copies, waits for them, and re-layouts: 20.6 us -> none  [the longest x4 10.4 us: with_halo(): before = lax.ppermute(last, axis, up)]
    slice x40 -> x0, local copies, waits for them, and re-layouts: 15.8 us -> none  [the longest x28 8.21 us: plain_diff(): lax.slice_in_dim(values, 1, extent, axis=along)]
    concatenate x4 -> x0, local copies, waits for them, and re-layouts: 13.3 us -> none  [with_halo(): value = jnp.concatenate([before, value, after], axis=dim)]
    all_to_all x0 -> x1, blocking collectives: none -> 13 us  [local(): got = lax.all_to_all(sums, 'gz', 0, 0, tiled=True)]
    slice x8 -> x0, other arithmetic: 12.6 us -> none  [with_halo(): last = lax.slice_in_dim(value, length - width, length, axis=dim)]
  transfers between devices with their start and end apart: 25 -> 8, of which waited for: 5 -> 5; matrix products, arithmetic and copies ran while one was open for 24% -> 0% of each run, Pallas kernels for 0% -> 1%
where the time goes in v1:
time: 67.1 us; the launch traced here: 66.7 us
  waiting for transfers between devices  20.4 us (30%)
  starting transfers between devices  17.2 us (26%)
  blocking collectives  13 us (19%)
  Pallas kernels  8.83 us (13%)
  local copies, waits for them, and re-layouts  5.81 us (9%)
  between operations  1.39 us (2%)
    ppermute x1, waiting for transfers between devices, local(): yb = lax.ppermute(yb, 'gy', swaps('gy', 1))  13.3 us
    all_to_all x1, blocking collectives, local(): got = lax.all_to_all(sums, 'gz', 0, 0, tiled=True)  13 us
    pallas_call x5, Pallas kernels, run(): pl.pallas_call(kernel, out_shape=[jax.ShapeDtypeStruct(s, F32) for s in o...  8.83 us
    unnamed x24, local copies, waits for them, and re-layouts  5.81 us
    ppermute x1, starting transfers between devices, local(): rim_up = lax.ppermute(rim_up, 'gz', ring('gz', 1))  4.3 us
    ppermute x1, starting transfers between devices, local(): zu = lax.ppermute(zu, 'gz', ring('gz', 1))  4.03 us
    ppermute x1, waiting for transfers between devices, local(): rim_down = lax.ppermute(rim_down, 'gz', ring('gz', -1))  3.82 us
    ppermute x1, starting transfers between devices, local(): zd = lax.ppermute(zd, 'gz', ring('gz', -1))  2.53 us
  transfers between devices with their start and end apart: 8, of which 5 were waited for; matrix products, arithmetic and copies ran while one was open for 0% of the time, Pallas kernels for 1%

profile of v1, /device:TPU:0, one launch (start us, length us, event | category | flops | bytes accessed | tf_op | source)
XLA Modules:
  0.0 66.7 jit_solution(196061218503296718)
XLA Ops:
  0.6 0.0 copy-start
  0.6 1.0 %copy-done = f32[3,8,32,128]{3,2,1,0:T(8,128)S(1)} copy-done((f32[3,8,32,128]{3,2,1,0:T(8,128)S(1)}, f32[3,8,32,128]{3,2,1,0:T(8,128)}, u32[]{:S(2)}) %copy-start) | copy-done | bytes 393240
  1.6 0.0 copy-start.2
  1.6 1.0 %copy-done.2 = f32[3,8,32,128]{3,2,1,0:T(8,128)S(1)} copy-done((f32[3,8,32,128]{3,2,1,0:T(8,128)S(1)}, f32[3,8,32,128]{3,2,1,0:T(8,128)}, u32[]{:S(2)}) %copy-start.2) | copy-done | bytes 393240
  2.6 0.0 copy-start.4
  2.6 1.0 %copy-done.4 = f32[3,8,32,128]{3,2,1,0:T(8,128)S(1)} copy-done((f32[3,8,32,128]{3,2,1,0:T(8,128)S(1)}, f32[3,8,32,128]{3,2,1,0:T(8,128)}, u32[]{:S(2)}) %copy-start.4) | copy-done | bytes 393240
  3.6 0.0 copy-start.6
  3.6 1.0 %copy-done.6 = f32[3,8,32,128]{3,2,1,0:T(8,128)S(1)} copy-done((f32[3,8,32,128]{3,2,1,0:T(8,128)S(1)}, f32[3,8,32,128]{3,2,1,0:T(8,128)}, u32[]{:S(2)}) %copy-start.6) | copy-done | bytes 393240
  4.6 0.0 copy-start.8
  4.6 0.9 %copy-done.8 = f32[8,32,128]{2,1,0:T(8,128)S(1)} copy-done((f32[8,32,128]{2,1,0:T(8,128)S(1)}, f32[8,32,128]{2,1,0:T(8,128)}, u32[]{:S(2)}) %copy-start.8) | copy-done | bytes 131096
  5.5 0.0 copy-start.9
  5.5 0.9 %copy-done.9 = f32[8,32,128]{2,1,0:T(8,128)S(1)} copy-done((f32[8,32,128]{2,1,0:T(8,128)S(1)}, f32[8,32,128]{2,1,0:T(8,128)}, u32[]{:S(2)}) %copy-start.9) | copy-done | bytes 131096
  6.4 0.0 copy-start.5
  6.4 0.0 copy-start.7
  6.4 0.6 shard_map.112
  7.1 4.0 %collective-permute-start = (f32[24,32,128]{2,1,0:T(8,128)S(1)}, f32[24,32,128]{2,1,0:T(8,128)S(1)}, u32[]{:S(2)}, u32[]{:S(2)}) collective-permute-start(f32[24,32,128]{2,1,0:T(8,128)S(1)} %get-tuple-element.20), channel_id=1, source_target_pairs={{0,16},{16,32},{32,48},{48,64},{64,80},{80,96},{96,112},{112,0},{1... | collective-permute-start | bytes 1179656 | tf_op jit(solution)/shard_map/ppermute | solution.py:418
  11.1 2.5 %collective-permute-start.1 = (f32[17,32,128]{2,1,0:T(8,128)S(1)}, f32[17,32,128]{2,1,0:T(8,128)S(1)}, u32[]{:S(2)}, u32[]{:S(2)}) collective-permute-start(f32[17,32,128]{2,1,0:T(8,128)S(1)} %get-tuple-element.21), channel_id=1, source_target_pairs={{0,112},{16,0},{32,16},{48,32},{64,48},{80,64},{96,80},{112,96},{1... | collective-permute-start | bytes 835592 | tf_op jit(solution)/shard_map/ppermute | solution.py:419
  13.6 0.0 collective-permute-start.2
  13.6 1.3 %collective-permute-start.3 = (f32[224,128]{1,0:T(8,128)S(1)}, f32[224,128]{1,0:T(8,128)S(1)}, u32[]{:S(2)}, u32[]{:S(2)}) collective-permute-start(f32[224,128]{1,0:T(8,128)S(1)} %get-tuple-element.23), channel_id=1, source_target_pairs={{4,8},{12,0},{8,4},{0,12},{5,9},{13,1},{9,5},{1,13},{6,10},{14,2},... | collective-permute-start | bytes 344072 | tf_op jit(solution)/shard_map/ppermute | solution.py:417
  14.9 0.1 collective-permute-done.2.ya
  15.0 13.3 %collective-permute-done.3.yb = f32[224,128]{1,0:T(8,128)S(1)} collective-permute-done((f32[224,128]{1,0:T(8,128)S(1)}, f32[224,128]{1,0:T(8,128)S(1)}, u32[]{:S(2)}, u32[]{:S(2)}) %collective-permute-start.3) | collective-permute-done | bytes 114720 | tf_op jit(solution)/shard_map/ppermute | solution.py:417
  28.2 0.3 shard_map.113
  28.5 1.6 %collective-permute-start.4 = (f32[2,40,128]{2,1,0:T(8,128)S(1)}, f32[2,40,128]{2,1,0:T(8,128)S(1)}, u32[]{:S(2)}, u32[]{:S(2)}) collective-permute-start(f32[2,40,128]{2,1,0:T(8,128)S(1)} %get-tuple-element.27), channel_id=1, source_target_pairs={{0,1},{2,3},{1,0},{3,2},{4,5},{6,7},{5,4},{7,6},{8,9},{10,11},{9,8... | collective-permute-start | bytes 122888 | tf_op jit(solution)/shard_map/ppermute | solution.py:423
  30.1 2.1 %collective-permute-start.5 = (f32[2,40,128]{2,1,0:T(8,128)S(1)}, f32[2,40,128]{2,1,0:T(8,128)S(1)}, u32[]{:S(2)}, u32[]{:S(2)}) collective-permute-start(f32[2,40,128]{2,1,0:T(8,128)S(1)} %get-tuple-element.28), channel_id=1, source_target_pairs={{1,2},{3,0},{2,1},{0,3},{5,6},{7,4},{6,5},{4,7},{9,10},{11,8},{10,... | collective-permute-start | bytes 122888 | tf_op jit(solution)/shard_map/ppermute | solution.py:424
  32.2 0.8 %collective-permute-done.4.xa = f32[2,40,128]{2,1,0:T(8,128)S(1)} collective-permute-done((f32[2,40,128]{2,1,0:T(8,128)S(1)}, f32[2,40,128]{2,1,0:T(8,128)S(1)}, u32[]{:S(2)}, u32[]{:S(2)}) %collective-permute-start.4) | collective-permute-done | bytes 40992 | tf_op jit(solution)/shard_map/ppermute | solution.py:423
  33.0 2.4 %collective-permute-done.5.xb = f32[2,40,128]{2,1,0:T(8,128)S(1)} collective-permute-done((f32[2,40,128]{2,1,0:T(8,128)S(1)}, f32[2,40,128]{2,1,0:T(8,128)S(1)}, u32[]{:S(2)}, u32[]{:S(2)}) %collective-permute-start.5) | collective-permute-done | bytes 40992 | tf_op jit(solution)/shard_map/ppermute | solution.py:424
  35.4 0.0 copy-start.1
  35.4 0.0 copy-start.3
  35.4 0.4 shard_map.114
  35.8 4.3 %collective-permute-start.6 = (f32[176,128]{1,0:T(8,128)S(1)}, f32[176,128]{1,0:T(8,128)S(1)}, u32[]{:S(2)}, u32[]{:S(2)}) collective-permute-start(f32[176,128]{1,0:T(8,128)S(1)} %get-tuple-element.32), channel_id=1, source_target_pairs={{0,16},{16,32},{32,48},{48,64},{64,80},{80,96},{96,112},{112,0},{1... | collective-permute-start | bytes 270344 | tf_op jit(solution)/shard_map/ppermute | solution.py:429
  40.2 1.4 %collective-permute-start.7 = (f32[152,128]{1,0:T(8,128)S(1)}, f32[152,128]{1,0:T(8,128)S(1)}, u32[]{:S(2)}, u32[]{:S(2)}) collective-permute-start(f32[152,128]{1,0:T(8,128)S(1)} %get-tuple-element.33), channel_id=1, source_target_pairs={{0,112},{16,0},{32,16},{48,32},{64,48},{80,64},{96,80},{112,96},{1... | collective-permute-start | bytes 233480 | tf_op jit(solution)/shard_map/ppermute | solution.py:430
  42.2 0.0 copy-start.10
  42.2 0.0 copy-start.11
  42.2 3.8 %collective-permute-done.7.rim_down = f32[152,128]{1,0:T(8,128)S(1)} collective-permute-done((f32[152,128]{1,0:T(8,128)S(1)}, f32[152,128]{1,0:T(8,128)S(1)}, u32[]{:S(2)}, u32[]{:S(2)}) %collective-permute-start.7) | collective-permute-done | bytes 77856 | tf_op jit(solution)/shard_map/ppermute | solution.py:430
  46.1 0.0 collective-permute-done.6.rim_up
  46.1 0.0 collective-permute-done.1.zd
  46.1 0.0 collective-permute-done.zu
  46.1 0.0 copy-done.5
  46.1 0.0 copy-done.7
  46.1 0.0 copy-done.1
  46.1 0.0 copy-done.3
  46.1 0.0 copy-done.10
  46.1 0.0 copy-done.11
  46.1 6.9 %shard_map.115 = (f32[16,32,128]{2,1,0:T(8,128)S(1)}, f32[3,8,32,128]{3,2,1,0:T(8,128)}, f32[3,8,32,128]{3,2,1,0:T(8,128)}) custom-call(s32[8]{0:T(128)S(1)} %copy-done.10, s32[3]{0:T(128)S(1)} %copy-done.11, s32[1]{0:T(128)S(6)} %copy.12.start, f32[3,8,32,128]{3,2,1,0:T(8,128)S(1)} %copy-done.1, f32[3,8,32,128]{3,2,1,0:T(8,128)S(1)} %copy-done.3, ...), custom_call_target="tpu_custom_call" | custom-call | flops 1000000 | bytes 4468784 | tf_op jit(solution)/shard_map/pallas_call | solution.py:385
  53.0 13.0 %all_to_all.5 = f32[16,32,128]{2,1,0:T(8,128)S(1)} all-to-all(f32[16,32,128]{2,1,0:T(8,128)S(1)} %get-tuple-element.34), channel_id=1, replica_groups=mesh['gz'=8,'gy'=4,'gx'=4] {'gz'}, dimensions={0} | all-to-all | bytes 524288 | tf_op jit(solution)/shard_map/all_to_all | solution.py:439
  66.1 0.6 shard_map.116
Async XLA Ops:
  0.6 1.0 %copy-start = (f32[3,8,32,128]{3,2,1,0:T(8,128)S(1)}, f32[3,8,32,128]{3,2,1,0:T(8,128)}, u32[]{:S(2)}) copy-start(f32[3,8,32,128]{3,2,1,0:T(8,128)} %e.3) | copy-start | bytes 1179652
  1.6 1.0 %copy-start.2 = (f32[3,8,32,128]{3,2,1,0:T(8,128)S(1)}, f32[3,8,32,128]{3,2,1,0:T(8,128)}, u32[]{:S(2)}) copy-start(f32[3,8,32,128]{3,2,1,0:T(8,128)} %h.3) | copy-start | bytes 1179652
  2.6 1.0 %copy-start.4 = (f32[3,8,32,128]{3,2,1,0:T(8,128)S(1)}, f32[3,8,32,128]{3,2,1,0:T(8,128)}, u32[]{:S(2)}) copy-start(f32[3,8,32,128]{3,2,1,0:T(8,128)} %ae.3) | copy-start | bytes 1179652
  3.6 1.0 %copy-start.6 = (f32[3,8,32,128]{3,2,1,0:T(8,128)S(1)}, f32[3,8,32,128]{3,2,1,0:T(8,128)}, u32[]{:S(2)}) copy-start(f32[3,8,32,128]{3,2,1,0:T(8,128)} %ah.3) | copy-start | bytes 1179652
  4.6 0.9 %copy-start.8 = (f32[8,32,128]{2,1,0:T(8,128)S(1)}, f32[8,32,128]{2,1,0:T(8,128)}, u32[]{:S(2)}) copy-start(f32[8,32,128]{2,1,0:T(8,128)} %eps.3) | copy-start | bytes 393220
  5.5 0.9 %copy-start.9 = (f32[8,32,128]{2,1,0:T(8,128)S(1)}, f32[8,32,128]{2,1,0:T(8,128)}, u32[]{:S(2)}) copy-start(f32[8,32,128]{2,1,0:T(8,128)} %cur.3) | copy-start | bytes 393220
  6.4 39.6 %copy-start.5 = (f32[3,8,32,128]{3,2,1,0:T(8,128)S(1)}, f32[3,8,32,128]{3,2,1,0:T(8,128)}, u32[]{:S(2)}) copy-start(f32[3,8,32,128]{3,2,1,0:T(8,128)} %ae.3) | copy-start | bytes 1179652
  6.4 39.6 %copy-start.7 = (f32[3,8,32,128]{3,2,1,0:T(8,128)S(1)}, f32[3,8,32,128]{3,2,1,0:T(8,128)}, u32[]{:S(2)}) copy-start(f32[3,8,32,128]{3,2,1,0:T(8,128)} %ah.3) | copy-start | bytes 1179652
  7.1 39.0 %collective-permute-start = (f32[24,32,128]{2,1,0:T(8,128)S(1)}, f32[24,32,128]{2,1,0:T(8,128)S(1)}, u32[]{:S(2)}, u32[]{:S(2)}) collective-permute-start(f32[24,32,128]{2,1,0:T(8,128)S(1)} %get-tuple-element.20), channel_id=1, source_target_pairs={{0,16},{16,32},{32,48},{48,64},{64,80},{80,96},{96,112},{112,0},{1... | collective-permute-start | bytes 1179656 | tf_op jit(solution)/shard_map/ppermute | solution.py:418
  11.1 35.0 %collective-permute-start.1 = (f32[17,32,128]{2,1,0:T(8,128)S(1)}, f32[17,32,128]{2,1,0:T(8,128)S(1)}, u32[]{:S(2)}, u32[]{:S(2)}) collective-permute-start(f32[17,32,128]{2,1,0:T(8,128)S(1)} %get-tuple-element.21), channel_id=1, source_target_pairs={{0,112},{16,0},{32,16},{48,32},{64,48},{80,64},{96,80},{112,96},{1... | collective-permute-start | bytes 835592 | tf_op jit(solution)/shard_map/ppermute | solution.py:419
  13.6 1.3 %collective-permute-start.2 = (f32[224,128]{1,0:T(8,128)S(1)}, f32[224,128]{1,0:T(8,128)S(1)}, u32[]{:S(2)}, u32[]{:S(2)}) collective-permute-start(f32[224,128]{1,0:T(8,128)S(1)} %get-tuple-element.22), channel_id=1, source_target_pairs={{0,4},{8,12},{4,0},{12,8},{1,5},{9,13},{5,1},{13,9},{2,6},{10,14},... | collective-permute-start | bytes 344072 | tf_op jit(solution)/shard_map/ppermute | solution.py:416
  13.6 14.6 %collective-permute-start.3 = (f32[224,128]{1,0:T(8,128)S(1)}, f32[224,128]{1,0:T(8,128)S(1)}, u32[]{:S(2)}, u32[]{:S(2)}) collective-permute-start(f32[224,128]{1,0:T(8,128)S(1)} %get-tuple-element.23), channel_id=1, source_target_pairs={{4,8},{12,0},{8,4},{0,12},{5,9},{13,1},{9,5},{1,13},{6,10},{14,2},... | collective-permute-start | bytes 344072 | tf_op jit(solution)/shard_map/ppermute | solution.py:417
  28.5 4.5 %collective-permute-start.4 = (f32[2,40,128]{2,1,0:T(8,128)S(1)}, f32[2,40,128]{2,1,0:T(8,128)S(1)}, u32[]{:S(2)}, u32[]{:S(2)}) collective-permute-start(f32[2,40,128]{2,1,0:T(8,128)S(1)} %get-tuple-element.27), channel_id=1, source_target_pairs={{0,1},{2,3},{1,0},{3,2},{4,5},{6,7},{5,4},{7,6},{8,9},{10,11},{9,8... | collective-permute-start | bytes 122888 | tf_op jit(solution)/shard_map/ppermute | solution.py:423
  30.1 5.4 %collective-permute-start.5 = (f32[2,40,128]{2,1,0:T(8,128)S(1)}, f32[2,40,128]{2,1,0:T(8,128)S(1)}, u32[]{:S(2)}, u32[]{:S(2)}) collective-permute-start(f32[2,40,128]{2,1,0:T(8,128)S(1)} %get-tuple-element.28), channel_id=1, source_target_pairs={{1,2},{3,0},{2,1},{0,3},{5,6},{7,4},{6,5},{4,7},{9,10},{11,8},{10,... | collective-permute-start | bytes 122888 | tf_op jit(solution)/shard_map/ppermute | solution.py:424
  35.4 10.7 %copy-start.1 = (f32[3,8,32,128]{3,2,1,0:T(8,128)S(1)}, f32[3,8,32,128]{3,2,1,0:T(8,128)}, u32[]{:S(2)}) copy-start(f32[3,8,32,128]{3,2,1,0:T(8,128)} %e.3) | copy-start | bytes 1179652
  35.4 10.7 %copy-start.3 = (f32[3,8,32,128]{3,2,1,0:T(8,128)S(1)}, f32[3,8,32,128]{3,2,1,0:T(8,128)}, u32[]{:S(2)}) copy-start(f32[3,8,32,128]{3,2,1,0:T(8,128)} %h.3) | copy-start | bytes 1179652
  35.8 10.2 %collective-permute-start.6 = (f32[176,128]{1,0:T(8,128)S(1)}, f32[176,128]{1,0:T(8,128)S(1)}, u32[]{:S(2)}, u32[]{:S(2)}) collective-permute-start(f32[176,128]{1,0:T(8,128)S(1)} %get-tuple-element.32), channel_id=1, source_target_pairs={{0,16},{16,32},{32,48},{48,64},{64,80},{80,96},{96,112},{112,0},{1... | collective-permute-start | bytes 270344 | tf_op jit(solution)/shard_map/ppermute | solution.py:429
  40.2 5.9 %collective-permute-start.7 = (f32[152,128]{1,0:T(8,128)S(1)}, f32[152,128]{1,0:T(8,128)S(1)}, u32[]{:S(2)}, u32[]{:S(2)}) collective-permute-start(f32[152,128]{1,0:T(8,128)S(1)} %get-tuple-element.33), channel_id=1, source_target_pairs={{0,112},{16,0},{32,16},{48,32},{64,48},{80,64},{96,80},{112,96},{1... | collective-permute-start | bytes 233480 | tf_op jit(solution)/shard_map/ppermute | solution.py:430
  42.2 3.9 %copy-start.10 = (s32[8]{0:T(128)S(1)}, s32[8]{0:T(128)}, u32[]{:S(2)}) copy-start(s32[8]{0:T(128)} %layer.1) | copy-start | bytes 100
  42.2 3.9 %copy-start.11 = (s32[3]{0:T(128)S(1)}, s32[3]{0:T(128)}, u32[]{:S(2)}) copy-start(s32[3]{0:T(128)} %pml.1) | copy-start | bytes 40

commit v2 on v1

--- a/solution.py
+++ b/solution.py
@@ -16,7 +16,19 @@
 COMPS = 14
 BELOW = [(k, 1) for k in range(14)] + [(k, 2) for k in (0, 1, 2, 3, 4, 6, 7, 8, 9, 10)]
 ABOVE = [(k, 0) for k in range(13)] + [(k, 1) for k in (0, 1, 6, 7)]
-BELOW_TILES, ABOVE_TILES = (len(BELOW) + 1) // 2, (len(ABOVE) + 1) // 2
+BELOW_ROWS = [(k, 1) for k in range(14)] + [(2, 2), (8, 2)]
+BELOW_LAST = [(2, 1), (8, 1)]
+ABOVE_ROWS = [(k, 0) for k in range(13)] + [(1, 1), (7, 1)]
+ABOVE_LAST = [(1, 0), (7, 0)]
+BELOW_SIDE = [(k, 1) for k in range(14)] + [(2, 2), (8, 2)]
+ABOVE_SIDE = [(k, 0) for k in range(13)] + [(0, 1), (6, 1)]
+
+
+def tiles_of(rows, last):
+    return (len(rows) + 3) // 4 + (len(last) + 3) // 4
+
+
+BELOW_TILES, ABOVE_TILES = tiles_of(BELOW_ROWS, BELOW_LAST), tiles_of(ABOVE_ROWS, ABOVE_LAST)
 
 
 def lanes(rows=8):
@@ -70,33 +82,42 @@
     return right, left
 
 
-def first_kernel(e, h, ae, ah, eps, cur, zu, zd, ya, yb, strips, right_out, left_out):
-    def plane(k, p):
-        if k < 12:
-            return (e, h, ae, ah)[k // 3][k % 3, p]
-        return (eps, cur)[k - 12][p]
-
+def first_kernel(e, h, ae, ah, eps, cur, f, ya, yb, sems):
+    copies = []
+    for k in range(COMPS):
+        source = (e, h, ae, ah)[k // 3].at[k % 3] if k < 12 else (eps, cur)[k - 12]
+        copies.append(pltpu.make_async_copy(source, f.at[k, 2 : PLANES + 2, 0:ROWS], sems.at[k]))
+    for copy in copies:
+        copy.start()
     even = parity("gy")
     sub = subs()
     for k in range(COMPS):
+        copies[k].wait()
         for half in range(2):
             up = jnp.zeros((8, COLS), F32)
             down = jnp.zeros((8, COLS), F32)
             for j in range(4):
-                block = plane(k, 4 * half + j)
+                idx = 4 * half + j + 2
                 mask = (sub >> 1) == j
-                up = jnp.where(mask, turn(block[24:32], 2 * j - 6, 0), up)
-                down = jnp.where(mask, turn(block[0:8], 2 * j, 0), down)
+                up = jnp.where(mask, turn(f[k, idx, 24:32], 2 * j - 6, 0), up)
+                down = jnp.where(mask, turn(f[k, idx, 0:8], 2 * j, 0), down)
             at = 8 * (2 * k + half)
             ya[at : at + 8] = jnp.where(even, up, down)
             yb[at : at + 8] = jnp.where(even, down, up)
+
+
+def face_kernel(f, after_a, after_b, zu, zd):
+    del after_a, after_b
     for i, (k, below) in enumerate(BELOW):
-        zu[i] = plane(k, PLANES - below)
+        zu[i] = f[k, PLANES + 2 - below, 0:ROWS]
     for i, (k, above) in enumerate(ABOVE):
-        zd[i] = plane(k, above)
+        zd[i] = f[k, above + 2, 0:ROWS]
+
+
+def strip_kernel(f, strips, right_out, left_out):
     values = []
     for k in range(COMPS):
-        value = strip([plane(k, p) for p in range(PLANES)], ROWS)
+        value = strip([f[k, p + 2, 0:ROWS] for p in range(PLANES)], ROWS)
         strips[k] = value
         values.append(value)
     right, left = face_pack(values, ROWS)
@@ -135,24 +156,33 @@
         xb[a, ROWS:TALL] = jnp.where(even, left[a], right[a])
 
 
-def rim_pack(out, items, plane_of, tiles, side, first_lane):
+def rim_pack(out, rows, last, sides, plane_of, extra, tiles, side):
     sub = subs()
-    kept = (sub < 2) | (sub >= 6)
-    count = (len(items) + 1) // 2
-    for i in range(count):
-        k, at = items[2 * i]
-        tile = tiles[k, plane_of(at)]
-        if 2 * i + 1 < len(items):
-            k, at = items[2 * i + 1]
-            tile = jnp.where(kept, tile, turn(tiles[k, plane_of(at)], 4, 0))
-        out[8 * i : 8 * i + 8] = tile
+    count = 0
+    for items, first in ((rows, 1), (last, extra)):
+        for i in range(0, len(items), 4):
+            tile = jnp.zeros((8, COLS), F32)
+            for j, (k, at) in enumerate(items[i : i + 4]):
+                tile = jnp.where((sub >> 1) == j, turn(tiles[k, plane_of(at)], 2 * j + first, 0), tile)
+            out[8 * count : 8 * count + 8] = tile
+            count += 1
     lane = lanes(TALL)
-    for a in range(2):
-        packed = jnp.zeros((TALL, COLS), F32)
-        for k in range(8 * a, min(8 * a + 8, COMPS)):
-            packed = jnp.where((lane >> 4) == k % 8, turn(side[k], 16 * (k % 8) - first_lane, 1), packed)
-        at = 8 * count + TALL * a
-        out[at : at + TALL] = packed
+    packed = jnp.zeros((TALL, COLS), F32)
+    for i, (k, at) in enumerate(sides):
+        packed = jnp.where((lane >> 3) == i, turn(side[k], 8 * i - 8 * (plane_of(at) + 2), 1), packed)
+    out[8 * count : 8 * count + TALL] = packed
+
+
+def rim_rows(rim, rows, last, extra):
+    got = {}
+    for i, item in enumerate(rows):
+        at = 8 * (i // 4)
+        got[item] = turn(rim[at : at + 8], -(2 * (i % 4) + 1), 0)
+    for i, item in enumerate(last):
+        at = 8 * ((len(rows) + 3) // 4 + i // 4)
+        tile = turn(rim[at : at + 8], -(2 * (i % 4) + extra), 0)
+        got[item] = jnp.where(subs() == (1 if extra == 0 else 6), tile, got[item])
+    return got
 
 
 def third_kernel(xa, xb, strips, strips_rim, tiles, sides, rim_up, rim_down):
@@ -175,8 +205,8 @@
         value = jnp.where(own, value, 0.0)
         sides[k] = value
         side.append(value)
-    rim_pack(rim_up, BELOW, lambda below: PLANES - below, tiles, side, 64)
-    rim_pack(rim_down, ABOVE, lambda above: above, tiles, side, 16)
+    rim_pack(rim_up, BELOW_ROWS, BELOW_LAST, BELOW_SIDE, lambda below: PLANES - below, 0, tiles, side)
+    rim_pack(rim_down, ABOVE_ROWS, ABOVE_LAST, ABOVE_SIDE, lambda above: above, 2, tiles, side)
 
 
 def profile(position, extent, thickness):
@@ -202,45 +232,43 @@
 
 
 def main_kernel(
-    layer, pml, start, e, h, ae, ah, eps, cur, zu, zd, tiles, sides, rim_up, rim_down,
-    sums, e_out, h_out,
-    f, one, rr, qq, gg, xf, xone, xr, xq, xg,
+    layer, pml, start, own, zu, zd, tiles, sides, rim_up, rim_down,
+    f, sums, e_out, h_out,
+    one, rr, qq, gg, xf, xone, xr, xq, xg,
 ):
     iz, iy, ix = (lax.axis_index(a) for a in ("gz", "gy", "gx"))
     nz, ny, nx = (PLANES * lax.axis_size("gz"), ROWS * lax.axis_size("gy"), COLS * lax.axis_size("gx"))
     has_above = (iz < lax.axis_size("gz") - 1).astype(F32)
     has_below = (iz > 0).astype(F32)
+    del own
     for k in range(COMPS):
         for p in range(PLANES):
-            if k < 12:
-                f[k, p + 2, 0:ROWS] = (e, h, ae, ah)[k // 3][k % 3, p]
-            else:
-                f[k, p + 2, 0:ROWS] = (eps, cur)[k - 12][p]
             f[k, p + 2, ROWS:TALL] = tiles[k, p]
     sent = set()
-    for items, faces, rim, place, keep in (
-        (BELOW, zu, rim_up, lambda below: 2 - below, has_below),
-        (ABOVE, zd, rim_down, lambda above: PLANES + 2 + above, has_above),
+    lane = lanes(TALL)
+    row = subs(TALL)
+    for k in range(COMPS):
+        xf[k] = sides[k]
+    for items, faces, rim, lists, place, extra, keep in (
+        (BELOW, zu, rim_up, (BELOW_ROWS, BELOW_LAST, BELOW_SIDE), lambda below: 2 - below, 0, has_below),
+        (ABOVE, zd, rim_down, (ABOVE_ROWS, ABOVE_LAST, ABOVE_SIDE), lambda above: PLANES + 2 + above, 2, has_above),
     ):
+        rows, last, side = lists
+        edge = rim_rows(rim, rows, last, extra)
         for i, (k, at) in enumerate(items):
             idx = place(at)
             sent.add((k, idx))
-            tile = rim[8 * (i // 2) : 8 * (i // 2) + 8]
             f[k, idx, 0:ROWS] = faces[i] * keep
-            f[k, idx, ROWS:TALL] = turn(tile, 4 * (i % 2), 0) * keep
+            f[k, idx, ROWS:TALL] = edge[k, at] * keep if (k, at) in edge else jnp.zeros((8, COLS), F32)
+        at = 8 * tiles_of(rows, last)
+        packed = rim[at : at + TALL] * keep
+        for i, (k, at) in enumerate(side):
+            idx = place(at)
+            xf[k] = jnp.where((lane >> 3) == idx, turn(packed, 8 * idx - 8 * i, 1), xf[k])
     for k in range(COMPS):
         for idx in (0, 1, PLANES + 2, PLANES + 3):
             if (k, idx) not in sent:
                 f[k, idx] = jnp.zeros((TALL, COLS), F32)
-    lane = lanes(TALL)
-    row = subs(TALL)
-    for k in range(COMPS):
-        at = 8 * BELOW_TILES + TALL * (k // 8)
-        low = turn(rim_up[at : at + TALL], -16 * (k % 8), 1) * has_below
-        at = 8 * ABOVE_TILES + TALL * (k // 8)
-        high = turn(rim_down[at : at + TALL], 80 - 16 * (k % 8), 1) * has_above
-        value = jnp.where(lane < 16, low, sides[k])
-        xf[k] = jnp.where((lane >= 80) & (lane < 96), high, value)
     y_at = ROWS * iy + jnp.where(row >= 36, row - TALL, row)
     x_at = COLS * ix + lane
     y_in = (y_at >= 0) & (y_at < ny)
@@ -377,19 +405,21 @@
     out[...] = total
 
 
-def call(kernel, outs, scratch=(), scalars=0, flops=1000000):
+def call(kernel, outs, scratch=(), scalars=0, far=0, aliases=None):
     def run(*args):
+        near = len(args) - scalars - far
         specs = [pl.BlockSpec(memory_space=pltpu.SMEM)] * scalars
-        specs += [pl.BlockSpec(memory_space=pltpu.VMEM)] * (len(args) - scalars)
+        specs += [pl.BlockSpec(memory_space=pltpu.VMEM)] * near + [pl.BlockSpec(memory_space=pl.ANY)] * far
         size = sum(4 * math.prod(s) for s in outs) + sum(4 * math.prod(a.shape) for a in args)
         return pl.pallas_call(
             kernel,
             out_shape=[jax.ShapeDtypeStruct(s, F32) for s in outs],
             in_specs=specs,
             out_specs=[pl.BlockSpec(memory_space=pltpu.VMEM)] * len(outs),
-            scratch_shapes=[pltpu.VMEM(s, F32) for s in scratch],
+            scratch_shapes=[pltpu.VMEM(s, F32) if isinstance(s, tuple) else s for s in scratch],
+            input_output_aliases=aliases or {},
             compiler_params=pltpu.CompilerParams(vmem_limit_bytes=24 * 2**20),
-            cost_estimate=pl.CostEstimate(flops=flops, bytes_accessed=size, transcendentals=0),
+            cost_estimate=pl.CostEstimate(flops=1000000, bytes_accessed=size, transcendentals=0),
         )(*args)
 
     return run
@@ -400,21 +430,23 @@
     return [(i, (i + step) % count) for i in range(count)]
 
 
-def swaps(axis, first):
+def swaps(axis, first, wrap=True):
     count = lax.axis_size(axis)
-    pairs = [(i % count, (i + 1) % count) for i in range(first, count, 2)]
+    pairs = [(i, (i + 1) % count) for i in range(first, count, 2) if wrap or i + 1 < count]
     return pairs + [(b, a) for a, b in pairs]
 
 
 def local(e_start, h_start, adjoint_e, adjoint_h, permittivity, current, layer_of_cell, pml_cells, start_step):
     raw = (e_start, h_start, adjoint_e, adjoint_h, permittivity, current)
-    block = (ROWS, COLS)
-    zu, zd, ya, yb, strips, right, left = call(
-        first_kernel,
-        [(len(BELOW),) + block, (len(ABOVE),) + block, (16 * COMPS, COLS), (16 * COMPS, COLS), (COMPS,) + block, (2,) + block, (2,) + block],
+    raw = [pltpu.with_memory_space_constraint(a, pltpu.HBM) for a in raw]
+    block, deep, tall = (ROWS, COLS), (DEEP, TALL, COLS), (TALL, COLS)
+    f, ya, yb = call(
+        first_kernel, [(COMPS,) + deep, (16 * COMPS, COLS), (16 * COMPS, COLS)], [pltpu.SemaphoreType.DMA((COMPS,))], far=6
     )(*raw)
+    yb = lax.ppermute(yb, "gy", swaps("gy", 1))
     ya = lax.ppermute(ya, "gy", swaps("gy", 0))
-    yb = lax.ppermute(yb, "gy", swaps("gy", 1))
+    strips, right, left = call(strip_kernel, [(COMPS,) + block, (2,) + block, (2,) + block])(f)
+    zu, zd = call(face_kernel, [(len(BELOW),) + block, (len(ABOVE),) + block], far=2)(f, ya, yb)
     zu = lax.ppermute(zu, "gz", ring("gz", 1))
     zd = lax.ppermute(zd, "gz", ring("gz", -1))
     tiles, strips_rim, xa, xb = call(
@@ -424,17 +456,17 @@
     xb = lax.ppermute(xb, "gx", swaps("gx", 1))
     sides, rim_up, rim_down = call(
         third_kernel,
-        [(COMPS, TALL, COLS), (8 * BELOW_TILES + 2 * TALL, COLS), (8 * ABOVE_TILES + 2 * TALL, COLS)],
+        [(COMPS,) + tall, (8 * BELOW_TILES + TALL, COLS), (8 * ABOVE_TILES + TALL, COLS)],
     )(xa, xb, strips, strips_rim, tiles)
     rim_up = lax.ppermute(rim_up, "gz", ring("gz", 1))
     rim_down = lax.ppermute(rim_down, "gz", ring("gz", -1))
-    deep, tall = (DEEP, TALL, COLS), (TALL, COLS)
-    sums, e_out, h_out = call(
+    _, sums, e_out, h_out = call(
         main_kernel,
-        [(LAYERS,) + block, (3, PLANES) + block, (3, PLANES) + block],
-        [(COMPS,) + deep, (6,) + deep, deep, deep, deep, (COMPS,) + tall, (6,) + tall, tall, tall, tall],
+        [(COMPS,) + deep, (LAYERS,) + block, (3, PLANES) + block, (3, PLANES) + block],
+        [(6,) + deep, deep, deep, deep, (COMPS,) + tall, (6,) + tall, tall, tall, tall],
         scalars=3,
-    )(layer_of_cell, pml_cells, start_step, *raw, zu, zd, tiles, sides, rim_up, rim_down)
+        aliases={3: 0},
+    )(layer_of_cell, pml_cells, start_step, f, zu, zd, tiles, sides, rim_up, rim_down)
     count = lax.axis_size("gz")
     got = lax.all_to_all(sums, "gz", 0, 0, tiled=True)
     (gradient,) = call(sum_kernel, [(LAYERS // count,) + block])(got.reshape((count, LAYERS // count) + block))

time: 67.1 us -> 52.6 us (0.78)
  waiting for transfers between devices: 20.4 us -> 9.26 us
  local copies, waits for them, and re-layouts: 5.81 us -> 0.01 us
  Pallas kernels: 8.83 us -> 10.5 us
  blocking collectives: 13 us -> 13.7 us
    ppermute x1, waiting for transfers between devices: 13.3 us -> 3.35 us  [local(): yb = lax.ppermute(yb, 'gy', swaps('gy', 1))]
    unnamed x24 -> x4, local copies, waits for them, and re-layouts: 5.81 us -> 0.01 us
    ppermute x1, starting transfers between devices: 1.41 us -> 4.64 us  [local(): rim_down = lax.ppermute(rim_down, 'gz', ring('gz', -1))]
    ppermute x1, starting transfers between devices: 4.3 us -> 1.07 us  [local(): rim_up = lax.ppermute(rim_up, 'gz', ring('gz', 1))]
    ppermute x1, waiting for transfers between devices: 3.82 us -> 1.36 us  [local(): rim_down = lax.ppermute(rim_down, 'gz', ring('gz', -1))]
    pallas_call x5 -> x7, Pallas kernels: 8.83 us -> 10.5 us  [run(): pl.pallas_call(kernel, out_shape=[jax.ShapeDtypeStruct(s, F32) for s in o...]
    ppermute x1, waiting for transfers between devices: 0.01 us -> 1.43 us  [local(): rim_up = lax.ppermute(rim_up, 'gz', ring('gz', 1))]
    ppermute x1, starting transfers between devices: 1.26 us -> 2.12 us  [local(): yb = lax.ppermute(yb, 'gy', swaps('gy', 1))]
  transfers between devices with their start and end apart: 8 -> 8, of which waited for: 5 -> 5; matrix products, arithmetic and copies ran while one was open for 0% -> 0% of each run, Pallas kernels for 1% -> 3%
where the time goes in v2:
time: 52.6 us; the launch traced here: 52.4 us
  starting transfers between devices  17.7 us (34%)
  blocking collectives  13.7 us (26%)
  Pallas kernels  10.5 us (20%)
  waiting for transfers between devices  9.26 us (18%)
  between operations  1.34 us (3%)
    all_to_all x1, blocking collectives, local(): got = lax.all_to_all(sums, 'gz', 0, 0, tiled=True)  13.7 us
    pallas_call x7, Pallas kernels, run(): pl.pallas_call(kernel, out_shape=[jax.ShapeDtypeStruct(s, F32) for s in o...  10.5 us
    ppermute x1, starting transfers between devices, local(): rim_down = lax.ppermute(rim_down, 'gz', ring('gz', -1))  4.64 us
    ppermute x1, starting transfers between devices, local(): zu = lax.ppermute(zu, 'gz', ring('gz', 1))  3.54 us
    ppermute x1, waiting for transfers between devices, local(): yb = lax.ppermute(yb, 'gy', swaps('gy', 1))  3.35 us
    ppermute x1, waiting for transfers between devices, local(): xb = lax.ppermute(xb, 'gx', swaps('gx', 1))  2.7 us
    ppermute x1, starting transfers between devices, local(): zd = lax.ppermute(zd, 'gz', ring('gz', -1))  2.53 us
    ppermute x1, starting transfers between devices, local(): yb = lax.ppermute(yb, 'gy', swaps('gy', 1))  2.12 us
  transfers between devices with their start and end apart: 8, of which 5 were waited for; matrix products, arithmetic and copies ran while one was open for 0% of the time, Pallas kernels for 3%

profile of v2, /device:TPU:0, one launch (start us, length us, event | category | flops | bytes accessed | tf_op | source)
XLA Modules:
  0.0 52.4 jit_solution(295603482504982064)
XLA Ops:
  0.6 1.6 %shard_map.112 = (f32[14,12,40,128]{3,2,1,0:T(8,128)S(1)}, f32[224,128]{1,0:T(8,128)S(1)}, f32[224,128]{1,0:T(8,128)S(1)}) custom-call(f32[3,8,32,128]{3,2,1,0:T(8,128)} %e.1, f32[3,8,32,128]{3,2,1,0:T(8,128)} %h.1, f32[3,8,32,128]{3,2,1,0:T(8,128)} %ae.1, f32[3,8,32,128]{3,2,1,0:T(8,128)} %ah.1, f32[8,32,128]{2,1,0:T(8,128)} %eps.1, f32[8,32,128]{2,1,0:T(8,128)} %cur.1), custom_call_target="tpu_custom_call" | custom-call | flops 1000000 | bytes 5505024 | tf_op jit(solution)/shard_map/pallas_call | solution.py:414
  2.3 0.1 collective-permute-start
  2.4 2.1 %collective-permute-start.1 = (f32[224,128]{1,0:T(8,128)S(1)}, f32[224,128]{1,0:T(8,128)S(1)}, u32[]{:S(2)}, u32[]{:S(2)}) collective-permute-start(f32[224,128]{1,0:T(8,128)S(1)} %get-tuple-element.23), channel_id=1, source_target_pairs={{4,8},{12,0},{8,4},{0,12},{5,9},{13,1},{9,5},{1,13},{6,10},{14,2},... | collective-permute-start | bytes 344072 | tf_op jit(solution)/shard_map/ppermute | solution.py:446
  4.5 0.0 collective-permute-done.after_a.ya
  4.5 3.4 %collective-permute-done.1.after_b.yb = f32[224,128]{1,0:T(8,128)S(1)} collective-permute-done((f32[224,128]{1,0:T(8,128)S(1)}, f32[224,128]{1,0:T(8,128)S(1)}, u32[]{:S(2)}, u32[]{:S(2)}) %collective-permute-start.1) | collective-permute-done | bytes 114720 | tf_op jit(solution)/shard_map/ppermute | solution.py:446
  7.9 0.0 copy-start
  7.9 0.0 copy-start.1
  7.9 3.5 %collective-permute-start.2 = (f32[24,32,128]{2,1,0:T(8,128)S(1)}, f32[24,32,128]{2,1,0:T(8,128)S(1)}, u32[]{:S(2)}, u32[]{:S(2)}) collective-permute-start(f32[24,32,128]{2,1,0:T(8,128)S(1)} %get-tuple-element.24), channel_id=1, source_target_pairs={{0,16},{16,32},{32,48},{48,64},{64,80},{80,96},{96,112},{112,0},{1... | collective-permute-start | bytes 1179656 | tf_op jit(solution)/shard_map/ppermute | solution.py:450
  11.4 2.5 %collective-permute-start.3 = (f32[17,32,128]{2,1,0:T(8,128)S(1)}, f32[17,32,128]{2,1,0:T(8,128)S(1)}, u32[]{:S(2)}, u32[]{:S(2)}) collective-permute-start(f32[17,32,128]{2,1,0:T(8,128)S(1)} %get-tuple-element.25), channel_id=1, source_target_pairs={{0,112},{16,0},{32,16},{48,32},{64,48},{80,64},{96,80},{112,96},{1... | collective-permute-start | bytes 835592 | tf_op jit(solution)/shard_map/ppermute | solution.py:451
  14.0 0.6 %shard_map.114 = (f32[14,32,128]{2,1,0:T(8,128)S(1)}, f32[2,32,128]{2,1,0:T(8,128)S(1)}, f32[2,32,128]{2,1,0:T(8,128)S(1)}) custom-call(f32[14,12,40,128]{3,2,1,0:T(8,128)S(1)} %get-tuple-element.21.f.own), custom_call_target="tpu_custom_call" | custom-call | flops 1000000 | bytes 3735552 | tf_op jit(solution)/shard_map/pallas_call | solution.py:414
  14.6 0.3 shard_map.115
  14.9 1.6 %collective-permute-start.4 = (f32[2,40,128]{2,1,0:T(8,128)S(1)}, f32[2,40,128]{2,1,0:T(8,128)S(1)}, u32[]{:S(2)}, u32[]{:S(2)}) collective-permute-start(f32[2,40,128]{2,1,0:T(8,128)S(1)} %get-tuple-element.29), channel_id=1, source_target_pairs={{0,1},{2,3},{1,0},{3,2},{4,5},{6,7},{5,4},{7,6},{8,9},{10,11},{9,8... | collective-permute-start | bytes 122888 | tf_op jit(solution)/shard_map/ppermute | solution.py:455
  16.5 2.1 %collective-permute-start.5 = (f32[2,40,128]{2,1,0:T(8,128)S(1)}, f32[2,40,128]{2,1,0:T(8,128)S(1)}, u32[]{:S(2)}, u32[]{:S(2)}) collective-permute-start(f32[2,40,128]{2,1,0:T(8,128)S(1)} %get-tuple-element.30), channel_id=1, source_target_pairs={{1,2},{3,0},{2,1},{0,3},{5,6},{7,4},{6,5},{4,7},{9,10},{11,8},{10,... | collective-permute-start | bytes 122888 | tf_op jit(solution)/shard_map/ppermute | solution.py:456
  18.6 0.4 collective-permute-done.4.xa
  19.0 2.7 %collective-permute-done.5.xb = f32[2,40,128]{2,1,0:T(8,128)S(1)} collective-permute-done((f32[2,40,128]{2,1,0:T(8,128)S(1)}, f32[2,40,128]{2,1,0:T(8,128)S(1)}, u32[]{:S(2)}, u32[]{:S(2)}) %collective-permute-start.5) | collective-permute-done | bytes 40992 | tf_op jit(solution)/shard_map/ppermute | solution.py:456
  21.7 0.4 shard_map.116
  22.1 1.1 %collective-permute-start.6 = (f32[80,128]{1,0:T(8,128)S(1)}, f32[80,128]{1,0:T(8,128)S(1)}, u32[]{:S(2)}, u32[]{:S(2)}) collective-permute-start(f32[80,128]{1,0:T(8,128)S(1)} %get-tuple-element.34), channel_id=1, source_target_pairs={{0,16},{16,32},{32,48},{48,64},{64,80},{80,96},{96,112},{112,0},{1... | collective-permute-start | bytes 122888 | tf_op jit(solution)/shard_map/ppermute | solution.py:461
  23.2 4.6 %collective-permute-start.7 = (f32[80,128]{1,0:T(8,128)S(1)}, f32[80,128]{1,0:T(8,128)S(1)}, u32[]{:S(2)}, u32[]{:S(2)}) collective-permute-start(f32[80,128]{1,0:T(8,128)S(1)} %get-tuple-element.35), channel_id=1, source_target_pairs={{0,112},{16,0},{32,16},{48,32},{64,48},{80,64},{96,80},{112,96},{1... | collective-permute-start | bytes 122888 | tf_op jit(solution)/shard_map/ppermute | solution.py:462
  28.5 1.4 %collective-permute-done.6.rim_up = f32[80,128]{1,0:T(8,128)S(1)} collective-permute-done((f32[80,128]{1,0:T(8,128)S(1)}, f32[80,128]{1,0:T(8,128)S(1)}, u32[]{:S(2)}, u32[]{:S(2)}) %collective-permute-start.6) | collective-permute-done | bytes 40992 | tf_op jit(solution)/shard_map/ppermute | solution.py:461
  29.9 1.4 %collective-permute-done.7.rim_down = f32[80,128]{1,0:T(8,128)S(1)} collective-permute-done((f32[80,128]{1,0:T(8,128)S(1)}, f32[80,128]{1,0:T(8,128)S(1)}, u32[]{:S(2)}, u32[]{:S(2)}) %collective-permute-start.7) | collective-permute-done | bytes 40992 | tf_op jit(solution)/shard_map/ppermute | solution.py:462
  31.3 0.0 collective-permute-done.3.zd
  31.3 0.0 collective-permute-done.2.zu
  31.3 0.0 copy-done
  31.3 0.0 copy-done.1
  31.3 6.8 %shard_map.117 = (f32[14,12,40,128]{3,2,1,0:T(8,128)S(1)}, f32[16,32,128]{2,1,0:T(8,128)S(1)}, f32[3,8,32,128]{3,2,1,0:T(8,128)}, f32[3,8,32,128]{3,2,1,0:T(8,128)}) custom-call(s32[8]{0:T(128)S(1)} %copy-done, s32[3]{0:T(128)S(1)} %copy-done.1, s32[1]{0:T(128)S(6)} %copy.14.start, ...), custom_call_target="tpu_custom_call", output_to_operand_aliasing={{0}: (3, {})} | custom-call | flops 1000000 | bytes 9429040 | tf_op jit(solution)/shard_map/pallas_call | solution.py:414
  38.1 13.7 %all_to_all.5 = f32[16,32,128]{2,1,0:T(8,128)S(1)} all-to-all(f32[16,32,128]{2,1,0:T(8,128)S(1)} %get-tuple-element.36), channel_id=1, replica_groups=mesh['gz'=8,'gy'=4,'gx'=4] {'gz'}, dimensions={0} | all-to-all | bytes 524288 | tf_op jit(solution)/shard_map/all_to_all | solution.py:471
  51.8 0.6 %shard_map.118 = f32[2,32,128]{2,1,0:T(8,128)} custom-call(f32[8,2,32,128]{3,2,1,0:T(8,128)S(1)} %bitcast.1), custom_call_target="tpu_custom_call" | custom-call | flops 1000000 | bytes 294912 | tf_op jit(solution)/shard_map/pallas_call | solution.py:414
  (1 shorter events, 0.0 us)
Async XLA Ops:
  2.3 2.2 %collective-permute-start = (f32[224,128]{1,0:T(8,128)S(1)}, f32[224,128]{1,0:T(8,128)S(1)}, u32[]{:S(2)}, u32[]{:S(2)}) collective-permute-start(f32[224,128]{1,0:T(8,128)S(1)} %get-tuple-element.22), channel_id=1, source_target_pairs={{0,4},{8,12},{4,0},{12,8},{1,5},{9,13},{5,1},{13,9},{2,6},{10,14},... | collective-permute-start | bytes 344072 | tf_op jit(solution)/shard_map/ppermute | solution.py:447
  2.4 5.5 %collective-permute-start.1 = (f32[224,128]{1,0:T(8,128)S(1)}, f32[224,128]{1,0:T(8,128)S(1)}, u32[]{:S(2)}, u32[]{:S(2)}) collective-permute-start(f32[224,128]{1,0:T(8,128)S(1)} %get-tuple-element.23), channel_id=1, source_target_pairs={{4,8},{12,0},{8,4},{0,12},{5,9},{13,1},{9,5},{1,13},{6,10},{14,2},... | collective-permute-start | bytes 344072 | tf_op jit(solution)/shard_map/ppermute | solution.py:446
  7.9 23.4 %copy-start = (s32[8]{0:T(128)S(1)}, s32[8]{0:T(128)}, u32[]{:S(2)}) copy-start(s32[8]{0:T(128)} %layer.1) | copy-start | bytes 100
  7.9 23.4 %copy-start.1 = (s32[3]{0:T(128)S(1)}, s32[3]{0:T(128)}, u32[]{:S(2)}) copy-start(s32[3]{0:T(128)} %pml.1) | copy-start | bytes 40
  7.9 23.4 %collective-permute-start.2 = (f32[24,32,128]{2,1,0:T(8,128)S(1)}, f32[24,32,128]{2,1,0:T(8,128)S(1)}, u32[]{:S(2)}, u32[]{:S(2)}) collective-permute-start(f32[24,32,128]{2,1,0:T(8,128)S(1)} %get-tuple-element.24), channel_id=1, source_target_pairs={{0,16},{16,32},{32,48},{48,64},{64,80},{80,96},{96,112},{112,0},{1... | collective-permute-start | bytes 1179656 | tf_op jit(solution)/shard_map/ppermute | solution.py:450
  11.4 19.8 %collective-permute-start.3 = (f32[17,32,128]{2,1,0:T(8,128)S(1)}, f32[17,32,128]{2,1,0:T(8,128)S(1)}, u32[]{:S(2)}, u32[]{:S(2)}) collective-permute-start(f32[17,32,128]{2,1,0:T(8,128)S(1)} %get-tuple-element.25), channel_id=1, source_target_pairs={{0,112},{16,0},{32,16},{48,32},{64,48},{80,64},{96,80},{112,96},{1... | collective-permute-start | bytes 835592 | tf_op jit(solution)/shard_map/ppermute | solution.py:451
  14.9 4.1 %collective-permute-start.4 = (f32[2,40,128]{2,1,0:T(8,128)S(1)}, f32[2,40,128]{2,1,0:T(8,128)S(1)}, u32[]{:S(2)}, u32[]{:S(2)}) collective-permute-start(f32[2,40,128]{2,1,0:T(8,128)S(1)} %get-tuple-element.29), channel_id=1, source_target_pairs={{0,1},{2,3},{1,0},{3,2},{4,5},{6,7},{5,4},{7,6},{8,9},{10,11},{9,8... | collective-permute-start | bytes 122888 | tf_op jit(solution)/shard_map/ppermute | solution.py:455
  16.5 5.2 %collective-permute-start.5 = (f32[2,40,128]{2,1,0:T(8,128)S(1)}, f32[2,40,128]{2,1,0:T(8,128)S(1)}, u32[]{:S(2)}, u32[]{:S(2)}) collective-permute-start(f32[2,40,128]{2,1,0:T(8,128)S(1)} %get-tuple-element.30), channel_id=1, source_target_pairs={{1,2},{3,0},{2,1},{0,3},{5,6},{7,4},{6,5},{4,7},{9,10},{11,8},{10,... | collective-permute-start | bytes 122888 | tf_op jit(solution)/shard_map/ppermute | solution.py:456
  22.1 7.8 %collective-permute-start.6 = (f32[80,128]{1,0:T(8,128)S(1)}, f32[80,128]{1,0:T(8,128)S(1)}, u32[]{:S(2)}, u32[]{:S(2)}) collective-permute-start(f32[80,128]{1,0:T(8,128)S(1)} %get-tuple-element.34), channel_id=1, source_target_pairs={{0,16},{16,32},{32,48},{48,64},{64,80},{80,96},{96,112},{112,0},{1... | collective-permute-start | bytes 122888 | tf_op jit(solution)/shard_map/ppermute | solution.py:461
  23.2 8.1 %collective-permute-start.7 = (f32[80,128]{1,0:T(8,128)S(1)}, f32[80,128]{1,0:T(8,128)S(1)}, u32[]{:S(2)}, u32[]{:S(2)}) collective-permute-start(f32[80,128]{1,0:T(8,128)S(1)} %get-tuple-element.35), channel_id=1, source_target_pairs={{0,112},{16,0},{32,16},{48,32},{64,48},{80,64},{96,80},{112,96},{1... | collective-permute-start | bytes 122888 | tf_op jit(solution)/shard_map/ppermute | solution.py:462

commit v3 on v2

v3 whole, which is shorter than its diff:
```python
import functools
import math

import jax
import jax.numpy as jnp
from jax import lax
from jax.experimental import pallas as pl
from jax.experimental.pallas import tpu as pltpu
from jax.sharding import PartitionSpec as P

F32 = jnp.float32
PLANES, ROWS, COLS = 8, 32, 128
DEEP, TALL = PLANES + 4, ROWS + 8
LAYERS = 16
PERIOD = 64
COMPS = 14
HALF = (3, 4, 5, 9, 10, 11)
UP_FACES = [(k, 7) for k in range(14)] + [(k, 6) for k in (3, 4, 9, 10)]
DOWN_FACES = [(k, 0) for k in (0, 1, 6, 7, 12) + HALF]
UP_ROWS = [(k, 7, 7) for k in range(14)] + [(k, 7, 0) for k in (2, 8)]
DOWN_ROWS = [(k, 0, 7) for k in (0, 1, 6, 7, 12, 3, 5, 9, 11)] + [(k, 0, 6) for k in (1, 7)]
UP_SIDES = [(k, 7) for k in range(14)] + [(k, 6) for k in (4, 10)]
DOWN_SIDES = DOWN_FACES


def face_rows(faces, rows):
    return ROWS * len(faces) + 8 * ((len(rows) + 3) // 4)


def lanes(rows=8):
    return lax.broadcasted_iota(jnp.int32, (rows, COLS), 1)


def subs(rows=8):
    return lax.broadcasted_iota(jnp.int32, (rows, COLS), 0)


def turn(value, shift, axis):
    shift = shift % value.shape[axis]
    return value if shift == 0 else pltpu.roll(value, shift, axis)


def slot(k):
    return k // 8, (k % 8) // 4, k % 4


def slot_mask(k, rows):
    _, half, pair = slot(k)
    lane = lanes(rows)
    inside = ((lane - 16 - 64 * half) & 127) < 64
    return inside & (((lane & 7) >> 1) == pair)


def window(p, rows):
    lane = lanes(rows)
    return (lane >= 8 * (p + 2)) & (lane < 8 * (p + 2) + 4)


def parity(axis):
    return lax.rem(lax.axis_index(axis), 2) == 0


def strip(planes, rows):
    out = jnp.zeros((rows, COLS), F32)
    for p, plane in enumerate(planes):
        out = jnp.where(window(p, rows), turn(plane, 8 * (p + 2) + 2, 1), out)
    return out


def face_pack(strips, rows):
    right = [jnp.zeros((rows, COLS), F32) for _ in range(2)]
    left = [jnp.zeros((rows, COLS), F32) for _ in range(2)]
    for k, value in enumerate(strips):
        array, half, pair = slot(k)
        mask = slot_mask(k, rows)
        right[array] = jnp.where(mask, turn(value, 2 * pair + 64 * half, 1), right[array])
        left[array] = jnp.where(mask, turn(value, 2 * pair - 2 + 64 * half, 1), left[array])
    return right, left


def first_kernel(e, h, ae, ah, eps, cur, f, ya, yb, sems):
    copies = []
    for k in range(COMPS):
        source = (e, h, ae, ah)[k // 3].at[k % 3] if k < 12 else (eps, cur)[k - 12]
        copies.append(pltpu.make_async_copy(source, f.at[k, 2 : PLANES + 2, 0:ROWS], sems.at[k]))
    for copy in copies:
        copy.start()
    even = parity("gy")
    sub = subs()
    for k in range(COMPS):
        copies[k].wait()
        for half in range(2):
            up = jnp.zeros((8, COLS), F32)
            down = jnp.zeros((8, COLS), F32)
            for j in range(4):
                idx = 4 * half + j + 2
                mask = (sub >> 1) == j
                up = jnp.where(mask, turn(f[k, idx, 24:32], 2 * j - 6, 0), up)
                down = jnp.where(mask, turn(f[k, idx, 0:8], 2 * j, 0), down)
            at = 8 * (2 * k + half)
            ya[at : at + 8] = jnp.where(even, up, down)
            yb[at : at + 8] = jnp.where(even, down, up)


def strip_kernel(f, strips, right_out, left_out):
    values = []
    for k in range(COMPS):
        value = strip([f[k, p + 2, 0:ROWS] for p in range(PLANES)], ROWS)
        strips[k] = value
        values.append(value)
    right, left = face_pack(values, ROWS)
    for a in range(2):
        right_out[a] = right[a]
        left_out[a] = left[a]


def profile(position, extent, thickness):
    distance = jnp.minimum(position, extent - 1 - position)
    depth = jnp.maximum(thickness - distance, 0).astype(F32) / thickness.astype(F32)
    return 0.8 * depth * depth


def magnetic(ex, ey, ez, ex_up, ey_up, hx, hy, hz, r, next_x, next_y, at=(0, 1, 2)):
    cx = (next_y(ez, 2) - ez) - (ey_up - ey)
    cy = (ex_up - ex) - (next_x(ez, 2) - ez)
    cz = (next_x(ey, 1) - ey) - (next_y(ex, 0) - ex)
    return [r * (h + h - 0.5 * c) - h for h, c in ((hx, cx), (hy, cy), (hz, cz))]


def electric(hx, hy, hz, hx_down, hy_down, ex, ey, ez, q, g, drive, prev_x, prev_y):
    cx = (hz - prev_y(hz, 2)) - (hy - hy_down)
    cy = (hx - hx_down) - (hz - prev_x(hz, 2))
    cz = (hy - prev_x(hy, 1)) - (hx - prev_y(hx, 0))
    if drive is not None:
        cz = cz - drive
    return [q * (g * e + c) for e, c in ((ex, cx), (ey, cy), (ez, cz))]


def grid_sizes():
    return PLANES * lax.axis_size("gz"), ROWS * lax.axis_size("gy"), COLS * lax.axis_size("gx")


def row_grid():
    row = subs(TALL)
    at = ROWS * lax.axis_index("gy") + jnp.where(row >= 36, row - TALL, row)
    return at, (at >= 0) & (at < grid_sizes()[1])


def damping(sigma, inside):
    return jnp.where(inside, 1.0 / (1.0 + 0.25 * sigma), 0.0)


def electric_coefficients(sigma, inside, permittivity):
    permittivity = jnp.maximum(permittivity, 1.0)
    return jnp.where(inside, 1.0 / (2.0 * permittivity + 0.5 * sigma), 0.0), 2.0 * permittivity - 0.5 * sigma


def block_sigma(pml):
    nz, ny, nx = grid_sizes()
    at, row_in = row_grid()
    flat = profile(at, ny, pml[1]) + profile(COLS * lax.axis_index("gx") + lanes(TALL), nx, pml[2])

    def of_plane(p):
        z_at = jnp.full((TALL, COLS), PLANES * lax.axis_index("gz") + p, jnp.int32)
        sigma = profile(z_at[0:8], nz, pml[0])
        sigma = jnp.concatenate([sigma] * (TALL // 8), axis=0) + flat
        return sigma, row_in & (z_at >= 0) & (z_at < nz)

    return of_plane


def side_sigma(pml):
    nz, ny, nx = grid_sizes()
    at, row_in = row_grid()
    lane = lanes(TALL)
    column = lane & 7
    x_at = COLS * lax.axis_index("gx") + jnp.where(column < 4, COLS - 2 + column, column - 6)
    z_at = PLANES * lax.axis_index("gz") + (lane >> 3) - 2
    inside = row_in & (z_at >= 0) & (z_at < nz) & (x_at >= 0) & (x_at < nx)
    return profile(z_at, nz, pml[0]) + profile(at, ny, pml[1]) + profile(x_at, nx, pml[2]), inside


def up_row(value, _):
    return pltpu.roll(value, TALL - 1, 0)


def down_row(value, _):
    return pltpu.roll(value, 1, 0)


def side_magnetic(e, h, r):
    return magnetic(
        *e, pltpu.roll(e[0], 120, 1), pltpu.roll(e[1], 120, 1), *h, r, lambda v, _: pltpu.roll(v, 127, 1), up_row
    )


def side_electric(h, e, q, g, drive):
    return electric(
        *h, pltpu.roll(h[0], 8, 1), pltpu.roll(h[1], 8, 1), *e, q, g, drive, lambda v, _: pltpu.roll(v, 1, 1), down_row
    )


def face_out(out, faces, rows, value_of):
    for i, (k, p) in enumerate(faces):
        out[ROWS * i : ROWS * i + ROWS] = value_of(k, p)[0:ROWS]
    sub = subs()
    for i in range(0, len(rows), 4):
        tile = jnp.zeros((8, COLS), F32)
        for j, (k, p, first) in enumerate(rows[i : i + 4]):
            tile = jnp.where((sub >> 1) == j, turn(value_of(k, p)[ROWS:TALL], 2 * j - first, 0), tile)
        at = ROWS * len(faces) + 2 * i
        out[at : at + 8] = tile


def face_in(ref, faces, rows, keep):
    got = {}
    for i, (k, p) in enumerate(faces):
        got[k, p] = [ref[ROWS * i : ROWS * i + ROWS] * keep, jnp.zeros((8, COLS), F32)]
    sub = subs()
    for i, (k, p, first) in enumerate(rows):
        at = ROWS * len(faces) + 8 * (i // 4)
        tile = turn(ref[at : at + 8], first - 2 * (i % 4), 0) * keep
        mask = (sub == first) | (sub == (first + 1) % 8)
        got[k, p][1] = jnp.where(mask, tile, got[k, p][1])
    return got


def second_kernel(pml, f, ya, yb, right_in, left_in, tiles, strips, xa, xb, zu, zd):
    index = lax.axis_index("gy")
    even = parity("gy")
    has_after = (index < lax.axis_size("gy") - 1).astype(F32)
    has_before = (index > 0).astype(F32)
    sub = subs()
    values = []
    for k in range(COMPS):
        planes = []
        for half in range(2):
            at = 8 * (2 * k + half)
            got_a, got_b = ya[at : at + 8], yb[at : at + 8]
            after = jnp.where(even, got_a, got_b) * has_after
            before = jnp.where(even, got_b, got_a) * has_before
            for j in range(4):
                tile = jnp.where(sub < 2, turn(after, -2 * j, 0), jnp.where(sub >= 6, turn(before, 6 - 2 * j, 0), 0.0))
                tiles[k, 4 * half + j] = tile
                planes.append(tile)
        value = strip(planes, 8)
        strips[k] = value
        values.append(value)
    right, left = face_pack(values, 8)
    even = parity("gx")
    for a in range(2):
        xa[a, 0:ROWS] = jnp.where(even, right_in[a], left_in[a])
        xb[a, 0:ROWS] = jnp.where(even, left_in[a], right_in[a])
        xa[a, ROWS:TALL] = jnp.where(even, right[a], left[a])
        xb[a, ROWS:TALL] = jnp.where(even, left[a], right[a])

    def field(k, p):
        return jnp.concatenate([f[k, p + 2, 0:ROWS], tiles[k, p]], axis=0)

    of_plane = block_sigma(pml)
    half = {}
    for p in (0, 6):
        r = damping(*of_plane(p))
        for base in (0, 6):
            new = magnetic(
                *[field(base + c, p) for c in range(3)], field(base, p + 1), field(base + 1, p + 1),
                *[field(base + 3 + c, p) for c in range(3)], r, lambda v, _: pltpu.roll(v, COLS - 1, 1), up_row,
            )
            for c in range(3):
                half[base + 3 + c, p] = new[c]

    def value_of(k, p):
        return half[k, p] if (k, p) in half else field(k, p)

    face_out(zu, UP_FACES, UP_ROWS, value_of)
    face_out(zd, DOWN_FACES, DOWN_ROWS, value_of)


def third_kernel(pml, xa, xb, strips, strips_rim, sides, rim_up, rim_down):
    index = lax.axis_index("gx")
    even = parity("gx")
    has_after = (index < lax.axis_size("gx") - 1).astype(F32)
    has_before = (index > 0).astype(F32)
    lane = lanes(TALL)
    pair_of = (lane & 7) >> 1
    own = (lane >= 16) & (lane < 80)
    after = [jnp.where(even, xa[a], xb[a]) * has_after for a in range(2)]
    before = [jnp.where(even, xb[a], xa[a]) * has_before for a in range(2)]
    side = []
    for k in range(COMPS):
        array, half, pair = slot(k)
        mine = jnp.concatenate([strips[k], strips_rim[k]], axis=0)
        value = jnp.where(pair_of == 0, mine, turn(mine, 4, 1))
        value = jnp.where(pair_of == 1, turn(after[array], 2 - 2 * pair - 64 * half, 1), value)
        value = jnp.where(pair_of == 2, turn(before[array], 4 - 2 * pair - 64 * half, 1), value)
        value = jnp.where(own, value, 0.0)
        sides[k] = value
        side.append(value)
    r = damping(*side_sigma(pml))
    stepped = list(side)
    for base in (0, 6):
        stepped[base + 3 : base + 6] = side_magnetic(side[base : base + 3], side[base + 3 : base + 6], r)
    for out, items in ((rim_up, UP_SIDES), (rim_down, DOWN_SIDES)):
        packed = jnp.zeros((TALL, COLS), F32)
        for i, (k, p) in enumerate(items):
            value = side[k] if p == 7 else stepped[k]
            packed = jnp.where((lane >> 3) == i, turn(value, 8 * i - 8 * (p + 2), 1), packed)
        out[...] = packed


def drive_factors(start):
    factors = []
    for k in (1, 2):
        phase = jnp.full((8, COLS), lax.rem(start[0] + k, PERIOD), jnp.int32).astype(F32)
        factor = jnp.sin(phase * (2.0 * math.pi / PERIOD))
        factors.append(jnp.concatenate([factor] * (TALL // 8), axis=0))
    return factors


def spread(first, split, gap):
    return lambda i: i + first + (gap if i >= split else 0)


def home(layer):
    mine = lax.axis_index("gz") >> 1
    return (((layer >> 2) ^ mine) << 2) + (layer & 3)


def run_steps(pml, start, layer, f, one, rr, qq, gg, xf, xone, frozen, planes, sums, put):
    sigma, inside = side_sigma(pml)
    xr = damping(sigma, inside)
    xq, xg = electric_coefficients(sigma, inside, xf[12])
    factors = drive_factors(start)
    lane = lanes(TALL)
    first_lane, last_lane = lane == 0, lane == COLS - 1
    held = (lane >> 3) == -1
    for idx in frozen:
        held = held | ((lane >> 3) == idx)

    def side_half(e_ref, e_base, h_base, hold):
        old = [xf[h_base + c] for c in range(3)]
        new = side_magnetic([e_ref[e_base + c] for c in range(3)], old, xr)
        for c in range(3):
            xf[h_base + c] = jnp.where(held, old[c], new[c]) if hold else new[c]

    def side_full(e_base, h_base, out_base, factor):
        drive = None if factor is None else xf[13] * factor
        new = side_electric(
            [xf[h_base + c] for c in range(3)], [xf[e_base + c] for c in range(3)], xq, xg, drive
        )
        for c in range(3):
            xone[out_base + c] = new[c]

    def plane_magnetic(idx, e_ref, x_ref, e_base, h_base):
        def next_x(value, c):
            halo = pltpu.roll(x_ref[e_base + c], 125 - 8 * idx, 1)
            return jnp.where(last_lane, halo, pltpu.roll(value, COLS - 1, 1))

        new = magnetic(
            *[e_ref[e_base + c, idx] for c in range(3)], e_ref[e_base, idx + 1], e_ref[e_base + 1, idx + 1],
            *[f[h_base + c, idx] for c in range(3)], rr[idx], next_x, up_row,
        )
        for c in range(3):
            f[h_base + c, idx] = new[c]

    def plane_electric(idx, e_ref, e_base, h_base, factor):
        def prev_x(value, c):
            halo = pltpu.roll(xf[h_base + c], 123 - 8 * idx, 1)
            return jnp.where(first_lane, halo, pltpu.roll(value, 1, 1))

        drive = None if factor is None else f[13, idx] * factor
        return electric(
            *[f[h_base + c, idx] for c in range(3)], f[h_base, idx - 1], f[h_base + 1, idx - 1],
            *[e_ref[e_base + c, idx] for c in range(3)], qq[idx], gg[idx], drive, prev_x, down_row,
        )

    def over(which, body):
        count, index = planes[which]

        for i in range(count):
            body(index(i))

    def body(idx):
        plane_magnetic(idx, f, xf, 0, 3)
        plane_magnetic(idx, f, xf, 6, 9)

    over(0, body)
    side_half(xf, 0, 3, True)
    side_half(xf, 6, 9, True)

    def body(idx):
        for base, out, factor in ((0, 0, factors[0]), (6, 3, None)):
            new = plane_electric(idx, f, base, base + 3, factor)
            for c in range(3):
                one[out + c, idx] = new[c]

    over(1, body)
    side_full(0, 3, 0, factors[0])
    side_full(6, 9, 3, None)

    def body(idx):
        plane_magnetic(idx, one, xone, 0, 3)
        plane_magnetic(idx, one, xone, 3, 9)

    over(2, body)
    side_half(xone, 0, 3, False)
    side_half(xone, 3, 9, False)

    def body(idx):
        two = plane_electric(idx, one, 0, 3, factors[1])
        zero = plane_electric(idx, one, 3, 9, None)
        density = jnp.zeros((ROWS, COLS), F32)
        for c in range(3):
            last = zero[c][0:ROWS]
            put(c, idx, last, f[9 + c, idx, 0:ROWS])
            density = density + f[c, idx, 0:ROWS] * last + one[c, idx, 0:ROWS] * one[3 + c, idx, 0:ROWS]
            density = density + two[c][0:ROWS] * f[6 + c, idx, 0:ROWS]
        sums[home(layer[idx - 2])] = density

    over(3, body)


def inner_kernel(layer, pml, start, own, tiles, sides, f, one, rr, qq, gg, sums, e_mid, h_mid, xf, xone):
    del own
    for k in range(COMPS):
        for p in range(PLANES):
            f[k, p + 2, ROWS:TALL] = tiles[k, p]
        xf[k] = sides[k]
    of_plane = block_sigma(pml)

    def coefficients(i, carry):
        sigma, inside = of_plane(i)
        rr[i + 2] = damping(sigma, inside)
        qq[i + 2], gg[i + 2] = electric_coefficients(sigma, inside, f[12, i + 2])
        return carry

    lax.fori_loop(0, PLANES, coefficients, 0)
    sums[...] = jnp.zeros((LAYERS, ROWS, COLS), F32)

    def put(c, idx, e_new, h_new):
        e_mid[c, idx - 4] = e_new
        h_mid[c, idx - 4] = h_new

    planes = [(7, lambda i: i + 2), (6, lambda i: i + 3), (5, lambda i: i + 3), (4, lambda i: i + 4)]
    run_steps(pml, start, layer, f, one, rr, qq, gg, xf, xone, (), planes, sums, put)


def outer_kernel(
    layer, pml, start, f_in, one_in, rr_in, qq_in, gg_in, sums_in, zu, zd, sides, rim_up, rim_down,
    f, one, rr, qq, gg, sums, e_rest, h_rest, first, second, third, xf, xone,
):
    del f_in, one_in, rr_in, qq_in, gg_in, sums_in
    index = lax.axis_index("gz")
    has_above = (index < lax.axis_size("gz") - 1).astype(F32)
    has_below = (index > 0).astype(F32)
    lane = lanes(TALL)
    for k in range(COMPS):
        xf[k] = sides[k]
    for ref, faces, rows, rim, items, shift, keep in (
        (zu, UP_FACES, UP_ROWS, rim_up, UP_SIDES, -6, has_below),
        (zd, DOWN_FACES, DOWN_ROWS, rim_down, DOWN_SIDES, PLANES + 2, has_above),
    ):
        for (k, p), (plane, tile) in face_in(ref, faces, rows, keep).items():
            f[k, p + shift, 0:ROWS] = plane
            f[k, p + shift, ROWS:TALL] = tile
        packed = rim[...] * keep
        for i, (k, p) in enumerate(items):
            xf[k] = jnp.where((lane >> 3) == p + shift, turn(packed, 8 * (p + shift) - 8 * i, 1), xf[k])
    last_lane = lane == COLS - 1
    top = PLANES + 2
    for k, idx in ((4, 0), (10, 0), (4, top), (5, top), (10, top), (11, top)):
        f[k, idx] = jnp.where(last_lane, turn(xf[k], 126 - 8 * idx, 1), f[k, idx])
    of_plane = block_sigma(pml)
    for idx in (1, top):
        sigma, inside = of_plane(idx - 2)
        rr[idx] = damping(sigma, inside)
        qq[idx], gg[idx] = electric_coefficients(sigma, inside, f[12, idx])

    def put(c, idx, e_new, h_new):
        at = idx - 2 if idx < 4 else idx - 6
        e_rest[c, at] = e_new
        h_rest[c, at] = h_new

    planes = [(2, lambda i: 8 * i + 1), (4, spread(1, 2, 6)), (4, spread(1, 2, 5)), (4, spread(2, 2, 4))]
    run_steps(pml, start, layer, f, one, rr, qq, gg, xf, xone, (0, top), planes, sums, put)
    for i, out in enumerate((first, second, third)):
        out[...] = sums[4 * i + 4 : 4 * i + 8]


def store_kernel(e_mid, h_mid, e_rest, h_rest, e_out, h_out, sems):
    copies = []
    for mid, rest, out in ((e_mid, e_rest, e_out), (h_mid, h_rest, h_out)):
        for source, at, first, count in ((mid, 0, 2, 4), (rest, 0, 0, 2), (rest, 2, 6, 2)):
            copies.append((source.at[:, at : at + count], out.at[:, first : first + count]))
    copies = [pltpu.make_async_copy(a, b, sems.at[i]) for i, (a, b) in enumerate(copies)]
    for copy in copies:
        copy.start()
    for copy in copies:
        copy.wait()


def fold_kernel(sums, first, second, third, kept, sent):
    upper = lax.rem(lax.axis_index("gz"), 2) == 1
    for i in range(2):
        low, high = (sums[j] + first[j] + second[j] + third[j] for j in (i, i + 2))
        kept[i] = jnp.where(upper, high, low)
        sent[i] = jnp.where(upper, low, high)


def sum_kernel(kept, got, out):
    out[...] = kept[...] + got[...]


def call(kernel, outs, scratch=(), scalars=0, far=0, aliases=None, out_space=pltpu.VMEM):
    def run(*args):
        near = len(args) - scalars - far
        specs = [pl.BlockSpec(memory_space=pltpu.SMEM)] * scalars
        specs += [pl.BlockSpec(memory_space=pltpu.VMEM)] * near + [pl.BlockSpec(memory_space=pl.ANY)] * far
        size = sum(4 * math.prod(s) for s in outs) + sum(4 * math.prod(a.shape) for a in args)
        return pl.pallas_call(
            kernel,
            out_shape=[jax.ShapeDtypeStruct(s, F32) for s in outs],
            in_specs=specs,
            out_specs=[pl.BlockSpec(memory_space=out_space)] * len(outs),
            scratch_shapes=[pltpu.VMEM(s, F32) if isinstance(s, tuple) else s for s in scratch],
            input_output_aliases=aliases or {},
            compiler_params=pltpu.CompilerParams(vmem_limit_bytes=24 * 2**20),
            cost_estimate=pl.CostEstimate(flops=1000000, bytes_accessed=size, transcendentals=0),
        )(*args)

    return run


def ring(axis, step):
    count = lax.axis_size(axis)
    return [(i, (i + step) % count) for i in range(count)]


def swaps(axis, first):
    count = lax.axis_size(axis)
    pairs = [(i, (i + 1) % count) for i in range(first, count, 2)]
    return pairs + [(b, a) for a, b in pairs]


def across(axis, bits):
    return [(i, i ^ bits) for i in range(lax.axis_size(axis))]


def inner_swaps():
    count, width = lax.axis_size("gy"), lax.axis_size("gx")
    pairs = []
    for j in range(width):
        pairs += [(i * width + j, (i + 1) * width + j) for i in range(1, count - 1, 2)]
        if j % 2 == 0:
            pairs += [(i * width + j, i * width + j + 1) for i in (0, count - 1)]
    return pairs + [(b, a) for a, b in pairs]


def local(e_start, h_start, adjoint_e, adjoint_h, permittivity, current, layer_of_cell, pml_cells, start_step):
    raw = (e_start, h_start, adjoint_e, adjoint_h, permittivity, current)
    raw = [pltpu.with_memory_space_constraint(a, pltpu.HBM) for a in raw]
    block, deep, tall = (ROWS, COLS), (DEEP, TALL, COLS), (TALL, COLS)
    f, ya, yb = call(
        first_kernel, [(COMPS,) + deep, (16 * COMPS, COLS), (16 * COMPS, COLS)], [pltpu.SemaphoreType.DMA((COMPS,))], far=6
    )(*raw)
    yb = lax.ppermute(yb, ("gy", "gx"), inner_swaps())
    ya = lax.ppermute(ya, "gy", swaps("gy", 0))
    strips, right, left = call(strip_kernel, [(COMPS,) + block, (2,) + block, (2,) + block])(f)
    side = (2,) + tall
    tiles, strips_rim, xa, xb, zu, zd = call(
        second_kernel,
        [(COMPS, PLANES, 8, COLS), (COMPS, 8, COLS), side, side, (face_rows(UP_FACES, UP_ROWS), COLS), (face_rows(DOWN_FACES, DOWN_ROWS), COLS)],
        scalars=1,
    )(pml_cells, f, ya, yb, right, left)
    zu = lax.ppermute(zu, "gz", ring("gz", 1))
    zd = lax.ppermute(zd, "gz", ring("gz", -1))
    xa = lax.ppermute(xa, "gx", swaps("gx", 0))
    xb = lax.ppermute(xb, "gx", swaps("gx", 1))
    sides, rim_up, rim_down = call(third_kernel, [(COMPS,) + tall, tall, tall], scalars=1)(pml_cells, xa, xb, strips, strips_rim)
    rim_up = lax.ppermute(rim_up, "gz", ring("gz", 1))
    rim_down = lax.ppermute(rim_down, "gz", ring("gz", -1))
    state = [(COMPS,) + deep, (6,) + deep, deep, deep, deep, (LAYERS,) + block]
    mid, out = (3, PLANES // 2) + block, (3, PLANES) + block
    side = [(COMPS,) + tall, (6,) + tall]
    *held, e_mid, h_mid = call(inner_kernel, state + [mid, mid], side, scalars=3, aliases={3: 0})(
        layer_of_cell, pml_cells, start_step, f, tiles, sides
    )
    quarter, pair = (LAYERS // 4,) + block, (2,) + block
    *_, sums, e_rest, h_rest, first, second, third = call(
        outer_kernel, state + [mid, mid, quarter, quarter, quarter], side, scalars=3, aliases={3 + i: i for i in range(len(state))}
    )(layer_of_cell, pml_cells, start_step, *held, zu, zd, sides, rim_up, rim_down)
    e_out, h_out = call(store_kernel, [out, out], [pltpu.SemaphoreType.DMA((6,))], out_space=pltpu.HBM)(e_mid, h_mid, e_rest, h_rest)
    first, second, third = (lax.ppermute(v, "gz", across("gz", m)) for v, m in ((first, 2), (second, 4), (third, 6)))
    kept, sent = call(fold_kernel, [pair, pair])(sums, first, second, third)
    (gradient,) = call(sum_kernel, [pair])(kept, lax.ppermute(sent, "gz", across("gz", 1)))
    return gradient, e_out, h_out


def solution(mesh):
    fields = P(None, "gz", "gy", "gx")
    cells = P("gz", "gy", "gx")
    return jax.shard_map(
        local,
        mesh=mesh,
        in_specs=(fields, fields, fields, fields, cells, cells, P("gz"), P(), P()),
        out_specs=(cells, fields, fields),
        check_vma=False,
    )
```

time: 52.6 us -> 47.7 us (0.907)
  blocking collectives: 13.7 us -> 0 us
  starting transfers between devices: 17.7 us -> 26.7 us
  Pallas kernels: 10.5 us -> 9.88 us
    all_to_all x1 -> x0, blocking collectives: 13.7 us -> none  [local(): got = lax.all_to_all(sums, 'gz', 0, 0, tiled=True)]
    ppermute x1 -> x5, starting transfers between devices: 2.12 us -> 10.8 us  [the longest x3 4.77 us: local(): lax.ppermute(v, 'gz', across('gz', m))]
    ppermute x1 -> x5, waiting for transfers between devices: 3.35 us -> 6.37 us  [the longest x3 2.83 us: local(): lax.ppermute(v, 'gz', across('gz', m))]
    ppermute x1, waiting for transfers between devices: 1.43 us -> 0.01 us  [local(): rim_up = lax.ppermute(rim_up, 'gz', ring('gz', 1))]
    ppermute x1, waiting for transfers between devices: 1.36 us -> 0.01 us  [local(): rim_down = lax.ppermute(rim_down, 'gz', ring('gz', -1))]
    pallas_call x7 -> x9, Pallas kernels: 10.5 us -> 9.88 us  [run(): pl.pallas_call(kernel, out_shape=[jax.ShapeDtypeStruct(s, F32) for s in o...]
  transfers between devices with their start and end apart: 8 -> 12, of which waited for: 5 -> 6; matrix products, arithmetic and copies ran while one was open for 0% -> 0% of each run, Pallas kernels for 3% -> 10%
where the time goes in v3:
time: 47.7 us; the launch traced here: 47.5 us
  starting transfers between devices  26.7 us (56%)
  Pallas kernels  9.88 us (21%)
  waiting for transfers between devices  9.5 us (20%)
  between operations  1.42 us (3%)
    pallas_call x9, Pallas kernels, run(): pl.pallas_call(kernel, out_shape=[jax.ShapeDtypeStruct(s, F32) for s in o...  9.88 us
    ppermute x3, starting transfers between devices, local(): lax.ppermute(v, 'gz', across('gz', m))  4.77 us
    ppermute x1, starting transfers between devices, local(): rim_down = lax.ppermute(rim_down, 'gz', ring('gz', -1))  4.64 us
    ppermute x1, starting transfers between devices, local(): lax.ppermute(sent, 'gz', across('gz', 1))  4.38 us
    ppermute x1, starting transfers between devices, local(): zu = lax.ppermute(zu, 'gz', ring('gz', 1))  4.02 us
    ppermute x3, waiting for transfers between devices, local(): lax.ppermute(v, 'gz', across('gz', m))  2.83 us
    ppermute x1, waiting for transfers between devices, local(): xb = lax.ppermute(xb, 'gx', swaps('gx', 1))  2.7 us
    ppermute x1, waiting for transfers between devices, local(): yb = lax.ppermute(yb, ('gy', 'gx'), inner_swaps())  2.57 us
  transfers between devices with their start and end apart: 12, of which 6 were waited for; matrix products, arithmetic and copies ran while one was open for 0% of the time, Pallas kernels for 10%

profile of v3, /device:TPU:0, one launch (start us, length us, event | category | flops | bytes accessed | tf_op | source)
XLA Modules:
  0.0 47.5 jit_solution(16572561333572516703)
XLA Ops:
  0.6 0.0 copy-start
  0.6 1.7 %shard_map.112 = (f32[14,12,40,128]{3,2,1,0:T(8,128)S(1)}, f32[224,128]{1,0:T(8,128)S(1)}, f32[224,128]{1,0:T(8,128)S(1)}) custom-call(f32[3,8,32,128]{3,2,1,0:T(8,128)} %e.1, f32[3,8,32,128]{3,2,1,0:T(8,128)} %h.1, f32[3,8,32,128]{3,2,1,0:T(8,128)} %ae.1, f32[3,8,32,128]{3,2,1,0:T(8,128)} %ah.1, f32[8,32,128]{2,1,0:T(8,128)} %eps.1, f32[8,32,128]{2,1,0:T(8,128)} %cur.1), custom_call_target="tpu_custom_call" | custom-call | flops 1000000 | bytes 5505024 | tf_op jit(solution)/shard_map/pallas_call | solution.py:520
  2.3 0.1 collective-permute-start
  2.4 1.7 %collective-permute-start.1 = (f32[224,128]{1,0:T(8,128)S(1)}, f32[224,128]{1,0:T(8,128)S(1)}, u32[]{:S(2)}, u32[]{:S(2)}) collective-permute-start(f32[224,128]{1,0:T(8,128)S(1)} %get-tuple-element.38), channel_id=1, source_target_pairs={{4,8},{0,1},{12,13},{5,9},{6,10},{2,3},{14,15},{7,11},{8,4},{1,0},... | collective-permute-start | bytes 344072 | tf_op jit(solution)/shard_map/ppermute | solution.py:566
  4.0 0.0 copy-start.1
  4.1 0.6 %shard_map.113 = (f32[14,32,128]{2,1,0:T(8,128)S(1)}, f32[2,32,128]{2,1,0:T(8,128)S(1)}, f32[2,32,128]{2,1,0:T(8,128)S(1)}) custom-call(f32[14,12,40,128]{3,2,1,0:T(8,128)S(1)} %get-tuple-element.36.f.own), custom_call_target="tpu_custom_call" | custom-call | flops 1000000 | bytes 3735552 | tf_op jit(solution)/shard_map/pallas_call | solution.py:520
  4.7 0.0 collective-permute-done.ya
  4.7 2.6 %collective-permute-done.1.yb = f32[224,128]{1,0:T(8,128)S(1)} collective-permute-done((f32[224,128]{1,0:T(8,128)S(1)}, f32[224,128]{1,0:T(8,128)S(1)}, u32[]{:S(2)}, u32[]{:S(2)}) %collective-permute-start.1) | collective-permute-done | bytes 114720 | tf_op jit(solution)/shard_map/ppermute | solution.py:566
  7.3 0.0 copy-done
  7.3 0.8 %shard_map.114 = (f32[14,8,8,128]{3,2,1,0:T(8,128)S(1)}, f32[14,8,128]{2,1,0:T(8,128)S(1)}, f32[2,40,128]{2,1,0:T(8,128)S(1)}, f32[2,40,128]{2,1,0:T(8,128)S(1)}...) custom-call(s32[3]{0:T(128)S(1)} %copy-done, f32[14,12,40,128]{3,2,1,0:T(8,128)S(1)} %get-tuple-element.36.f.own, ...), custom_call_target="tpu_custom_call" | custom-call | flops 1000000 | bytes 4837388 | tf_op jit(solution)/shard_map/pallas_call | solution.py:520
  8.1 4.0 %collective-permute-start.4 = (f32[608,128]{1,0:T(8,128)S(1)}, f32[608,128]{1,0:T(8,128)S(1)}, u32[]{:S(2)}, u32[]{:S(2)}) collective-permute-start(f32[608,128]{1,0:T(8,128)S(1)} %get-tuple-element.53), channel_id=1, source_target_pairs={{0,16},{16,32},{32,48},{48,64},{64,80},{80,96},{96,112},{112,0},{1... | collective-permute-start | bytes 933896 | tf_op jit(solution)/shard_map/ppermute | solution.py:575
  12.1 2.5 %collective-permute-start.5 = (f32[376,128]{1,0:T(8,128)S(1)}, f32[376,128]{1,0:T(8,128)S(1)}, u32[]{:S(2)}, u32[]{:S(2)}) collective-permute-start(f32[376,128]{1,0:T(8,128)S(1)} %get-tuple-element.54), channel_id=1, source_target_pairs={{0,112},{16,0},{32,16},{48,32},{64,48},{80,64},{96,80},{112,96},{1... | collective-permute-start | bytes 577544 | tf_op jit(solution)/shard_map/ppermute | solution.py:576
  14.6 1.5 %collective-permute-start.2 = (f32[2,40,128]{2,1,0:T(8,128)S(1)}, f32[2,40,128]{2,1,0:T(8,128)S(1)}, u32[]{:S(2)}, u32[]{:S(2)}) collective-permute-start(f32[2,40,128]{2,1,0:T(8,128)S(1)} %get-tuple-element.42), channel_id=1, source_target_pairs={{0,1},{2,3},{1,0},{3,2},{4,5},{6,7},{5,4},{7,6},{8,9},{10,11},{9,8... | collective-permute-start | bytes 122888 | tf_op jit(solution)/shard_map/ppermute | solution.py:577
  16.1 2.1 %collective-permute-start.3 = (f32[2,40,128]{2,1,0:T(8,128)S(1)}, f32[2,40,128]{2,1,0:T(8,128)S(1)}, u32[]{:S(2)}, u32[]{:S(2)}) collective-permute-start(f32[2,40,128]{2,1,0:T(8,128)S(1)} %get-tuple-element.43), channel_id=1, source_target_pairs={{1,2},{3,0},{2,1},{0,3},{5,6},{7,4},{6,5},{4,7},{9,10},{11,8},{10,... | collective-permute-start | bytes 122888 | tf_op jit(solution)/shard_map/ppermute | solution.py:578
  18.2 0.4 collective-permute-done.2.xa
  18.6 2.7 %collective-permute-done.3.xb = f32[2,40,128]{2,1,0:T(8,128)S(1)} collective-permute-done((f32[2,40,128]{2,1,0:T(8,128)S(1)}, f32[2,40,128]{2,1,0:T(8,128)S(1)}, u32[]{:S(2)}, u32[]{:S(2)}) %collective-permute-start.3) | collective-permute-done | bytes 40992 | tf_op jit(solution)/shard_map/ppermute | solution.py:578
  21.4 1.0 %shard_map.115 = (f32[14,40,128]{2,1,0:T(8,128)S(1)}, f32[40,128]{1,0:T(8,128)S(1)}, f32[40,128]{1,0:T(8,128)S(1)}) custom-call(s32[3]{0:T(128)S(1)} %copy-done, f32[2,40,128]{2,1,0:T(8,128)S(1)} %collective-permute-done.2.xa, f32[2,40,128]{2,1,0:T(8,128)S(1)} %collective-permute-done.3.xb, f32[14,32,128]{2,1,0:T(8,128)S(1)} %get-tuple-element.44.strips, ...), custom_call_target="tpu_custom_call" | custom-call | flops 1000000 | bytes 696332 | tf_op jit(solution)/shard_map/pallas_call | solution.py:520
  22.3 1.1 %collective-permute-start.6 = (f32[40,128]{1,0:T(8,128)S(1)}, f32[40,128]{1,0:T(8,128)S(1)}, u32[]{:S(2)}, u32[]{:S(2)}) collective-permute-start(f32[40,128]{1,0:T(8,128)S(1)} %get-tuple-element.55), channel_id=1, source_target_pairs={{0,16},{16,32},{32,48},{48,64},{64,80},{80,96},{96,112},{112,0},{1... | collective-permute-start | bytes 61448 | tf_op jit(solution)/shard_map/ppermute | solution.py:580
  23.4 4.6 %collective-permute-start.7 = (f32[40,128]{1,0:T(8,128)S(1)}, f32[40,128]{1,0:T(8,128)S(1)}, u32[]{:S(2)}, u32[]{:S(2)}) collective-permute-start(f32[40,128]{1,0:T(8,128)S(1)} %get-tuple-element.56), channel_id=1, source_target_pairs={{0,112},{16,0},{32,16},{48,32},{64,48},{80,64},{96,80},{112,96},{1... | collective-permute-start | bytes 61448 | tf_op jit(solution)/shard_map/ppermute | solution.py:581
  28.7 0.0 copy-done.1
  28.7 2.3 %shard_map.116 = (f32[14,12,40,128]{3,2,1,0:T(8,128)S(1)}, f32[6,12,40,128]{3,2,1,0:T(8,128)S(1)}, f32[12,40,128]{2,1,0:T(8,128)S(1)}, f32[12,40,128]{2,1,0:T(8,...) custom-call(s32[8]{0:T(128)S(1)} %copy-done.1, ...), custom_call_target="tpu_custom_call", output_to_operand_aliasing={{0}: (3, {})} | custom-call | flops 1000000 | bytes 10494000 | tf_op jit(solution)/shard_map/pallas_call | solution.py:520
  31.1 0.0 collective-permute-done.6.rim_up
  31.1 0.0 collective-permute-done.7.rim_down
  31.1 0.0 collective-permute-done.5.zd
  31.1 0.0 collective-permute-done.4.zu
  31.1 1.9 %shard_map.117 = (f32[14,12,40,128]{3,2,1,0:T(8,128)S(1)}, f32[6,12,40,128]{3,2,1,0:T(8,128)S(1)}, f32[12,40,128]{2,1,0:T(8,128)S(1)}, f32[12,40,128]{2,1,0:T(8,...) custom-call(s32[8]{0:T(128)S(1)} %copy-done.1, ...), custom_call_target="tpu_custom_call", output_to_operand_aliasing={{0}: (3, {}), {1}: (4, {}), {2}: (5, {}), {3}: (6, {}), {4}... | custom-call | flops 1000000 | bytes 13250608 | tf_op jit(solution)/shard_map/pallas_call | solution.py:520
  33.0 0.1 collective-permute-start.8
  33.1 2.0 %collective-permute-start.9 = (f32[4,32,128]{2,1,0:T(8,128)S(1)}, f32[4,32,128]{2,1,0:T(8,128)S(1)}, u32[]{:S(2)}, u32[]{:S(2)}) collective-permute-start(f32[4,32,128]{2,1,0:T(8,128)S(1)} %get-tuple-element.59), channel_id=1, source_target_pairs={{0,64},{16,80},{32,96},{48,112},{64,0},{80,16},{96,32},{112,48},{1... | collective-permute-start | bytes 196616 | tf_op jit(solution)/shard_map/ppermute | solution.py:593
  35.1 2.6 %collective-permute-start.10 = (f32[4,32,128]{2,1,0:T(8,128)S(1)}, f32[4,32,128]{2,1,0:T(8,128)S(1)}, u32[]{:S(2)}, u32[]{:S(2)}) collective-permute-start(f32[4,32,128]{2,1,0:T(8,128)S(1)} %get-tuple-element.60), channel_id=1, source_target_pairs={{0,96},{16,112},{32,64},{48,80},{64,32},{80,48},{96,0},{112,16},{1... | collective-permute-start | bytes 196616 | tf_op jit(solution)/shard_map/ppermute | solution.py:593
  37.8 0.0 collective-permute-done.8.first
  37.8 1.2 %collective-permute-done.9.second = f32[4,32,128]{2,1,0:T(8,128)S(1)} collective-permute-done((f32[4,32,128]{2,1,0:T(8,128)S(1)}, f32[4,32,128]{2,1,0:T(8,128)S(1)}, u32[]{:S(2)}, u32[]{:S(2)}) %collective-permute-start.9) | collective-permute-done | bytes 65568 | tf_op jit(solution)/shard_map/ppermute | solution.py:593
  38.9 1.7 %collective-permute-done.10.third = f32[4,32,128]{2,1,0:T(8,128)S(1)} collective-permute-done((f32[4,32,128]{2,1,0:T(8,128)S(1)}, f32[4,32,128]{2,1,0:T(8,128)S(1)}, u32[]{:S(2)}, u32[]{:S(2)}) %collective-permute-start.10) | collective-permute-done | bytes 65568 | tf_op jit(solution)/shard_map/ppermute | solution.py:593
  40.6 4.4 %collective-permute-start.11 = (f32[2,32,128]{2,1,0:T(8,128)S(1)}, f32[2,32,128]{2,1,0:T(8,128)S(1)}, u32[]{:S(2)}, u32[]{:S(2)}) collective-permute-start(f32[2,32,128]{2,1,0:T(8,128)S(1)} %get-tuple-element.62), channel_id=1, source_target_pairs={{0,16},{16,0},{32,48},{48,32},{64,80},{80,64},{96,112},{112,96},{1... | collective-permute-start | bytes 98312 | tf_op jit(solution)/shard_map/ppermute | solution.py:595
  45.0 0.9 %shard_map.120 = (f32[3,8,32,128]{3,2,1,0:T(8,128)}, f32[3,8,32,128]{3,2,1,0:T(8,128)}) custom-call(f32[3,4,32,128]{3,2,1,0:T(8,128)S(1)} %get-tuple-element.63.e_mid, f32[3,4,32,128]{3,2,1,0:T(8,128)S(1)} %get-tuple-element.64.h_mid, f32[3,4,32,128]{3,2,1,0:T(8,128)S(1)} %get-tuple-element.65.e_rest, f32[3,4,32,128]{3,2,1,0:T(8,128)S(1)} %get-tuple-element.66.h_rest), custom_call_target="tpu_custom_call" | custom-call | flops 1000000 | bytes 1572864 | tf_op jit(solution)/shard_map/pallas_call | solution.py:520
  45.9 1.0 %collective-permute-done.11.got = f32[2,32,128]{2,1,0:T(8,128)S(1)} collective-permute-done((f32[2,32,128]{2,1,0:T(8,128)S(1)}, f32[2,32,128]{2,1,0:T(8,128)S(1)}, u32[]{:S(2)}, u32[]{:S(2)}) %collective-permute-start.11) | collective-permute-done | bytes 32800 | tf_op jit(solution)/shard_map/ppermute | solution.py:595
  46.9 0.6 %shard_map.119 = f32[2,32,128]{2,1,0:T(8,128)} custom-call(f32[2,32,128]{2,1,0:T(8,128)S(1)} %get-tuple-element.61.kept, f32[2,32,128]{2,1,0:T(8,128)S(1)} %collective-permute-done.11.got), custom_call_target="tpu_custom_call" | custom-call | flops 1000000 | bytes 98304 | tf_op jit(solution)/shard_map/pallas_call | solution.py:520
  (1 shorter events, 0.0 us)
Async XLA Ops:
  0.6 6.6 %copy-start = (s32[3]{0:T(128)S(1)}, s32[3]{0:T(128)}, u32[]{:S(2)}) copy-start(s32[3]{0:T(128)} %pml.7) | copy-start | bytes 40
  2.3 2.4 %collective-permute-start = (f32[224,128]{1,0:T(8,128)S(1)}, f32[224,128]{1,0:T(8,128)S(1)}, u32[]{:S(2)}, u32[]{:S(2)}) collective-permute-start(f32[224,128]{1,0:T(8,128)S(1)} %get-tuple-element.37), channel_id=1, source_target_pairs={{0,4},{8,12},{4,0},{12,8},{1,5},{9,13},{5,1},{13,9},{2,6},{10,14},... | collective-permute-start | bytes 344072 | tf_op jit(solution)/shard_map/ppermute | solution.py:567
  2.4 4.9 %collective-permute-start.1 = (f32[224,128]{1,0:T(8,128)S(1)}, f32[224,128]{1,0:T(8,128)S(1)}, u32[]{:S(2)}, u32[]{:S(2)}) collective-permute-start(f32[224,128]{1,0:T(8,128)S(1)} %get-tuple-element.38), channel_id=1, source_target_pairs={{4,8},{0,1},{12,13},{5,9},{6,10},{2,3},{14,15},{7,11},{8,4},{1,0},... | collective-permute-start | bytes 344072 | tf_op jit(solution)/shard_map/ppermute | solution.py:566
  4.0 24.7 %copy-start.1 = (s32[8]{0:T(128)S(1)}, s32[8]{0:T(128)}, u32[]{:S(2)}) copy-start(s32[8]{0:T(128)} %layer.3) | copy-start | bytes 100
  8.1 23.0 %collective-permute-start.4 = (f32[608,128]{1,0:T(8,128)S(1)}, f32[608,128]{1,0:T(8,128)S(1)}, u32[]{:S(2)}, u32[]{:S(2)}) collective-permute-start(f32[608,128]{1,0:T(8,128)S(1)} %get-tuple-element.53), channel_id=1, source_target_pairs={{0,16},{16,32},{32,48},{48,64},{64,80},{80,96},{96,112},{112,0},{1... | collective-permute-start | bytes 933896 | tf_op jit(solution)/shard_map/ppermute | solution.py:575
  12.1 19.0 %collective-permute-start.5 = (f32[376,128]{1,0:T(8,128)S(1)}, f32[376,128]{1,0:T(8,128)S(1)}, u32[]{:S(2)}, u32[]{:S(2)}) collective-permute-start(f32[376,128]{1,0:T(8,128)S(1)} %get-tuple-element.54), channel_id=1, source_target_pairs={{0,112},{16,0},{32,16},{48,32},{64,48},{80,64},{96,80},{112,96},{1... | collective-permute-start | bytes 577544 | tf_op jit(solution)/shard_map/ppermute | solution.py:576
  14.6 4.0 %collective-permute-start.2 = (f32[2,40,128]{2,1,0:T(8,128)S(1)}, f32[2,40,128]{2,1,0:T(8,128)S(1)}, u32[]{:S(2)}, u32[]{:S(2)}) collective-permute-start(f32[2,40,128]{2,1,0:T(8,128)S(1)} %get-tuple-element.42), channel_id=1, source_target_pairs={{0,1},{2,3},{1,0},{3,2},{4,5},{6,7},{5,4},{7,6},{8,9},{10,11},{9,8... | collective-permute-start | bytes 122888 | tf_op jit(solution)/shard_map/ppermute | solution.py:577
  16.1 5.2 %collective-permute-start.3 = (f32[2,40,128]{2,1,0:T(8,128)S(1)}, f32[2,40,128]{2,1,0:T(8,128)S(1)}, u32[]{:S(2)}, u32[]{:S(2)}) collective-permute-start(f32[2,40,128]{2,1,0:T(8,128)S(1)} %get-tuple-element.43), channel_id=1, source_target_pairs={{1,2},{3,0},{2,1},{0,3},{5,6},{7,4},{6,5},{4,7},{9,10},{11,8},{10,... | collective-permute-start | bytes 122888 | tf_op jit(solution)/shard_map/ppermute | solution.py:578
  22.3 8.7 %collective-permute-start.6 = (f32[40,128]{1,0:T(8,128)S(1)}, f32[40,128]{1,0:T(8,128)S(1)}, u32[]{:S(2)}, u32[]{:S(2)}) collective-permute-start(f32[40,128]{1,0:T(8,128)S(1)} %get-tuple-element.55), channel_id=1, source_target_pairs={{0,16},{16,32},{32,48},{48,64},{64,80},{80,96},{96,112},{112,0},{1... | collective-permute-start | bytes 61448 | tf_op jit(solution)/shard_map/ppermute | solution.py:580
  23.4 7.7 %collective-permute-start.7 = (f32[40,128]{1,0:T(8,128)S(1)}, f32[40,128]{1,0:T(8,128)S(1)}, u32[]{:S(2)}, u32[]{:S(2)}) collective-permute-start(f32[40,128]{1,0:T(8,128)S(1)} %get-tuple-element.56), channel_id=1, source_target_pairs={{0,112},{16,0},{32,16},{48,32},{64,48},{80,64},{96,80},{112,96},{1... | collective-permute-start | bytes 61448 | tf_op jit(solution)/shard_map/ppermute | solution.py:581
  33.0 4.8 %collective-permute-start.8 = (f32[4,32,128]{2,1,0:T(8,128)S(1)}, f32[4,32,128]{2,1,0:T(8,128)S(1)}, u32[]{:S(2)}, u32[]{:S(2)}) collective-permute-start(f32[4,32,128]{2,1,0:T(8,128)S(1)} %get-tuple-element.58), channel_id=1, source_target_pairs={{0,32},{16,48},{32,0},{48,16},{64,96},{80,112},{96,64},{112,80},{1... | collective-permute-start | bytes 196616 | tf_op jit(solution)/shard_map/ppermute | solution.py:593
  33.1 5.8 %collective-permute-start.9 = (f32[4,32,128]{2,1,0:T(8,128)S(1)}, f32[4,32,128]{2,1,0:T(8,128)S(1)}, u32[]{:S(2)}, u32[]{:S(2)}) collective-permute-start(f32[4,32,128]{2,1,0:T(8,128)S(1)} %get-tuple-element.59), channel_id=1, source_target_pairs={{0,64},{16,80},{32,96},{48,112},{64,0},{80,16},{96,32},{112,48},{1... | collective-permute-start | bytes 196616 | tf_op jit(solution)/shard_map/ppermute | solution.py:593
  35.1 5.5 %collective-permute-start.10 = (f32[4,32,128]{2,1,0:T(8,128)S(1)}, f32[4,32,128]{2,1,0:T(8,128)S(1)}, u32[]{:S(2)}, u32[]{:S(2)}) collective-permute-start(f32[4,32,128]{2,1,0:T(8,128)S(1)} %get-tuple-element.60), channel_id=1, source_target_pairs={{0,96},{16,112},{32,64},{48,80},{64,32},{80,48},{96,0},{112,16},{1... | collective-permute-start | bytes 196616 | tf_op jit(solution)/shard_map/ppermute | solution.py:593
  40.6 6.3 %collective-permute-start.11 = (f32[2,32,128]{2,1,0:T(8,128)S(1)}, f32[2,32,128]{2,1,0:T(8,128)S(1)}, u32[]{:S(2)}, u32[]{:S(2)}) collective-permute-start(f32[2,32,128]{2,1,0:T(8,128)S(1)} %get-tuple-element.62), channel_id=1, source_target_pairs={{0,16},{16,0},{32,48},{48,32},{64,80},{80,64},{96,112},{112,96},{1... | collective-permute-start | bytes 98312 | tf_op jit(solution)/shard_map/ppermute | solution.py:595

commit v4 on v3

--- a/solution.py
+++ b/solution.py
@@ -14,13 +14,11 @@
 LAYERS = 16
 PERIOD = 64
 COMPS = 14
-HALF = (3, 4, 5, 9, 10, 11)
-UP_FACES = [(k, 7) for k in range(14)] + [(k, 6) for k in (3, 4, 9, 10)]
-DOWN_FACES = [(k, 0) for k in (0, 1, 6, 7, 12) + HALF]
-UP_ROWS = [(k, 7, 7) for k in range(14)] + [(k, 7, 0) for k in (2, 8)]
-DOWN_ROWS = [(k, 0, 7) for k in (0, 1, 6, 7, 12, 3, 5, 9, 11)] + [(k, 0, 6) for k in (1, 7)]
-UP_SIDES = [(k, 7) for k in range(14)] + [(k, 6) for k in (4, 10)]
-DOWN_SIDES = DOWN_FACES
+UP_FACES = [("h", k) for k in (3, 4, 9, 10)] + [("e", k) for k in (0, 1, 2, 6, 7, 8)] + [("f", 12)]
+DOWN_FACES = [("f", k) for k in (0, 1, 6, 7, 12)] + [("e", k) for k in (0, 1, 6, 7)]
+UP_ROWS = [("h", k, 7) for k in (3, 4, 9, 10)] + [("e", 2, 7), ("e", 8, 7), ("f", 12, 7)]
+DOWN_ROWS = [("f", k, 7) for k in (0, 1, 6, 7, 12)] + [("e", 1, 7), ("e", 7, 7), ("f", 1, 6), ("f", 7, 6)]
+UP_SIDES, DOWN_SIDES = UP_FACES, DOWN_FACES
 
 
 def face_rows(faces, rows):
@@ -102,7 +100,10 @@
             yb[at : at + 8] = jnp.where(even, down, up)
 
 
-def strip_kernel(f, strips, right_out, left_out):
+def strip_kernel(start, f, strips, right_out, left_out, factors):
+    for k in range(2):
+        phase = jnp.full((8, COLS), lax.rem(start[0] + k + 1, PERIOD), jnp.int32).astype(F32)
+        factors[k] = jnp.sin(phase * (2.0 * math.pi / PERIOD))
     values = []
     for k in range(COMPS):
         value = strip([f[k, p + 2, 0:ROWS] for p in range(PLANES)], ROWS)
@@ -200,32 +201,32 @@
     )
 
 
-def face_out(out, faces, rows, value_of):
-    for i, (k, p) in enumerate(faces):
-        out[ROWS * i : ROWS * i + ROWS] = value_of(k, p)[0:ROWS]
+def face_out(out, faces, rows, values):
+    for i, item in enumerate(faces):
+        out[ROWS * i : ROWS * i + ROWS] = values[item][0:ROWS]
     sub = subs()
     for i in range(0, len(rows), 4):
         tile = jnp.zeros((8, COLS), F32)
-        for j, (k, p, first) in enumerate(rows[i : i + 4]):
-            tile = jnp.where((sub >> 1) == j, turn(value_of(k, p)[ROWS:TALL], 2 * j - first, 0), tile)
+        for j, (kind, k, first) in enumerate(rows[i : i + 4]):
+            tile = jnp.where((sub >> 1) == j, turn(values[kind, k][ROWS:TALL], 2 * j - first, 0), tile)
         at = ROWS * len(faces) + 2 * i
         out[at : at + 8] = tile
 
 
 def face_in(ref, faces, rows, keep):
     got = {}
-    for i, (k, p) in enumerate(faces):
-        got[k, p] = [ref[ROWS * i : ROWS * i + ROWS] * keep, jnp.zeros((8, COLS), F32)]
+    for i, item in enumerate(faces):
+        got[item] = [ref[ROWS * i : ROWS * i + ROWS] * keep, jnp.zeros((8, COLS), F32)]
     sub = subs()
-    for i, (k, p, first) in enumerate(rows):
+    for i, (kind, k, first) in enumerate(rows):
         at = ROWS * len(faces) + 8 * (i // 4)
         tile = turn(ref[at : at + 8], first - 2 * (i % 4), 0) * keep
         mask = (sub == first) | (sub == (first + 1) % 8)
-        got[k, p][1] = jnp.where(mask, tile, got[k, p][1])
-    return got
-
-
-def second_kernel(pml, f, ya, yb, right_in, left_in, tiles, strips, xa, xb, zu, zd):
+        got[kind, k][1] = jnp.where(mask, tile, got[kind, k][1])
+    return {item: jnp.concatenate(parts, axis=0) for item, parts in got.items()}
+
+
+def second_kernel(ya, yb, right_in, left_in, tiles, strips, xa, xb):
     index = lax.axis_index("gy")
     even = parity("gy")
     has_after = (index < lax.axis_size("gy") - 1).astype(F32)
@@ -254,29 +255,44 @@
         xa[a, ROWS:TALL] = jnp.where(even, right[a], left[a])
         xb[a, ROWS:TALL] = jnp.where(even, left[a], right[a])
 
+
+def face_kernel(pml, f, tiles, factors, zu, zd):
     def field(k, p):
         return jnp.concatenate([f[k, p + 2, 0:ROWS], tiles[k, p]], axis=0)
 
     of_plane = block_sigma(pml)
-    half = {}
-    for p in (0, 6):
-        r = damping(*of_plane(p))
+    zero = jnp.zeros((TALL, COLS), F32)
+    drive = jnp.concatenate([factors[0]] * (TALL // 8), axis=0) * field(13, 7)
+
+    def next_x(value, _):
+        return pltpu.roll(value, COLS - 1, 1)
+
+    def prev_x(value, _):
+        return pltpu.roll(value, 1, 1)
+
+    def half_step(base, p):
+        up = [field(base + c, p + 1) for c in range(2)] if p < 7 else [zero, zero]
+        return magnetic(
+            *[field(base + c, p) for c in range(3)], *up, *[field(base + 3 + c, p) for c in range(3)],
+            damping(*of_plane(p)), next_x, up_row,
+        )
+
+    for out, p, faces, rows in ((zu, 7, UP_FACES, UP_ROWS), (zd, 0, DOWN_FACES, DOWN_ROWS)):
+        values = {("f", k): field(k, p) for k in (0, 1, 6, 7, 12)}
+        q, g = electric_coefficients(*of_plane(p), values["f", 12])
         for base in (0, 6):
-            new = magnetic(
-                *[field(base + c, p) for c in range(3)], field(base, p + 1), field(base + 1, p + 1),
-                *[field(base + 3 + c, p) for c in range(3)], r, lambda v, _: pltpu.roll(v, COLS - 1, 1), up_row,
+            h = half_step(base, p)
+            down = half_step(base, 6)[0:2] if p == 7 else [zero, zero]
+            e = electric(
+                *h, *down, *[field(base + c, p) for c in range(3)], q, g, drive if p == 7 and base == 0 else None, prev_x, down_row
             )
             for c in range(3):
-                half[base + 3 + c, p] = new[c]
-
-    def value_of(k, p):
-        return half[k, p] if (k, p) in half else field(k, p)
-
-    face_out(zu, UP_FACES, UP_ROWS, value_of)
-    face_out(zd, DOWN_FACES, DOWN_ROWS, value_of)
-
-
-def third_kernel(pml, xa, xb, strips, strips_rim, sides, rim_up, rim_down):
+                values["h", base + 3 + c] = h[c]
+                values["e", base + c] = e[c]
+        face_out(out, faces, rows, values)
+
+
+def third_kernel(pml, xa, xb, strips, strips_rim, factors, sides, rim_up, rim_down):
     index = lax.axis_index("gx")
     even = parity("gx")
     has_after = (index < lax.axis_size("gx") - 1).astype(F32)
@@ -296,29 +312,23 @@
         value = jnp.where(own, value, 0.0)
         sides[k] = value
         side.append(value)
-    r = damping(*side_sigma(pml))
-    stepped = list(side)
+    sigma, inside = side_sigma(pml)
+    r = damping(sigma, inside)
+    q, g = electric_coefficients(sigma, inside, side[12])
+    drive = jnp.concatenate([factors[0]] * (TALL // 8), axis=0) * side[13]
+    values = {("f", k): side[k] for k in range(COMPS)}
     for base in (0, 6):
-        stepped[base + 3 : base + 6] = side_magnetic(side[base : base + 3], side[base + 3 : base + 6], r)
-    for out, items in ((rim_up, UP_SIDES), (rim_down, DOWN_SIDES)):
+        e = side[base : base + 3]
+        h = [jnp.where(own, v, 0.0) for v in side_magnetic(e, side[base + 3 : base + 6], r)]
+        e = side_electric(h, e, q, g, drive if base == 0 else None)
+        for c in range(3):
+            values["h", base + 3 + c] = h[c]
+            values["e", base + c] = e[c]
+    for out, items, p in ((rim_up, UP_SIDES, 7), (rim_down, DOWN_SIDES, 0)):
         packed = jnp.zeros((TALL, COLS), F32)
-        for i, (k, p) in enumerate(items):
-            value = side[k] if p == 7 else stepped[k]
-            packed = jnp.where((lane >> 3) == i, turn(value, 8 * i - 8 * (p + 2), 1), packed)
+        for i, item in enumerate(items):
+            packed = jnp.where((lane >> 3) == i, turn(values[item], 8 * i - 8 * (p + 2), 1), packed)
         out[...] = packed
-
-
-def drive_factors(start):
-    factors = []
-    for k in (1, 2):
-        phase = jnp.full((8, COLS), lax.rem(start[0] + k, PERIOD), jnp.int32).astype(F32)
-        factor = jnp.sin(phase * (2.0 * math.pi / PERIOD))
-        factors.append(jnp.concatenate([factor] * (TALL // 8), axis=0))
-    return factors
-
-
-def spread(first, split, gap):
-    return lambda i: i + first + (gap if i >= split else 0)
 
 
 def home(layer):
@@ -326,22 +336,18 @@
     return (((layer >> 2) ^ mine) << 2) + (layer & 3)
 
 
-def run_steps(pml, start, layer, f, one, rr, qq, gg, xf, xone, frozen, planes, sums, put):
+def run_steps(pml, factors, layer, f, one, rr, qq, gg, xf, xone, planes, sums, put, halo=None):
     sigma, inside = side_sigma(pml)
     xr = damping(sigma, inside)
     xq, xg = electric_coefficients(sigma, inside, xf[12])
-    factors = drive_factors(start)
+    factors = [jnp.concatenate([factors[k]] * (TALL // 8), axis=0) for k in range(2)]
     lane = lanes(TALL)
     first_lane, last_lane = lane == 0, lane == COLS - 1
-    held = (lane >> 3) == -1
-    for idx in frozen:
-        held = held | ((lane >> 3) == idx)
-
-    def side_half(e_ref, e_base, h_base, hold):
-        old = [xf[h_base + c] for c in range(3)]
-        new = side_magnetic([e_ref[e_base + c] for c in range(3)], old, xr)
+
+    def side_half(e_ref, e_base, h_base):
+        new = side_magnetic([e_ref[e_base + c] for c in range(3)], [xf[h_base + c] for c in range(3)], xr)
         for c in range(3):
-            xf[h_base + c] = jnp.where(held, old[c], new[c]) if hold else new[c]
+            xf[h_base + c] = new[c]
 
     def side_full(e_base, h_base, out_base, factor):
         drive = None if factor is None else xf[13] * factor
@@ -375,18 +381,18 @@
         )
 
     def over(which, body):
-        count, index = planes[which]
-
-        for i in range(count):
-            body(index(i))
+        for idx in planes[which]:
+            body(idx)
 
     def body(idx):
         plane_magnetic(idx, f, xf, 0, 3)
         plane_magnetic(idx, f, xf, 6, 9)
 
     over(0, body)
-    side_half(xf, 0, 3, True)
-    side_half(xf, 6, 9, True)
+    side_half(xf, 0, 3)
+    side_half(xf, 6, 9)
+    if halo is not None:
+        halo(xr, xq, sides=False)
 
     def body(idx):
         for base, out, factor in ((0, 0, factors[0]), (6, 3, None)):
@@ -397,14 +403,16 @@
     over(1, body)
     side_full(0, 3, 0, factors[0])
     side_full(6, 9, 3, None)
+    if halo is not None:
+        halo(xr, xq, sides=True)
 
     def body(idx):
         plane_magnetic(idx, one, xone, 0, 3)
         plane_magnetic(idx, one, xone, 3, 9)
 
     over(2, body)
-    side_half(xone, 0, 3, False)
-    side_half(xone, 3, 9, False)
+    side_half(xone, 0, 3)
+    side_half(xone, 3, 9)
 
     def body(idx):
         two = plane_electric(idx, one, 0, 3, factors[1])
@@ -420,7 +428,7 @@
     over(3, body)
 
 
-def inner_kernel(layer, pml, start, own, tiles, sides, f, one, rr, qq, gg, sums, e_mid, h_mid, xf, xone):
+def inner_kernel(layer, pml, factors, own, tiles, sides, f, one, rr, qq, gg, sums, e_mid, h_mid, xf, xone):
     del own
     for k in range(COMPS):
         for p in range(PLANES):
@@ -441,12 +449,12 @@
         e_mid[c, idx - 4] = e_new
         h_mid[c, idx - 4] = h_new
 
-    planes = [(7, lambda i: i + 2), (6, lambda i: i + 3), (5, lambda i: i + 3), (4, lambda i: i + 4)]
-    run_steps(pml, start, layer, f, one, rr, qq, gg, xf, xone, (), planes, sums, put)
+    planes = [range(2, 9), range(3, 9), range(3, 8), range(4, 8)]
+    run_steps(pml, factors, layer, f, one, rr, qq, gg, xf, xone, planes, sums, put)
 
 
 def outer_kernel(
-    layer, pml, start, f_in, one_in, rr_in, qq_in, gg_in, sums_in, zu, zd, sides, rim_up, rim_down,
+    layer, pml, factors, f_in, one_in, rr_in, qq_in, gg_in, sums_in, zu, zd, sides, rim_up, rim_down,
     f, one, rr, qq, gg, sums, e_rest, h_rest, first, second, third, xf, xone,
 ):
     del f_in, one_in, rr_in, qq_in, gg_in, sums_in
@@ -454,35 +462,71 @@
     has_above = (index < lax.axis_size("gz") - 1).astype(F32)
     has_below = (index > 0).astype(F32)
     lane = lanes(TALL)
+    low, top = 1, PLANES + 2
     for k in range(COMPS):
         xf[k] = sides[k]
-    for ref, faces, rows, rim, items, shift, keep in (
-        (zu, UP_FACES, UP_ROWS, rim_up, UP_SIDES, -6, has_below),
-        (zd, DOWN_FACES, DOWN_ROWS, rim_down, DOWN_SIDES, PLANES + 2, has_above),
+    got = {}
+    for ref, faces, rows, rim, items, idx, keep in (
+        (zu, UP_FACES, UP_ROWS, rim_up, UP_SIDES, low, has_below),
+        (zd, DOWN_FACES, DOWN_ROWS, rim_down, DOWN_SIDES, top, has_above),
     ):
-        for (k, p), (plane, tile) in face_in(ref, faces, rows, keep).items():
-            f[k, p + shift, 0:ROWS] = plane
-            f[k, p + shift, ROWS:TALL] = tile
         packed = rim[...] * keep
-        for i, (k, p) in enumerate(items):
-            xf[k] = jnp.where((lane >> 3) == p + shift, turn(packed, 8 * (p + shift) - 8 * i, 1), xf[k])
-    last_lane = lane == COLS - 1
-    top = PLANES + 2
-    for k, idx in ((4, 0), (10, 0), (4, top), (5, top), (10, top), (11, top)):
-        f[k, idx] = jnp.where(last_lane, turn(xf[k], 126 - 8 * idx, 1), f[k, idx])
+        planes = face_in(ref, faces, rows, keep)
+        for i, (kind, k) in enumerate(items):
+            if kind != "f":
+                at_last, at_first = turn(packed, 126 - 8 * i, 1), turn(packed, -6 - 8 * i, 1)
+                fixed = jnp.where(lane == COLS - 1, at_last, planes[kind, k])
+                planes[kind, k] = jnp.where(lane == 0, at_first, fixed) if kind == "e" else fixed
+            got[kind, k, idx] = (planes[kind, k], turn(packed, 8 * idx - 8 * i, 1))
+        for k in (0, 1, 6, 7, 12):
+            if ("f", k) in planes:
+                f[k, idx] = planes["f", k]
+                xf[k] = jnp.where((lane >> 3) == idx, got["f", k, idx][1], xf[k])
     of_plane = block_sigma(pml)
-    for idx in (1, top):
+    for idx in (low, top):
         sigma, inside = of_plane(idx - 2)
         rr[idx] = damping(sigma, inside)
         qq[idx], gg[idx] = electric_coefficients(sigma, inside, f[12, idx])
+
+    def add_z(q, x, y, prev_x):
+        return q * ((y - prev_x(y)) - (x - down_row(x, 0)))
+
+    def halo(xr, xq, sides):
+        q, q_top, r_half = qq[low], qq[top], 0.5 * rr[low]
+        for base, out in ((0, 0), (6, 3)):
+            x_side = 0.5 * xr * pltpu.roll(xf[base + 1], 120, 1)
+            y_side = -0.5 * xr * pltpu.roll(xf[base], 120, 1)
+            if sides:
+                added = got["e", base + 2, low][1] + add_z(xq, x_side, y_side, lambda v: pltpu.roll(v, 1, 1))
+                xone[out + 2] = jnp.where((lane >> 3) == low, added, xone[out + 2])
+                added = got["e", base, top][1] + xq * pltpu.roll(xf[base + 4], 8, 1)
+                xone[out] = jnp.where((lane >> 3) == top, added, xone[out])
+                added = got["e", base + 1, top][1] - xq * pltpu.roll(xf[base + 3], 8, 1)
+                xone[out + 1] = jnp.where((lane >> 3) == top, added, xone[out + 1])
+                continue
+            x, y = r_half * f[base + 1, 2], -r_half * f[base, 2]
+
+            def prev_x(value):
+                return jnp.where(lane == 0, pltpu.roll(y_side, 123 - 8 * low, 1), pltpu.roll(value, 1, 1))
+
+            for k, term, side_term in ((base + 3, x, x_side), (base + 4, y, y_side)):
+                plane, side = got["h", k, low]
+                f[k, low] = plane + term
+                xf[k] = jnp.where((lane >> 3) == low, side + side_term, xf[k])
+            f[base + 5, low] = jnp.zeros((TALL, COLS), F32)
+            one[out, low] = got["e", base, low][0] - q * y
+            one[out + 1, low] = got["e", base + 1, low][0] + q * x
+            one[out + 2, low] = got["e", base + 2, low][0] + add_z(q, x, y, prev_x)
+            one[out, top] = got["e", base, top][0] + q_top * f[base + 4, top - 1]
+            one[out + 1, top] = got["e", base + 1, top][0] - q_top * f[base + 3, top - 1]
 
     def put(c, idx, e_new, h_new):
         at = idx - 2 if idx < 4 else idx - 6
         e_rest[c, at] = e_new
         h_rest[c, at] = h_new
 
-    planes = [(2, lambda i: 8 * i + 1), (4, spread(1, 2, 6)), (4, spread(1, 2, 5)), (4, spread(2, 2, 4))]
-    run_steps(pml, start, layer, f, one, rr, qq, gg, xf, xone, (0, top), planes, sums, put)
+    planes = [(9,), (2, 9), (1, 2, 8, 9), (2, 3, 8, 9)]
+    run_steps(pml, factors, layer, f, one, rr, qq, gg, xf, xone, planes, sums, put, halo)
     for i, out in enumerate((first, second, third)):
         out[...] = sums[4 * i + 4 : 4 * i + 8]
 
@@ -511,7 +555,7 @@
     out[...] = kept[...] + got[...]
 
 
-def call(kernel, outs, scratch=(), scalars=0, far=0, aliases=None, out_space=pltpu.VMEM):
+def call(kernel, outs, scratch=(), scalars=0, far=0, aliases=None, out_space=pltpu.VMEM, flops=1000000):
     def run(*args):
         near = len(args) - scalars - far
         specs = [pl.BlockSpec(memory_space=pltpu.SMEM)] * scalars
@@ -525,7 +569,7 @@
             scratch_shapes=[pltpu.VMEM(s, F32) if isinstance(s, tuple) else s for s in scratch],
             input_output_aliases=aliases or {},
             compiler_params=pltpu.CompilerParams(vmem_limit_bytes=24 * 2**20),
-            cost_estimate=pl.CostEstimate(flops=1000000, bytes_accessed=size, transcendentals=0),
+            cost_estimate=pl.CostEstimate(flops=flops, bytes_accessed=size, transcendentals=0),
         )(*args)
 
     return run
@@ -565,30 +609,30 @@
     )(*raw)
     yb = lax.ppermute(yb, ("gy", "gx"), inner_swaps())
     ya = lax.ppermute(ya, "gy", swaps("gy", 0))
-    strips, right, left = call(strip_kernel, [(COMPS,) + block, (2,) + block, (2,) + block])(f)
+    strips, right, left, factors = call(
+        strip_kernel, [(COMPS,) + block, (2,) + block, (2,) + block, (2, 8, COLS)], scalars=1
+    )(start_step, f)
     side = (2,) + tall
-    tiles, strips_rim, xa, xb, zu, zd = call(
-        second_kernel,
-        [(COMPS, PLANES, 8, COLS), (COMPS, 8, COLS), side, side, (face_rows(UP_FACES, UP_ROWS), COLS), (face_rows(DOWN_FACES, DOWN_ROWS), COLS)],
-        scalars=1,
-    )(pml_cells, f, ya, yb, right, left)
+    tiles, strips_rim, xa, xb = call(second_kernel, [(COMPS, PLANES, 8, COLS), (COMPS, 8, COLS), side, side])(ya, yb, right, left)
+    sizes = [(face_rows(*lists), COLS) for lists in ((UP_FACES, UP_ROWS), (DOWN_FACES, DOWN_ROWS))]
+    zu, zd = call(face_kernel, sizes, scalars=1)(pml_cells, f, tiles, factors)
     zu = lax.ppermute(zu, "gz", ring("gz", 1))
     zd = lax.ppermute(zd, "gz", ring("gz", -1))
     xa = lax.ppermute(xa, "gx", swaps("gx", 0))
     xb = lax.ppermute(xb, "gx", swaps("gx", 1))
-    sides, rim_up, rim_down = call(third_kernel, [(COMPS,) + tall, tall, tall], scalars=1)(pml_cells, xa, xb, strips, strips_rim)
+    sides, rim_up, rim_down = call(third_kernel, [(COMPS,) + tall, tall, tall], scalars=1)(pml_cells, xa, xb, strips, strips_rim, factors)
     rim_up = lax.ppermute(rim_up, "gz", ring("gz", 1))
     rim_down = lax.ppermute(rim_down, "gz", ring("gz", -1))
     state = [(COMPS,) + deep, (6,) + deep, deep, deep, deep, (LAYERS,) + block]
     mid, out = (3, PLANES // 2) + block, (3, PLANES) + block
     side = [(COMPS,) + tall, (6,) + tall]
-    *held, e_mid, h_mid = call(inner_kernel, state + [mid, mid], side, scalars=3, aliases={3: 0})(
-        layer_of_cell, pml_cells, start_step, f, tiles, sides
+    *held, e_mid, h_mid = call(inner_kernel, state + [mid, mid], side, scalars=2, aliases={3: 0}, flops=10**11)(
+        layer_of_cell, pml_cells, factors, f, tiles, sides
     )
     quarter, pair = (LAYERS // 4,) + block, (2,) + block
     *_, sums, e_rest, h_rest, first, second, third = call(
-        outer_kernel, state + [mid, mid, quarter, quarter, quarter], side, scalars=3, aliases={3 + i: i for i in range(len(state))}
-    )(layer_of_cell, pml_cells, start_step, *held, zu, zd, sides, rim_up, rim_down)
+        outer_kernel, state + [mid, mid, quarter, quarter, quarter], side, scalars=2, aliases={3 + i: i for i in range(len(state))}
+    )(layer_of_cell, pml_cells, factors, *held, zu, zd, sides, rim_up, rim_down)
     e_out, h_out = call(store_kernel, [out, out], [pltpu.SemaphoreType.DMA((6,))], out_space=pltpu.HBM)(e_mid, h_mid, e_rest, h_rest)
     first, second, third = (lax.ppermute(v, "gz", across("gz", m)) for v, m in ((first, 2), (second, 4), (third, 6)))
     kept, sent = call(fold_kernel, [pair, pair])(sums, first, second, third)

time: 47.7 us -> 46.5 us (0.975)
  starting transfers between devices: 26.7 us -> 24.7 us
  Pallas kernels: 9.88 us -> 10.4 us
    ppermute x1, starting transfers between devices: 4.02 us -> 0.01 us  [local(): zu = lax.ppermute(zu, 'gz', ring('gz', 1))]
    ppermute x1, starting transfers between devices: 2.53 us -> 6.4 us  [local(): zd = lax.ppermute(zd, 'gz', ring('gz', -1))]
    ppermute x1, waiting for transfers between devices: 2.7 us -> 0.01 us  [local(): xb = lax.ppermute(xb, 'gx', swaps('gx', 1))]
    ppermute x1, starting transfers between devices: 4.38 us -> 2.27 us  [local(): lax.ppermute(sent, 'gz', across('gz', 1))]
    ppermute x3, waiting for transfers between devices: 2.83 us -> 4.54 us  [local(): lax.ppermute(v, 'gz', across('gz', m))]
    ppermute x1, waiting for transfers between devices: 0.97 us -> 2.3 us  [local(): lax.ppermute(sent, 'gz', across('gz', 1))]
    ppermute x1, starting transfers between devices: 1.07 us -> 2.04 us  [local(): rim_up = lax.ppermute(rim_up, 'gz', ring('gz', 1))]
    ppermute x1, starting transfers between devices: 4.64 us -> 3.74 us  [local(): rim_down = lax.ppermute(rim_down, 'gz', ring('gz', -1))]
  transfers between devices with their start and end apart: 12 -> 12, of which waited for: 6 -> 6; matrix products, arithmetic and copies ran while one was open for 0% -> 0% of each run, Pallas kernels for 10% -> 13%
where the time goes in v4:
time: 46.5 us; the launch traced here: 46.4 us
  starting transfers between devices  24.7 us (53%)
  Pallas kernels  10.4 us (22%)
  waiting for transfers between devices  9.86 us (21%)
  between operations  1.39 us (3%)
    pallas_call x10, Pallas kernels, run(): pl.pallas_call(kernel, out_shape=[jax.ShapeDtypeStruct(s, F32) for s in o...  10.4 us
    ppermute x1, starting transfers between devices, local(): zd = lax.ppermute(zd, 'gz', ring('gz', -1))  6.4 us
    ppermute x3, starting transfers between devices, local(): lax.ppermute(v, 'gz', across('gz', m))  4.77 us
    ppermute x3, waiting for transfers between devices, local(): lax.ppermute(v, 'gz', across('gz', m))  4.54 us
    ppermute x1, starting transfers between devices, local(): rim_down = lax.ppermute(rim_down, 'gz', ring('gz', -1))  3.74 us
    ppermute x1, waiting for transfers between devices, local(): lax.ppermute(sent, 'gz', across('gz', 1))  2.3 us
    ppermute x1, starting transfers between devices, local(): lax.ppermute(sent, 'gz', across('gz', 1))  2.27 us
    ppermute x1, starting transfers between devices, local(): xb = lax.ppermute(xb, 'gx', swaps('gx', 1))  2.1 us
  transfers between devices with their start and end apart: 12, of which 6 were waited for; matrix products, arithmetic and copies ran while one was open for 0% of the time, Pallas kernels for 13%

profile of v4, /device:TPU:0, one launch (start us, length us, event | category | flops | bytes accessed | tf_op | source)
XLA Modules:
  0.0 46.4 jit_solution(9726382482628558344)
XLA Ops:
  0.6 0.0 copy-start
  0.6 1.7 %shard_map.112 = (f32[14,12,40,128]{3,2,1,0:T(8,128)S(1)}, f32[224,128]{1,0:T(8,128)S(1)}, f32[224,128]{1,0:T(8,128)S(1)}) custom-call(f32[3,8,32,128]{3,2,1,0:T(8,128)} %e.1, f32[3,8,32,128]{3,2,1,0:T(8,128)} %h.1, f32[3,8,32,128]{3,2,1,0:T(8,128)} %ae.1, f32[3,8,32,128]{3,2,1,0:T(8,128)} %ah.1, f32[8,32,128]{2,1,0:T(8,128)} %eps.1, f32[8,32,128]{2,1,0:T(8,128)} %cur.1), custom_call_target="tpu_custom_call" | custom-call | flops 1000000 | bytes 5505024 | tf_op jit(solution)/shard_map/pallas_call | solution.py:564
  2.3 0.1 collective-permute-start
  2.4 1.7 %collective-permute-start.1 = (f32[224,128]{1,0:T(8,128)S(1)}, f32[224,128]{1,0:T(8,128)S(1)}, u32[]{:S(2)}, u32[]{:S(2)}) collective-permute-start(f32[224,128]{1,0:T(8,128)S(1)} %get-tuple-element.40), channel_id=1, source_target_pairs={{4,8},{0,1},{12,13},{5,9},{6,10},{2,3},{14,15},{7,11},{8,4},{1,0},... | collective-permute-start | bytes 344072 | tf_op jit(solution)/shard_map/ppermute | solution.py:610
  4.7 0.0 copy-start.1
  4.7 0.6 %shard_map.113 = (f32[14,32,128]{2,1,0:T(8,128)S(1)}, f32[2,32,128]{2,1,0:T(8,128)S(1)}, f32[2,32,128]{2,1,0:T(8,128)S(1)}, f32[2,8,128]{2,1,0:T(8,128)S(1)}) custom-call(s32[1]{0:T(128)S(6)} %copy.26.start, f32[14,12,40,128]{3,2,1,0:T(8,128)S(1)} %get-tuple-element.37.f.own), custom_call_target="tpu_custom_call" | custom-call | flops 1000000 | bytes 3743748 | tf_op jit(solution)/shard_map/pallas_call | solution.py:564
  5.4 0.0 collective-permute-done.ya
  5.4 1.9 %collective-permute-done.1.yb = f32[224,128]{1,0:T(8,128)S(1)} collective-permute-done((f32[224,128]{1,0:T(8,128)S(1)}, f32[224,128]{1,0:T(8,128)S(1)}, u32[]{:S(2)}, u32[]{:S(2)}) %collective-permute-start.1) | collective-permute-done | bytes 114720 | tf_op jit(solution)/shard_map/ppermute | solution.py:610
  7.3 0.3 shard_map.114
  7.5 1.7 %collective-permute-start.2 = (f32[2,40,128]{2,1,0:T(8,128)S(1)}, f32[2,40,128]{2,1,0:T(8,128)S(1)}, u32[]{:S(2)}, u32[]{:S(2)}) collective-permute-start(f32[2,40,128]{2,1,0:T(8,128)S(1)} %get-tuple-element.44), channel_id=1, source_target_pairs={{0,1},{2,3},{1,0},{3,2},{4,5},{6,7},{5,4},{7,6},{8,9},{10,11},{9,8... | collective-permute-start | bytes 122888 | tf_op jit(solution)/shard_map/ppermute | solution.py:621
  9.2 2.1 %collective-permute-start.3 = (f32[2,40,128]{2,1,0:T(8,128)S(1)}, f32[2,40,128]{2,1,0:T(8,128)S(1)}, u32[]{:S(2)}, u32[]{:S(2)}) collective-permute-start(f32[2,40,128]{2,1,0:T(8,128)S(1)} %get-tuple-element.45), channel_id=1, source_target_pairs={{1,2},{3,0},{2,1},{0,3},{5,6},{7,4},{6,5},{4,7},{9,10},{11,8},{10,... | collective-permute-start | bytes 122888 | tf_op jit(solution)/shard_map/ppermute | solution.py:622
  11.3 0.0 copy-done
  11.3 0.8 %shard_map.117 = (f32[368,128]{1,0:T(8,128)S(1)}, f32[312,128]{1,0:T(8,128)S(1)}) custom-call(s32[3]{0:T(128)S(1)} %copy-done, f32[14,12,40,128]{3,2,1,0:T(8,128)S(1)} %get-tuple-element.37.f.own, f32[14,8,8,128]{3,2,1,0:T(8,128)S(1)} %get-tuple-element.43.tiles, f32[2,8,128]{2,1,0:T(8,128)S(1)} %get-tuple-element.38.factors), custom_call_target="tpu_custom_call" | custom-call | flops 1000000 | bytes 4255756 | tf_op jit(solution)/shard_map/pallas_call | solution.py:564
  12.1 6.4 %collective-permute-start.5 = (f32[312,128]{1,0:T(8,128)S(1)}, f32[312,128]{1,0:T(8,128)S(1)}, u32[]{:S(2)}, u32[]{:S(2)}) collective-permute-start(f32[312,128]{1,0:T(8,128)S(1)} %get-tuple-element.56), channel_id=1, source_target_pairs={{0,112},{16,0},{32,16},{48,32},{64,48},{80,64},{96,80},{112,96},{1... | collective-permute-start | bytes 479240 | tf_op jit(solution)/shard_map/ppermute | solution.py:620
  18.5 0.0 collective-permute-start.4
  18.5 0.0 collective-permute-done.2.xa
  18.5 0.0 collective-permute-done.3.xb
  18.5 1.1 %shard_map.115 = (f32[14,40,128]{2,1,0:T(8,128)S(1)}, f32[40,128]{1,0:T(8,128)S(1)}, f32[40,128]{1,0:T(8,128)S(1)}) custom-call(s32[3]{0:T(128)S(1)} %copy-done, f32[2,40,128]{2,1,0:T(8,128)S(1)} %collective-permute-done.2.xa, f32[2,40,128]{2,1,0:T(8,128)S(1)} %collective-permute-done.3.xb, f32[14,32,128]{2,1,0:T(8,128)S(1)} %get-tuple-element.46.strips, ...), custom_call_target="tpu_custom_call" | custom-call | flops 1000000 | bytes 704524 | tf_op jit(solution)/shard_map/pallas_call | solution.py:564
  19.6 2.0 %collective-permute-start.6 = (f32[40,128]{1,0:T(8,128)S(1)}, f32[40,128]{1,0:T(8,128)S(1)}, u32[]{:S(2)}, u32[]{:S(2)}) collective-permute-start(f32[40,128]{1,0:T(8,128)S(1)} %get-tuple-element.57), channel_id=1, source_target_pairs={{0,16},{16,32},{32,48},{48,64},{64,80},{80,96},{96,112},{112,0},{1... | collective-permute-start | bytes 61448 | tf_op jit(solution)/shard_map/ppermute | solution.py:624
  21.6 3.7 %collective-permute-start.7 = (f32[40,128]{1,0:T(8,128)S(1)}, f32[40,128]{1,0:T(8,128)S(1)}, u32[]{:S(2)}, u32[]{:S(2)}) collective-permute-start(f32[40,128]{1,0:T(8,128)S(1)} %get-tuple-element.58), channel_id=1, source_target_pairs={{0,112},{16,0},{32,16},{48,32},{64,48},{80,64},{96,80},{112,96},{1... | collective-permute-start | bytes 61448 | tf_op jit(solution)/shard_map/ppermute | solution.py:625
  25.4 0.0 copy-done.1
  25.4 2.4 %shard_map.116 = (f32[14,12,40,128]{3,2,1,0:T(8,128)S(1)}, f32[6,12,40,128]{3,2,1,0:T(8,128)S(1)}, f32[12,40,128]{2,1,0:T(8,128)S(1)}, f32[12,40,128]{2,1,0:T(8,...) custom-call(s32[8]{0:T(128)S(1)} %copy-done.1, ...), custom_call_target="tpu_custom_call", output_to_operand_aliasing={{0}: (3, {})} | custom-call | flops 99999997952 | bytes 10502188 | tf_op jit(solution)/shard_map/pallas_call | solution.py:564
  27.8 0.8 %collective-permute-done.6.rim_up = f32[40,128]{1,0:T(8,128)S(1)} collective-permute-done((f32[40,128]{1,0:T(8,128)S(1)}, f32[40,128]{1,0:T(8,128)S(1)}, u32[]{:S(2)}, u32[]{:S(2)}) %collective-permute-start.6) | collective-permute-done | bytes 20512 | tf_op jit(solution)/shard_map/ppermute | solution.py:624
  28.5 0.3 collective-permute-done.7.rim_down
  28.9 0.0 collective-permute-done.5.zd
  28.9 0.0 collective-permute-done.4.zu
  28.9 2.0 %shard_map.118 = (f32[14,12,40,128]{3,2,1,0:T(8,128)S(1)}, f32[6,12,40,128]{3,2,1,0:T(8,128)S(1)}, f32[12,40,128]{2,1,0:T(8,128)S(1)}, f32[12,40,128]{2,1,0:T(8,...) custom-call(s32[8]{0:T(128)S(1)} %copy-done.1, ...), custom_call_target="tpu_custom_call", output_to_operand_aliasing={{0}: (3, {}), {1}: (4, {}), {2}: (5, {}), {3}: (6, {}), {4}... | custom-call | flops 1000000 | bytes 13103148 | tf_op jit(solution)/shard_map/pallas_call | solution.py:564
  30.9 0.1 collective-permute-start.8
  31.0 3.8 %collective-permute-start.9 = (f32[4,32,128]{2,1,0:T(8,128)S(1)}, f32[4,32,128]{2,1,0:T(8,128)S(1)}, u32[]{:S(2)}, u32[]{:S(2)}) collective-permute-start(f32[4,32,128]{2,1,0:T(8,128)S(1)} %get-tuple-element.61), channel_id=1, source_target_pairs={{0,64},{16,80},{32,96},{48,112},{64,0},{80,16},{96,32},{112,48},{1... | collective-permute-start | bytes 196616 | tf_op jit(solution)/shard_map/ppermute | solution.py:637
  34.7 0.9 %collective-permute-start.10 = (f32[4,32,128]{2,1,0:T(8,128)S(1)}, f32[4,32,128]{2,1,0:T(8,128)S(1)}, u32[]{:S(2)}, u32[]{:S(2)}) collective-permute-start(f32[4,32,128]{2,1,0:T(8,128)S(1)} %get-tuple-element.62), channel_id=1, source_target_pairs={{0,96},{16,112},{32,64},{48,80},{64,32},{80,48},{96,0},{112,16},{1... | collective-permute-start | bytes 196616 | tf_op jit(solution)/shard_map/ppermute | solution.py:637
  35.7 0.0 collective-permute-done.8.first
  35.7 2.0 %collective-permute-done.9.second = f32[4,32,128]{2,1,0:T(8,128)S(1)} collective-permute-done((f32[4,32,128]{2,1,0:T(8,128)S(1)}, f32[4,32,128]{2,1,0:T(8,128)S(1)}, u32[]{:S(2)}, u32[]{:S(2)}) %collective-permute-start.9) | collective-permute-done | bytes 65568 | tf_op jit(solution)/shard_map/ppermute | solution.py:637
  37.7 2.5 %collective-permute-done.10.third = f32[4,32,128]{2,1,0:T(8,128)S(1)} collective-permute-done((f32[4,32,128]{2,1,0:T(8,128)S(1)}, f32[4,32,128]{2,1,0:T(8,128)S(1)}, u32[]{:S(2)}, u32[]{:S(2)}) %collective-permute-start.10) | collective-permute-done | bytes 65568 | tf_op jit(solution)/shard_map/ppermute | solution.py:637
  40.2 2.3 %collective-permute-start.11 = (f32[2,32,128]{2,1,0:T(8,128)S(1)}, f32[2,32,128]{2,1,0:T(8,128)S(1)}, u32[]{:S(2)}, u32[]{:S(2)}) collective-permute-start(f32[2,32,128]{2,1,0:T(8,128)S(1)} %get-tuple-element.64), channel_id=1, source_target_pairs={{0,16},{16,0},{32,48},{48,32},{64,80},{80,64},{96,112},{112,96},{1... | collective-permute-start | bytes 98312 | tf_op jit(solution)/shard_map/ppermute | solution.py:639
  42.5 0.9 %shard_map.121 = (f32[3,8,32,128]{3,2,1,0:T(8,128)}, f32[3,8,32,128]{3,2,1,0:T(8,128)}) custom-call(f32[3,4,32,128]{3,2,1,0:T(8,128)S(1)} %get-tuple-element.65.e_mid, f32[3,4,32,128]{3,2,1,0:T(8,128)S(1)} %get-tuple-element.66.h_mid, f32[3,4,32,128]{3,2,1,0:T(8,128)S(1)} %get-tuple-element.67.e_rest, f32[3,4,32,128]{3,2,1,0:T(8,128)S(1)} %get-tuple-element.68.h_rest), custom_call_target="tpu_custom_call" | custom-call | flops 1000000 | bytes 1572864 | tf_op jit(solution)/shard_map/pallas_call | solution.py:564
  43.4 2.3 %collective-permute-done.11.got = f32[2,32,128]{2,1,0:T(8,128)S(1)} collective-permute-done((f32[2,32,128]{2,1,0:T(8,128)S(1)}, f32[2,32,128]{2,1,0:T(8,128)S(1)}, u32[]{:S(2)}, u32[]{:S(2)}) %collective-permute-start.11) | collective-permute-done | bytes 32800 | tf_op jit(solution)/shard_map/ppermute | solution.py:639
  45.7 0.6 %shard_map.120 = f32[2,32,128]{2,1,0:T(8,128)} custom-call(f32[2,32,128]{2,1,0:T(8,128)S(1)} %get-tuple-element.63.kept, f32[2,32,128]{2,1,0:T(8,128)S(1)} %collective-permute-done.11.got), custom_call_target="tpu_custom_call" | custom-call | flops 1000000 | bytes 98304 | tf_op jit(solution)/shard_map/pallas_call | solution.py:564
  (1 shorter events, 0.0 us)
Async XLA Ops:
  0.6 10.7 %copy-start = (s32[3]{0:T(128)S(1)}, s32[3]{0:T(128)}, u32[]{:S(2)}) copy-start(s32[3]{0:T(128)} %pml.7) | copy-start | bytes 40
  2.3 3.1 %collective-permute-start = (f32[224,128]{1,0:T(8,128)S(1)}, f32[224,128]{1,0:T(8,128)S(1)}, u32[]{:S(2)}, u32[]{:S(2)}) collective-permute-start(f32[224,128]{1,0:T(8,128)S(1)} %get-tuple-element.39), channel_id=1, source_target_pairs={{0,4},{8,12},{4,0},{12,8},{1,5},{9,13},{5,1},{13,9},{2,6},{10,14},... | collective-permute-start | bytes 344072 | tf_op jit(solution)/shard_map/ppermute | solution.py:611
  2.4 4.9 %collective-permute-start.1 = (f32[224,128]{1,0:T(8,128)S(1)}, f32[224,128]{1,0:T(8,128)S(1)}, u32[]{:S(2)}, u32[]{:S(2)}) collective-permute-start(f32[224,128]{1,0:T(8,128)S(1)} %get-tuple-element.40), channel_id=1, source_target_pairs={{4,8},{0,1},{12,13},{5,9},{6,10},{2,3},{14,15},{7,11},{8,4},{1,0},... | collective-permute-start | bytes 344072 | tf_op jit(solution)/shard_map/ppermute | solution.py:610
  4.7 20.7 %copy-start.1 = (s32[8]{0:T(128)S(1)}, s32[8]{0:T(128)}, u32[]{:S(2)}) copy-start(s32[8]{0:T(128)} %layer.3) | copy-start | bytes 100
  7.5 10.9 %collective-permute-start.2 = (f32[2,40,128]{2,1,0:T(8,128)S(1)}, f32[2,40,128]{2,1,0:T(8,128)S(1)}, u32[]{:S(2)}, u32[]{:S(2)}) collective-permute-start(f32[2,40,128]{2,1,0:T(8,128)S(1)} %get-tuple-element.44), channel_id=1, source_target_pairs={{0,1},{2,3},{1,0},{3,2},{4,5},{6,7},{5,4},{7,6},{8,9},{10,11},{9,8... | collective-permute-start | bytes 122888 | tf_op jit(solution)/shard_map/ppermute | solution.py:621
  9.2 9.3 %collective-permute-start.3 = (f32[2,40,128]{2,1,0:T(8,128)S(1)}, f32[2,40,128]{2,1,0:T(8,128)S(1)}, u32[]{:S(2)}, u32[]{:S(2)}) collective-permute-start(f32[2,40,128]{2,1,0:T(8,128)S(1)} %get-tuple-element.45), channel_id=1, source_target_pairs={{1,2},{3,0},{2,1},{0,3},{5,6},{7,4},{6,5},{4,7},{9,10},{11,8},{10,... | collective-permute-start | bytes 122888 | tf_op jit(solution)/shard_map/ppermute | solution.py:622
  12.1 16.8 %collective-permute-start.5 = (f32[312,128]{1,0:T(8,128)S(1)}, f32[312,128]{1,0:T(8,128)S(1)}, u32[]{:S(2)}, u32[]{:S(2)}) collective-permute-start(f32[312,128]{1,0:T(8,128)S(1)} %get-tuple-element.56), channel_id=1, source_target_pairs={{0,112},{16,0},{32,16},{48,32},{64,48},{80,64},{96,80},{112,96},{1... | collective-permute-start | bytes 479240 | tf_op jit(solution)/shard_map/ppermute | solution.py:620
  18.5 10.4 %collective-permute-start.4 = (f32[368,128]{1,0:T(8,128)S(1)}, f32[368,128]{1,0:T(8,128)S(1)}, u32[]{:S(2)}, u32[]{:S(2)}) collective-permute-start(f32[368,128]{1,0:T(8,128)S(1)} %get-tuple-element.55), channel_id=1, source_target_pairs={{0,16},{16,32},{32,48},{48,64},{64,80},{80,96},{96,112},{112,0},{1... | collective-permute-start | bytes 565256 | tf_op jit(solution)/shard_map/ppermute | solution.py:619
  19.6 8.9 %collective-permute-start.6 = (f32[40,128]{1,0:T(8,128)S(1)}, f32[40,128]{1,0:T(8,128)S(1)}, u32[]{:S(2)}, u32[]{:S(2)}) collective-permute-start(f32[40,128]{1,0:T(8,128)S(1)} %get-tuple-element.57), channel_id=1, source_target_pairs={{0,16},{16,32},{32,48},{48,64},{64,80},{80,96},{96,112},{112,0},{1... | collective-permute-start | bytes 61448 | tf_op jit(solution)/shard_map/ppermute | solution.py:624
  21.6 7.2 %collective-permute-start.7 = (f32[40,128]{1,0:T(8,128)S(1)}, f32[40,128]{1,0:T(8,128)S(1)}, u32[]{:S(2)}, u32[]{:S(2)}) collective-permute-start(f32[40,128]{1,0:T(8,128)S(1)} %get-tuple-element.58), channel_id=1, source_target_pairs={{0,112},{16,0},{32,16},{48,32},{64,48},{80,64},{96,80},{112,96},{1... | collective-permute-start | bytes 61448 | tf_op jit(solution)/shard_map/ppermute | solution.py:625
  30.9 4.8 %collective-permute-start.8 = (f32[4,32,128]{2,1,0:T(8,128)S(1)}, f32[4,32,128]{2,1,0:T(8,128)S(1)}, u32[]{:S(2)}, u32[]{:S(2)}) collective-permute-start(f32[4,32,128]{2,1,0:T(8,128)S(1)} %get-tuple-element.60), channel_id=1, source_target_pairs={{0,32},{16,48},{32,0},{48,16},{64,96},{80,112},{96,64},{112,80},{1... | collective-permute-start | bytes 196616 | tf_op jit(solution)/shard_map/ppermute | solution.py:637
  31.0 6.7 %collective-permute-start.9 = (f32[4,32,128]{2,1,0:T(8,128)S(1)}, f32[4,32,128]{2,1,0:T(8,128)S(1)}, u32[]{:S(2)}, u32[]{:S(2)}) collective-permute-start(f32[4,32,128]{2,1,0:T(8,128)S(1)} %get-tuple-element.61), channel_id=1, source_target_pairs={{0,64},{16,80},{32,96},{48,112},{64,0},{80,16},{96,32},{112,48},{1... | collective-permute-start | bytes 196616 | tf_op jit(solution)/shard_map/ppermute | solution.py:637
  34.7 5.5 %collective-permute-start.10 = (f32[4,32,128]{2,1,0:T(8,128)S(1)}, f32[4,32,128]{2,1,0:T(8,128)S(1)}, u32[]{:S(2)}, u32[]{:S(2)}) collective-permute-start(f32[4,32,128]{2,1,0:T(8,128)S(1)} %get-tuple-element.62), channel_id=1, source_target_pairs={{0,96},{16,112},{32,64},{48,80},{64,32},{80,48},{96,0},{112,16},{1... | collective-permute-start | bytes 196616 | tf_op jit(solution)/shard_map/ppermute | solution.py:637
  40.2 5.5 %collective-permute-start.11 = (f32[2,32,128]{2,1,0:T(8,128)S(1)}, f32[2,32,128]{2,1,0:T(8,128)S(1)}, u32[]{:S(2)}, u32[]{:S(2)}) collective-permute-start(f32[2,32,128]{2,1,0:T(8,128)S(1)} %get-tuple-element.64), channel_id=1, source_target_pairs={{0,16},{16,0},{32,48},{48,32},{64,80},{80,64},{96,112},{112,96},{1... | collective-permute-start | bytes 98312 | tf_op jit(solution)/shard_map/ppermute | solution.py:639

commit v5 on v4

--- a/solution.py
+++ b/solution.py
@@ -23,6 +23,9 @@
 
 def face_rows(faces, rows):
     return ROWS * len(faces) + 8 * ((len(rows) + 3) // 4)
+
+
+FACE_ROWS = max(face_rows(UP_FACES, UP_ROWS), face_rows(DOWN_FACES, DOWN_ROWS))
 
 
 def lanes(rows=8):
@@ -100,7 +103,13 @@
             yb[at : at + 8] = jnp.where(even, down, up)
 
 
-def strip_kernel(start, f, strips, right_out, left_out, factors):
+def strip_kernel(start, pml, f, strips, right_out, left_out, factors, rr, ss, xr, xs):
+    of_plane = block_sigma(pml)
+    for idx in range(1, PLANES + 3):
+        sigma, inside = of_plane(idx - 2)
+        rr[idx], ss[idx] = damping(sigma, inside), 0.5 * sigma
+    sigma, inside = side_sigma(pml)
+    xr[...], xs[...] = damping(sigma, inside), 0.5 * sigma
     for k in range(2):
         phase = jnp.full((8, COLS), lax.rem(start[0] + k + 1, PERIOD), jnp.int32).astype(F32)
         factors[k] = jnp.sin(phase * (2.0 * math.pi / PERIOD))
@@ -151,9 +160,9 @@
     return jnp.where(inside, 1.0 / (1.0 + 0.25 * sigma), 0.0)
 
 
-def electric_coefficients(sigma, inside, permittivity):
-    permittivity = jnp.maximum(permittivity, 1.0)
-    return jnp.where(inside, 1.0 / (2.0 * permittivity + 0.5 * sigma), 0.0), 2.0 * permittivity - 0.5 * sigma
+def electric_coefficients(r, half_sigma, permittivity):
+    twice = 2.0 * jnp.maximum(permittivity, 1.0)
+    return jnp.where(r > 0.0, 1.0 / (twice + half_sigma), 0.0), twice - half_sigma
 
 
 def block_sigma(pml):
@@ -201,16 +210,17 @@
     )
 
 
-def face_out(out, faces, rows, values):
-    for i, item in enumerate(faces):
-        out[ROWS * i : ROWS * i + ROWS] = values[item][0:ROWS]
+def face_blocks(faces, rows, values):
+    blocks = [values[item][0:ROWS] for item in faces]
     sub = subs()
     for i in range(0, len(rows), 4):
         tile = jnp.zeros((8, COLS), F32)
         for j, (kind, k, first) in enumerate(rows[i : i + 4]):
             tile = jnp.where((sub >> 1) == j, turn(values[kind, k][ROWS:TALL], 2 * j - first, 0), tile)
-        at = ROWS * len(faces) + 2 * i
-        out[at : at + 8] = tile
+        blocks.append(tile)
+    whole = jnp.concatenate(blocks, axis=0)
+    fill = FACE_ROWS - whole.shape[0]
+    return jnp.concatenate([whole, jnp.zeros((fill, COLS), F32)], axis=0) if fill else whole
 
 
 def face_in(ref, faces, rows, keep):
@@ -256,11 +266,10 @@
         xb[a, ROWS:TALL] = jnp.where(even, left[a], right[a])
 
 
-def face_kernel(pml, f, tiles, factors, zu, zd):
+def face_kernel(f, tiles, factors, rr, ss, za, zb):
     def field(k, p):
         return jnp.concatenate([f[k, p + 2, 0:ROWS], tiles[k, p]], axis=0)
 
-    of_plane = block_sigma(pml)
     zero = jnp.zeros((TALL, COLS), F32)
     drive = jnp.concatenate([factors[0]] * (TALL // 8), axis=0) * field(13, 7)
 
@@ -274,12 +283,13 @@
         up = [field(base + c, p + 1) for c in range(2)] if p < 7 else [zero, zero]
         return magnetic(
             *[field(base + c, p) for c in range(3)], *up, *[field(base + 3 + c, p) for c in range(3)],
-            damping(*of_plane(p)), next_x, up_row,
+            rr[p + 2], next_x, up_row,
         )
 
-    for out, p, faces, rows in ((zu, 7, UP_FACES, UP_ROWS), (zd, 0, DOWN_FACES, DOWN_ROWS)):
+    sent = []
+    for p, faces, rows in ((7, UP_FACES, UP_ROWS), (0, DOWN_FACES, DOWN_ROWS)):
         values = {("f", k): field(k, p) for k in (0, 1, 6, 7, 12)}
-        q, g = electric_coefficients(*of_plane(p), values["f", 12])
+        q, g = electric_coefficients(rr[p + 2], ss[p + 2], values["f", 12])
         for base in (0, 6):
             h = half_step(base, p)
             down = half_step(base, 6)[0:2] if p == 7 else [zero, zero]
@@ -289,10 +299,13 @@
             for c in range(3):
                 values["h", base + 3 + c] = h[c]
                 values["e", base + c] = e[c]
-        face_out(out, faces, rows, values)
-
-
-def third_kernel(pml, xa, xb, strips, strips_rim, factors, sides, rim_up, rim_down):
+        sent.append(face_blocks(faces, rows, values))
+    even = parity("gz")
+    za[...] = jnp.where(even, sent[0], sent[1])
+    zb[...] = jnp.where(even, sent[1], sent[0])
+
+
+def third_kernel(xa, xb, strips, strips_rim, factors, xr, xs, sides, rim_a, rim_b):
     index = lax.axis_index("gx")
     even = parity("gx")
     has_after = (index < lax.axis_size("gx") - 1).astype(F32)
@@ -312,9 +325,8 @@
         value = jnp.where(own, value, 0.0)
         sides[k] = value
         side.append(value)
-    sigma, inside = side_sigma(pml)
-    r = damping(sigma, inside)
-    q, g = electric_coefficients(sigma, inside, side[12])
+    r = xr[...]
+    q, g = electric_coefficients(r, xs[...], side[12])
     drive = jnp.concatenate([factors[0]] * (TALL // 8), axis=0) * side[13]
     values = {("f", k): side[k] for k in range(COMPS)}
     for base in (0, 6):
@@ -324,11 +336,15 @@
         for c in range(3):
             values["h", base + 3 + c] = h[c]
             values["e", base + c] = e[c]
-    for out, items, p in ((rim_up, UP_SIDES, 7), (rim_down, DOWN_SIDES, 0)):
+    sent = []
+    for items, p in ((UP_SIDES, 7), (DOWN_SIDES, 0)):
         packed = jnp.zeros((TALL, COLS), F32)
         for i, item in enumerate(items):
             packed = jnp.where((lane >> 3) == i, turn(values[item], 8 * i - 8 * (p + 2), 1), packed)
-        out[...] = packed
+        sent.append(packed)
+    even = parity("gz")
+    rim_a[...] = jnp.where(even, sent[0], sent[1])
+    rim_b[...] = jnp.where(even, sent[1], sent[0])
 
 
 def home(layer):
@@ -336,10 +352,9 @@
     return (((layer >> 2) ^ mine) << 2) + (layer & 3)
 
 
-def run_steps(pml, factors, layer, f, one, rr, qq, gg, xf, xone, planes, sums, put, halo=None):
-    sigma, inside = side_sigma(pml)
-    xr = damping(sigma, inside)
-    xq, xg = electric_coefficients(sigma, inside, xf[12])
+def run_steps(side_loss, factors, f, one, rr, qq, gg, xf, xone, planes, put_field, put_density, halo=None):
+    xr = side_loss[0][...]
+    xq, xg = electric_coefficients(xr, side_loss[1][...], xf[12])
     factors = [jnp.concatenate([factors[k]] * (TALL // 8), axis=0) for k in range(2)]
     lane = lanes(TALL)
     first_lane, last_lane = lane == 0, lane == COLS - 1
@@ -420,44 +435,46 @@
         density = jnp.zeros((ROWS, COLS), F32)
         for c in range(3):
             last = zero[c][0:ROWS]
-            put(c, idx, last, f[9 + c, idx, 0:ROWS])
+            put_field(c, idx, last, f[9 + c, idx, 0:ROWS])
             density = density + f[c, idx, 0:ROWS] * last + one[c, idx, 0:ROWS] * one[3 + c, idx, 0:ROWS]
             density = density + two[c][0:ROWS] * f[6 + c, idx, 0:ROWS]
-        sums[home(layer[idx - 2])] = density
+        put_density(idx, density)
 
     over(3, body)
 
 
-def inner_kernel(layer, pml, factors, own, tiles, sides, f, one, rr, qq, gg, sums, e_mid, h_mid, xf, xone):
+def inner_kernel(layer, factors, rr, ss, xr, xs, own, tiles, sides, f, one, qq, gg, sums, e_mid, h_mid, homes, xf, xone):
     del own
     for k in range(COMPS):
         for p in range(PLANES):
             f[k, p + 2, ROWS:TALL] = tiles[k, p]
         xf[k] = sides[k]
-    of_plane = block_sigma(pml)
 
     def coefficients(i, carry):
-        sigma, inside = of_plane(i)
-        rr[i + 2] = damping(sigma, inside)
-        qq[i + 2], gg[i + 2] = electric_coefficients(sigma, inside, f[12, i + 2])
+        qq[i + 2], gg[i + 2] = electric_coefficients(rr[i + 2], ss[i + 2], f[12, i + 2])
         return carry
 
     lax.fori_loop(0, PLANES, coefficients, 0)
     sums[...] = jnp.zeros((LAYERS, ROWS, COLS), F32)
+    for i, p in enumerate((0, 1, 6, 7)):
+        homes[i] = jnp.full((8, COLS), home(layer[p]), jnp.int32).astype(F32)
 
     def put(c, idx, e_new, h_new):
         e_mid[c, idx - 4] = e_new
         h_mid[c, idx - 4] = h_new
 
+    def put_density(idx, density):
+        sums[home(layer[idx - 2])] = density
+
     planes = [range(2, 9), range(3, 9), range(3, 8), range(4, 8)]
-    run_steps(pml, factors, layer, f, one, rr, qq, gg, xf, xone, planes, sums, put)
+    run_steps((xr, xs), factors, f, one, rr, qq, gg, xf, xone, planes, put, put_density)
 
 
 def outer_kernel(
-    layer, pml, factors, f_in, one_in, rr_in, qq_in, gg_in, sums_in, zu, zd, sides, rim_up, rim_down,
-    f, one, rr, qq, gg, sums, e_rest, h_rest, first, second, third, xf, xone,
+    factors, rr, ss, xr, xs, f_in, one_in, qq_in, gg_in, sums, homes, za, zb, sides, rim_a, rim_b,
+    f, one, qq, gg, e_rest, h_rest, zeroth, first, second, third, xf, xone,
 ):
-    del f_in, one_in, rr_in, qq_in, gg_in, sums_in
+    del f_in, one_in, qq_in, gg_in
     index = lax.axis_index("gz")
     has_above = (index < lax.axis_size("gz") - 1).astype(F32)
     has_below = (index > 0).astype(F32)
@@ -466,11 +483,13 @@
     for k in range(COMPS):
         xf[k] = sides[k]
     got = {}
-    for ref, faces, rows, rim, items, idx, keep in (
-        (zu, UP_FACES, UP_ROWS, rim_up, UP_SIDES, low, has_below),
-        (zd, DOWN_FACES, DOWN_ROWS, rim_down, DOWN_SIDES, top, has_above),
+    even = parity("gz")
+    for pick, faces, rows, items, idx, keep in (
+        (lambda a, b: jnp.where(even, b, a), UP_FACES, UP_ROWS, UP_SIDES, low, has_below),
+        (lambda a, b: jnp.where(even, a, b), DOWN_FACES, DOWN_ROWS, DOWN_SIDES, top, has_above),
     ):
-        packed = rim[...] * keep
+        ref = pick(za[...], zb[...])
+        packed = pick(rim_a[...], rim_b[...]) * keep
         planes = face_in(ref, faces, rows, keep)
         for i, (kind, k) in enumerate(items):
             if kind != "f":
@@ -482,11 +501,8 @@
             if ("f", k) in planes:
                 f[k, idx] = planes["f", k]
                 xf[k] = jnp.where((lane >> 3) == idx, got["f", k, idx][1], xf[k])
-    of_plane = block_sigma(pml)
     for idx in (low, top):
-        sigma, inside = of_plane(idx - 2)
-        rr[idx] = damping(sigma, inside)
-        qq[idx], gg[idx] = electric_coefficients(sigma, inside, f[12, idx])
+        qq[idx], gg[idx] = electric_coefficients(rr[idx], ss[idx], f[12, idx])
 
     def add_z(q, x, y, prev_x):
         return q * ((y - prev_x(y)) - (x - down_row(x, 0)))
@@ -525,10 +541,20 @@
         e_rest[c, at] = e_new
         h_rest[c, at] = h_new
 
+    late = []
+
+    def put_density(idx, density):
+        late.append(density)
+
     planes = [(9,), (2, 9), (1, 2, 8, 9), (2, 3, 8, 9)]
-    run_steps(pml, factors, layer, f, one, rr, qq, gg, xf, xone, planes, sums, put, halo)
-    for i, out in enumerate((first, second, third)):
-        out[...] = sums[4 * i + 4 : 4 * i + 8]
+    run_steps((xr, xs), factors, f, one, rr, qq, gg, xf, xone, planes, put, put_density, halo)
+    for i, out in enumerate((zeroth, first, second, third)):
+        for j in range(4):
+            total = sums[4 * i + j]
+            for at, density in enumerate(late):
+                here = homes[at] == float(4 * i + j)
+                total = total + jnp.where(jnp.concatenate([here] * (ROWS // 8), axis=0), density, 0.0)
+            out[j] = total
 
 
 def store_kernel(e_mid, h_mid, e_rest, h_rest, e_out, h_out, sems):
@@ -575,11 +601,6 @@
     return run
 
 
-def ring(axis, step):
-    count = lax.axis_size(axis)
-    return [(i, (i + step) % count) for i in range(count)]
-
-
 def swaps(axis, first):
     count = lax.axis_size(axis)
     pairs = [(i, (i + 1) % count) for i in range(first, count, 2)]
@@ -609,33 +630,34 @@
     )(*raw)
     yb = lax.ppermute(yb, ("gy", "gx"), inner_swaps())
     ya = lax.ppermute(ya, "gy", swaps("gy", 0))
-    strips, right, left, factors = call(
-        strip_kernel, [(COMPS,) + block, (2,) + block, (2,) + block, (2, 8, COLS)], scalars=1
-    )(start_step, f)
+    strips, right, left, *loss = call(
+        strip_kernel, [(COMPS,) + block, (2,) + block, (2,) + block, (2, 8, COLS), deep, deep, tall, tall], scalars=2
+    )(start_step, pml_cells, f)
     side = (2,) + tall
     tiles, strips_rim, xa, xb = call(second_kernel, [(COMPS, PLANES, 8, COLS), (COMPS, 8, COLS), side, side])(ya, yb, right, left)
-    sizes = [(face_rows(*lists), COLS) for lists in ((UP_FACES, UP_ROWS), (DOWN_FACES, DOWN_ROWS))]
-    zu, zd = call(face_kernel, sizes, scalars=1)(pml_cells, f, tiles, factors)
-    zu = lax.ppermute(zu, "gz", ring("gz", 1))
-    zd = lax.ppermute(zd, "gz", ring("gz", -1))
+    za, zb = call(face_kernel, [(FACE_ROWS, COLS)] * 2)(f, tiles, *loss[:3])
+    za = lax.ppermute(za, "gz", swaps("gz", 0))
+    zb = lax.ppermute(zb, "gz", swaps("gz", 1))
     xa = lax.ppermute(xa, "gx", swaps("gx", 0))
     xb = lax.ppermute(xb, "gx", swaps("gx", 1))
-    sides, rim_up, rim_down = call(third_kernel, [(COMPS,) + tall, tall, tall], scalars=1)(pml_cells, xa, xb, strips, strips_rim, factors)
-    rim_up = lax.ppermute(rim_up, "gz", ring("gz", 1))
-    rim_down = lax.ppermute(rim_down, "gz", ring("gz", -1))
-    state = [(COMPS,) + deep, (6,) + deep, deep, deep, deep, (LAYERS,) + block]
+    sides, rim_a, rim_b = call(third_kernel, [(COMPS,) + tall, tall, tall])(
+        xa, xb, strips, strips_rim, loss[0], *loss[3:]
+    )
+    rim_a = lax.ppermute(rim_a, "gz", swaps("gz", 0))
+    rim_b = lax.ppermute(rim_b, "gz", swaps("gz", 1))
+    state = [(COMPS,) + deep, (6,) + deep, deep, deep]
     mid, out = (3, PLANES // 2) + block, (3, PLANES) + block
     side = [(COMPS,) + tall, (6,) + tall]
-    *held, e_mid, h_mid = call(inner_kernel, state + [mid, mid], side, scalars=2, aliases={3: 0}, flops=10**11)(
-        layer_of_cell, pml_cells, factors, f, tiles, sides
+    *held, sums, e_mid, h_mid, homes = call(inner_kernel, state + [(LAYERS,) + block, mid, mid, (4, 8, COLS)], side, scalars=1, aliases={6: 0}, flops=10**11)(
+        layer_of_cell, *loss, f, tiles, sides
     )
     quarter, pair = (LAYERS // 4,) + block, (2,) + block
-    *_, sums, e_rest, h_rest, first, second, third = call(
-        outer_kernel, state + [mid, mid, quarter, quarter, quarter], side, scalars=2, aliases={3 + i: i for i in range(len(state))}
-    )(layer_of_cell, pml_cells, factors, *held, zu, zd, sides, rim_up, rim_down)
+    *_, e_rest, h_rest, zeroth, first, second, third = call(
+        outer_kernel, state + [mid, mid] + [quarter] * 4, side, aliases={5 + i: i for i in range(len(state))}
+    )(*loss, *held, sums, homes, za, zb, sides, rim_a, rim_b)
     e_out, h_out = call(store_kernel, [out, out], [pltpu.SemaphoreType.DMA((6,))], out_space=pltpu.HBM)(e_mid, h_mid, e_rest, h_rest)
     first, second, third = (lax.ppermute(v, "gz", across("gz", m)) for v, m in ((first, 2), (second, 4), (third, 6)))
-    kept, sent = call(fold_kernel, [pair, pair])(sums, first, second, third)
+    kept, sent = call(fold_kernel, [pair, pair])(zeroth, first, second, third)
     (gradient,) = call(sum_kernel, [pair])(kept, lax.ppermute(sent, "gz", across("gz", 1)))
     return gradient, e_out, h_out
 

time: 46.5 us -> 43.3 us (0.931)
  starting transfers between devices: 24.7 us -> 23.2 us
  Pallas kernels: 10.4 us -> 9.03 us
  waiting for transfers between devices: 9.86 us -> 8.92 us
  local copies, waits for them, and re-layouts: 0.01 us -> 0.65 us
    ppermute x4, waiting for transfers between devices: 1.11 us -> 3.59 us  [the longest x1 2.67 us: local(): rim_b = lax.ppermute(rim_b, 'gz', swaps('gz', 1))]
    ppermute x4, starting transfers between devices: 12.2 us -> 10.3 us  [the longest x1 3.96 us: local(): za = lax.ppermute(za, 'gz', swaps('gz', 0))]
    ppermute x3, waiting for transfers between devices: 4.54 us -> 2.69 us  [local(): lax.ppermute(v, 'gz', across('gz', m))]
    pallas_call x10, Pallas kernels: 10.4 us -> 9.03 us  [run(): pl.pallas_call(kernel, out_shape=[jax.ShapeDtypeStruct(s, F32) for s in o...]
    ppermute x1, waiting for transfers between devices: 1.9 us -> 0.7 us  [local(): yb = lax.ppermute(yb, ('gy', 'gx'), inner_swaps())]
    unnamed x4, local copies, waits for them, and re-layouts: 0.01 us -> 0.65 us
  transfers between devices with their start and end apart: 12 -> 12, of which waited for: 6 -> 6; matrix products, arithmetic and copies ran while one was open for 0% -> 0% of each run, Pallas kernels for 13% -> 12%
where the time goes in v5:
time: 43.3 us; the launch traced here: 43.2 us
  starting transfers between devices  23.2 us (54%)
  Pallas kernels  9.03 us (21%)
  waiting for transfers between devices  8.92 us (21%)
  between operations  1.38 us (3%)
  local copies, waits for them, and re-layouts  0.65 us (2%)
    pallas_call x10, Pallas kernels, run(): pl.pallas_call(kernel, out_shape=[jax.ShapeDtypeStruct(s, F32) for s in o...  9.03 us
    ppermute x3, starting transfers between devices, local(): lax.ppermute(v, 'gz', across('gz', m))  4.78 us
    ppermute x1, starting transfers between devices, local(): za = lax.ppermute(za, 'gz', swaps('gz', 0))  3.96 us
    ppermute x3, waiting for transfers between devices, local(): lax.ppermute(v, 'gz', across('gz', m))  2.69 us
    ppermute x1, waiting for transfers between devices, local(): rim_b = lax.ppermute(rim_b, 'gz', swaps('gz', 1))  2.67 us
    ppermute x1, starting transfers between devices, local(): lax.ppermute(sent, 'gz', across('gz', 1))  2.64 us
    ppermute x1, starting transfers between devices, local(): zb = lax.ppermute(zb, 'gz', swaps('gz', 1))  2.54 us
    ppermute x1, starting transfers between devices, local(): xb = lax.ppermute(xb, 'gx', swaps('gx', 1))  2.1 us
  transfers between devices with their start and end apart: 12, of which 6 were waited for; matrix products, arithmetic and copies ran while one was open for 0% of the time, Pallas kernels for 12%

profile of v5, /device:TPU:0, one launch (start us, length us, event | category | flops | bytes accessed | tf_op | source)
XLA Modules:
  0.0 43.2 jit_solution(12900656384694497184)
XLA Ops:
  0.6 1.6 %shard_map.112 = (f32[14,12,40,128]{3,2,1,0:T(8,128)S(1)}, f32[224,128]{1,0:T(8,128)S(1)}, f32[224,128]{1,0:T(8,128)S(1)}) custom-call(f32[3,8,32,128]{3,2,1,0:T(8,128)} %e.1, f32[3,8,32,128]{3,2,1,0:T(8,128)} %h.1, f32[3,8,32,128]{3,2,1,0:T(8,128)} %ae.1, f32[3,8,32,128]{3,2,1,0:T(8,128)} %ah.1, f32[8,32,128]{2,1,0:T(8,128)} %eps.1, f32[8,32,128]{2,1,0:T(8,128)} %cur.1), custom_call_target="tpu_custom_call" | custom-call | flops 1000000 | bytes 5505024 | tf_op jit(solution)/shard_map/pallas_call | solution.py:590
  2.3 0.1 collective-permute-start
  2.4 1.7 %collective-permute-start.1 = (f32[224,128]{1,0:T(8,128)S(1)}, f32[224,128]{1,0:T(8,128)S(1)}, u32[]{:S(2)}, u32[]{:S(2)}) collective-permute-start(f32[224,128]{1,0:T(8,128)S(1)} %get-tuple-element.48), channel_id=1, source_target_pairs={{4,8},{0,1},{12,13},{5,9},{6,10},{2,3},{14,15},{7,11},{8,4},{1,0},... | collective-permute-start | bytes 344072 | tf_op jit(solution)/shard_map/ppermute | solution.py:631
  4.7 0.0 copy-start
  4.7 0.6 %copy-done = s32[3]{0:T(128)S(1)} copy-done((s32[3]{0:T(128)S(1)}, s32[3]{0:T(128)}, u32[]{:S(2)}) %copy-start) | copy-done | bytes 36
  5.3 0.0 copy-start.1
  5.3 1.2 %shard_map.113 = (f32[14,32,128]{2,1,0:T(8,128)S(1)}, f32[2,32,128]{2,1,0:T(8,128)S(1)}, f32[2,32,128]{2,1,0:T(8,128)S(1)}, f32[2,8,128]{2,1,0:T(8,128)S(1)}, f3...) custom-call(s32[1]{0:T(128)S(6)} %copy.22.start, ...), custom_call_target="tpu_custom_call" | custom-call | flops 1000000 | bytes 4276240 | tf_op jit(solution)/shard_map/pallas_call | solution.py:590
  6.5 0.0 collective-permute-done.ya
  6.5 0.7 %collective-permute-done.1.yb = f32[224,128]{1,0:T(8,128)S(1)} collective-permute-done((f32[224,128]{1,0:T(8,128)S(1)}, f32[224,128]{1,0:T(8,128)S(1)}, u32[]{:S(2)}, u32[]{:S(2)}) %collective-permute-start.1) | collective-permute-done | bytes 114720 | tf_op jit(solution)/shard_map/ppermute | solution.py:631
  7.3 0.3 shard_map.114
  7.5 1.7 %collective-permute-start.2 = (f32[2,40,128]{2,1,0:T(8,128)S(1)}, f32[2,40,128]{2,1,0:T(8,128)S(1)}, u32[]{:S(2)}, u32[]{:S(2)}) collective-permute-start(f32[2,40,128]{2,1,0:T(8,128)S(1)} %get-tuple-element.52), channel_id=1, source_target_pairs={{0,1},{2,3},{1,0},{3,2},{4,5},{6,7},{5,4},{7,6},{8,9},{10,11},{9,8... | collective-permute-start | bytes 122888 | tf_op jit(solution)/shard_map/ppermute | solution.py:641
  9.2 2.1 %collective-permute-start.3 = (f32[2,40,128]{2,1,0:T(8,128)S(1)}, f32[2,40,128]{2,1,0:T(8,128)S(1)}, u32[]{:S(2)}, u32[]{:S(2)}) collective-permute-start(f32[2,40,128]{2,1,0:T(8,128)S(1)} %get-tuple-element.53), channel_id=1, source_target_pairs={{1,2},{3,0},{2,1},{0,3},{5,6},{7,4},{6,5},{4,7},{9,10},{11,8},{10,... | collective-permute-start | bytes 122888 | tf_op jit(solution)/shard_map/ppermute | solution.py:642
  11.3 0.2 shard_map.117
  11.5 4.0 %collective-permute-start.4 = (f32[368,128]{1,0:T(8,128)S(1)}, f32[368,128]{1,0:T(8,128)S(1)}, u32[]{:S(2)}, u32[]{:S(2)}) collective-permute-start(f32[368,128]{1,0:T(8,128)S(1)} %get-tuple-element.63), channel_id=1, source_target_pairs={{0,16},{32,48},{64,80},{96,112},{16,0},{48,32},{80,64},{112,96},{1... | collective-permute-start | bytes 565256 | tf_op jit(solution)/shard_map/ppermute | solution.py:639
  15.5 2.5 %collective-permute-start.5 = (f32[368,128]{1,0:T(8,128)S(1)}, f32[368,128]{1,0:T(8,128)S(1)}, u32[]{:S(2)}, u32[]{:S(2)}) collective-permute-start(f32[368,128]{1,0:T(8,128)S(1)} %get-tuple-element.64), channel_id=1, source_target_pairs={{16,32},{48,64},{80,96},{112,0},{32,16},{64,48},{96,80},{0,112},{1... | collective-permute-start | bytes 565256 | tf_op jit(solution)/shard_map/ppermute | solution.py:640
  18.0 0.0 collective-permute-done.2.xa
  18.0 0.0 collective-permute-done.3.xb
  18.0 0.6 %shard_map.115 = (f32[14,40,128]{2,1,0:T(8,128)S(1)}, f32[40,128]{1,0:T(8,128)S(1)}, f32[40,128]{1,0:T(8,128)S(1)}) custom-call(f32[2,40,128]{2,1,0:T(8,128)S(1)} %collective-permute-done.2.xa, f32[2,40,128]{2,1,0:T(8,128)S(1)} %collective-permute-done.3.xb, f32[14,32,128]{2,1,0:T(8,128)S(1)} %get-tuple-element.54.strips, ...), custom_call_target="tpu_custom_call" | custom-call | flops 1000000 | bytes 745472 | tf_op jit(solution)/shard_map/pallas_call | solution.py:590
  18.6 2.1 %collective-permute-start.6 = (f32[40,128]{1,0:T(8,128)S(1)}, f32[40,128]{1,0:T(8,128)S(1)}, u32[]{:S(2)}, u32[]{:S(2)}) collective-permute-start(f32[40,128]{1,0:T(8,128)S(1)} %get-tuple-element.65), channel_id=1, source_target_pairs={{0,16},{32,48},{64,80},{96,112},{16,0},{48,32},{80,64},{112,96},{1... | collective-permute-start | bytes 61448 | tf_op jit(solution)/shard_map/ppermute | solution.py:646
  20.7 1.7 %collective-permute-start.7 = (f32[40,128]{1,0:T(8,128)S(1)}, f32[40,128]{1,0:T(8,128)S(1)}, u32[]{:S(2)}, u32[]{:S(2)}) collective-permute-start(f32[40,128]{1,0:T(8,128)S(1)} %get-tuple-element.66), channel_id=1, source_target_pairs={{16,32},{48,64},{80,96},{112,0},{32,16},{64,48},{96,80},{0,112},{1... | collective-permute-start | bytes 61448 | tf_op jit(solution)/shard_map/ppermute | solution.py:647
  22.4 0.0 copy-done.1
  22.4 2.1 %shard_map.116 = (f32[14,12,40,128]{3,2,1,0:T(8,128)S(1)}, f32[6,12,40,128]{3,2,1,0:T(8,128)S(1)}, f32[12,40,128]{2,1,0:T(8,128)S(1)}, f32[12,40,128]{2,1,0:T(8,...) custom-call(s32[8]{0:T(128)S(1)} %copy-done.1, ...), custom_call_target="tpu_custom_call", output_to_operand_aliasing={{0}: (6, {})} | custom-call | flops 99999997952 | bytes 10805280 | tf_op jit(solution)/shard_map/pallas_call | solution.py:590
  24.5 0.9 %collective-permute-done.6.rim_a = f32[40,128]{1,0:T(8,128)S(1)} collective-permute-done((f32[40,128]{1,0:T(8,128)S(1)}, f32[40,128]{1,0:T(8,128)S(1)}, u32[]{:S(2)}, u32[]{:S(2)}) %collective-permute-start.6) | collective-permute-done | bytes 20512 | tf_op jit(solution)/shard_map/ppermute | solution.py:646
  25.4 2.7 %collective-permute-done.7.rim_b = f32[40,128]{1,0:T(8,128)S(1)} collective-permute-done((f32[40,128]{1,0:T(8,128)S(1)}, f32[40,128]{1,0:T(8,128)S(1)}, u32[]{:S(2)}, u32[]{:S(2)}) %collective-permute-start.7) | collective-permute-done | bytes 20512 | tf_op jit(solution)/shard_map/ppermute | solution.py:647
  28.1 0.0 collective-permute-done.4.za
  28.1 0.0 collective-permute-done.5.zb
  28.1 1.5 %shard_map.118 = (f32[14,12,40,128]{3,2,1,0:T(8,128)S(1)}, f32[6,12,40,128]{3,2,1,0:T(8,128)S(1)}, f32[12,40,128]{2,1,0:T(8,128)S(1)}, f32[12,40,128]{2,1,0:T(8,...) custom-call(f32[2,8,128]{2,1,0:T(8,128)S(1)} %get-tuple-element.42.f, ...), custom_call_target="tpu_custom_call", output_to_operand_aliasing={{0}: (5, {}), {1}: (6, {}), {2}: (7, {}), {3}: (8, {})} | custom-call | flops 1000000 | bytes 12992512 | tf_op jit(solution)/shard_map/pallas_call | solution.py:590
  29.6 0.4 %collective-permute-start.8 = (f32[4,32,128]{2,1,0:T(8,128)S(1)}, f32[4,32,128]{2,1,0:T(8,128)S(1)}, u32[]{:S(2)}, u32[]{:S(2)}) collective-permute-start(f32[4,32,128]{2,1,0:T(8,128)S(1)} %get-tuple-element.68), channel_id=1, source_target_pairs={{0,32},{16,48},{32,0},{48,16},{64,96},{80,112},{96,64},{112,80},{1... | collective-permute-start | bytes 196616 | tf_op jit(solution)/shard_map/ppermute | solution.py:659
  30.0 1.5 %collective-permute-start.9 = (f32[4,32,128]{2,1,0:T(8,128)S(1)}, f32[4,32,128]{2,1,0:T(8,128)S(1)}, u32[]{:S(2)}, u32[]{:S(2)}) collective-permute-start(f32[4,32,128]{2,1,0:T(8,128)S(1)} %get-tuple-element.69), channel_id=1, source_target_pairs={{0,64},{16,80},{32,96},{48,112},{64,0},{80,16},{96,32},{112,48},{1... | collective-permute-start | bytes 196616 | tf_op jit(solution)/shard_map/ppermute | solution.py:659
  31.6 2.8 %collective-permute-start.10 = (f32[4,32,128]{2,1,0:T(8,128)S(1)}, f32[4,32,128]{2,1,0:T(8,128)S(1)}, u32[]{:S(2)}, u32[]{:S(2)}) collective-permute-start(f32[4,32,128]{2,1,0:T(8,128)S(1)} %get-tuple-element.70), channel_id=1, source_target_pairs={{0,96},{16,112},{32,64},{48,80},{64,32},{80,48},{96,0},{112,16},{1... | collective-permute-start | bytes 196616 | tf_op jit(solution)/shard_map/ppermute | solution.py:659
  34.4 0.0 collective-permute-done.8.first
  34.4 1.4 %collective-permute-done.9.second = f32[4,32,128]{2,1,0:T(8,128)S(1)} collective-permute-done((f32[4,32,128]{2,1,0:T(8,128)S(1)}, f32[4,32,128]{2,1,0:T(8,128)S(1)}, u32[]{:S(2)}, u32[]{:S(2)}) %collective-permute-start.9) | collective-permute-done | bytes 65568 | tf_op jit(solution)/shard_map/ppermute | solution.py:659
  35.8 1.3 %collective-permute-done.10.third = f32[4,32,128]{2,1,0:T(8,128)S(1)} collective-permute-done((f32[4,32,128]{2,1,0:T(8,128)S(1)}, f32[4,32,128]{2,1,0:T(8,128)S(1)}, u32[]{:S(2)}, u32[]{:S(2)}) %collective-permute-start.10) | collective-permute-done | bytes 65568 | tf_op jit(solution)/shard_map/ppermute | solution.py:659
  37.1 2.6 %collective-permute-start.11 = (f32[2,32,128]{2,1,0:T(8,128)S(1)}, f32[2,32,128]{2,1,0:T(8,128)S(1)}, u32[]{:S(2)}, u32[]{:S(2)}) collective-permute-start(f32[2,32,128]{2,1,0:T(8,128)S(1)} %get-tuple-element.72), channel_id=1, source_target_pairs={{0,16},{16,0},{32,48},{48,32},{64,80},{80,64},{96,112},{112,96},{1... | collective-permute-start | bytes 98312 | tf_op jit(solution)/shard_map/ppermute | solution.py:661
  39.7 0.9 %shard_map.121 = (f32[3,8,32,128]{3,2,1,0:T(8,128)}, f32[3,8,32,128]{3,2,1,0:T(8,128)}) custom-call(f32[3,4,32,128]{3,2,1,0:T(8,128)S(1)} %get-tuple-element.73.e_mid, f32[3,4,32,128]{3,2,1,0:T(8,128)S(1)} %get-tuple-element.74.h_mid, f32[3,4,32,128]{3,2,1,0:T(8,128)S(1)} %get-tuple-element.75.e_rest, f32[3,4,32,128]{3,2,1,0:T(8,128)S(1)} %get-tuple-element.76.h_rest), custom_call_target="tpu_custom_call" | custom-call | flops 1000000 | bytes 1572864 | tf_op jit(solution)/shard_map/pallas_call | solution.py:590
  40.6 1.9 %collective-permute-done.11.got = f32[2,32,128]{2,1,0:T(8,128)S(1)} collective-permute-done((f32[2,32,128]{2,1,0:T(8,128)S(1)}, f32[2,32,128]{2,1,0:T(8,128)S(1)}, u32[]{:S(2)}, u32[]{:S(2)}) %collective-permute-start.11) | collective-permute-done | bytes 32800 | tf_op jit(solution)/shard_map/ppermute | solution.py:661
  42.6 0.6 %shard_map.120 = f32[2,32,128]{2,1,0:T(8,128)} custom-call(f32[2,32,128]{2,1,0:T(8,128)S(1)} %get-tuple-element.71.kept, f32[2,32,128]{2,1,0:T(8,128)S(1)} %collective-permute-done.11.got), custom_call_target="tpu_custom_call" | custom-call | flops 1000000 | bytes 98304 | tf_op jit(solution)/shard_map/pallas_call | solution.py:590
  (1 shorter events, 0.0 us)
Async XLA Ops:
  2.3 4.3 %collective-permute-start = (f32[224,128]{1,0:T(8,128)S(1)}, f32[224,128]{1,0:T(8,128)S(1)}, u32[]{:S(2)}, u32[]{:S(2)}) collective-permute-start(f32[224,128]{1,0:T(8,128)S(1)} %get-tuple-element.47), channel_id=1, source_target_pairs={{0,4},{8,12},{4,0},{12,8},{1,5},{9,13},{5,1},{13,9},{2,6},{10,14},... | collective-permute-start | bytes 344072 | tf_op jit(solution)/shard_map/ppermute | solution.py:632
  2.4 4.9 %collective-permute-start.1 = (f32[224,128]{1,0:T(8,128)S(1)}, f32[224,128]{1,0:T(8,128)S(1)}, u32[]{:S(2)}, u32[]{:S(2)}) collective-permute-start(f32[224,128]{1,0:T(8,128)S(1)} %get-tuple-element.48), channel_id=1, source_target_pairs={{4,8},{0,1},{12,13},{5,9},{6,10},{2,3},{14,15},{7,11},{8,4},{1,0},... | collective-permute-start | bytes 344072 | tf_op jit(solution)/shard_map/ppermute | solution.py:631
  4.7 0.7 %copy-start = (s32[3]{0:T(128)S(1)}, s32[3]{0:T(128)}, u32[]{:S(2)}) copy-start(s32[3]{0:T(128)} %pml.1) | copy-start | bytes 40
  5.3 17.1 %copy-start.1 = (s32[8]{0:T(128)S(1)}, s32[8]{0:T(128)}, u32[]{:S(2)}) copy-start(s32[8]{0:T(128)} %layer.1) | copy-start | bytes 100
  7.5 10.5 %collective-permute-start.2 = (f32[2,40,128]{2,1,0:T(8,128)S(1)}, f32[2,40,128]{2,1,0:T(8,128)S(1)}, u32[]{:S(2)}, u32[]{:S(2)}) collective-permute-start(f32[2,40,128]{2,1,0:T(8,128)S(1)} %get-tuple-element.52), channel_id=1, source_target_pairs={{0,1},{2,3},{1,0},{3,2},{4,5},{6,7},{5,4},{7,6},{8,9},{10,11},{9,8... | collective-permute-start | bytes 122888 | tf_op jit(solution)/shard_map/ppermute | solution.py:641
  9.2 8.8 %collective-permute-start.3 = (f32[2,40,128]{2,1,0:T(8,128)S(1)}, f32[2,40,128]{2,1,0:T(8,128)S(1)}, u32[]{:S(2)}, u32[]{:S(2)}) collective-permute-start(f32[2,40,128]{2,1,0:T(8,128)S(1)} %get-tuple-element.53), channel_id=1, source_target_pairs={{1,2},{3,0},{2,1},{0,3},{5,6},{7,4},{6,5},{4,7},{9,10},{11,8},{10,... | collective-permute-start | bytes 122888 | tf_op jit(solution)/shard_map/ppermute | solution.py:642
  11.5 16.6 %collective-permute-start.4 = (f32[368,128]{1,0:T(8,128)S(1)}, f32[368,128]{1,0:T(8,128)S(1)}, u32[]{:S(2)}, u32[]{:S(2)}) collective-permute-start(f32[368,128]{1,0:T(8,128)S(1)} %get-tuple-element.63), channel_id=1, source_target_pairs={{0,16},{32,48},{64,80},{96,112},{16,0},{48,32},{80,64},{112,96},{1... | collective-permute-start | bytes 565256 | tf_op jit(solution)/shard_map/ppermute | solution.py:639
  15.5 12.6 %collective-permute-start.5 = (f32[368,128]{1,0:T(8,128)S(1)}, f32[368,128]{1,0:T(8,128)S(1)}, u32[]{:S(2)}, u32[]{:S(2)}) collective-permute-start(f32[368,128]{1,0:T(8,128)S(1)} %get-tuple-element.64), channel_id=1, source_target_pairs={{16,32},{48,64},{80,96},{112,0},{32,16},{64,48},{96,80},{0,112},{1... | collective-permute-start | bytes 565256 | tf_op jit(solution)/shard_map/ppermute | solution.py:640
  18.6 6.8 %collective-permute-start.6 = (f32[40,128]{1,0:T(8,128)S(1)}, f32[40,128]{1,0:T(8,128)S(1)}, u32[]{:S(2)}, u32[]{:S(2)}) collective-permute-start(f32[40,128]{1,0:T(8,128)S(1)} %get-tuple-element.65), channel_id=1, source_target_pairs={{0,16},{32,48},{64,80},{96,112},{16,0},{48,32},{80,64},{112,96},{1... | collective-permute-start | bytes 61448 | tf_op jit(solution)/shard_map/ppermute | solution.py:646
  20.7 7.4 %collective-permute-start.7 = (f32[40,128]{1,0:T(8,128)S(1)}, f32[40,128]{1,0:T(8,128)S(1)}, u32[]{:S(2)}, u32[]{:S(2)}) collective-permute-start(f32[40,128]{1,0:T(8,128)S(1)} %get-tuple-element.66), channel_id=1, source_target_pairs={{16,32},{48,64},{80,96},{112,0},{32,16},{64,48},{96,80},{0,112},{1... | collective-permute-start | bytes 61448 | tf_op jit(solution)/shard_map/ppermute | solution.py:647
  29.6 4.8 %collective-permute-start.8 = (f32[4,32,128]{2,1,0:T(8,128)S(1)}, f32[4,32,128]{2,1,0:T(8,128)S(1)}, u32[]{:S(2)}, u32[]{:S(2)}) collective-permute-start(f32[4,32,128]{2,1,0:T(8,128)S(1)} %get-tuple-element.68), channel_id=1, source_target_pairs={{0,32},{16,48},{32,0},{48,16},{64,96},{80,112},{96,64},{112,80},{1... | collective-permute-start | bytes 196616 | tf_op jit(solution)/shard_map/ppermute | solution.py:659
  30.0 5.8 %collective-permute-start.9 = (f32[4,32,128]{2,1,0:T(8,128)S(1)}, f32[4,32,128]{2,1,0:T(8,128)S(1)}, u32[]{:S(2)}, u32[]{:S(2)}) collective-permute-start(f32[4,32,128]{2,1,0:T(8,128)S(1)} %get-tuple-element.69), channel_id=1, source_target_pairs={{0,64},{16,80},{32,96},{48,112},{64,0},{80,16},{96,32},{112,48},{1... | collective-permute-start | bytes 196616 | tf_op jit(solution)/shard_map/ppermute | solution.py:659
  31.6 5.5 %collective-permute-start.10 = (f32[4,32,128]{2,1,0:T(8,128)S(1)}, f32[4,32,128]{2,1,0:T(8,128)S(1)}, u32[]{:S(2)}, u32[]{:S(2)}) collective-permute-start(f32[4,32,128]{2,1,0:T(8,128)S(1)} %get-tuple-element.70), channel_id=1, source_target_pairs={{0,96},{16,112},{32,64},{48,80},{64,32},{80,48},{96,0},{112,16},{1... | collective-permute-start | bytes 196616 | tf_op jit(solution)/shard_map/ppermute | solution.py:659
  37.1 5.5 %collective-permute-start.11 = (f32[2,32,128]{2,1,0:T(8,128)S(1)}, f32[2,32,128]{2,1,0:T(8,128)S(1)}, u32[]{:S(2)}, u32[]{:S(2)}) collective-permute-start(f32[2,32,128]{2,1,0:T(8,128)S(1)} %get-tuple-element.72), channel_id=1, source_target_pairs={{0,16},{16,0},{32,48},{48,32},{64,80},{80,64},{96,112},{112,96},{1... | collective-permute-start | bytes 98312 | tf_op jit(solution)/shard_map/ppermute | solution.py:661

commit v6 on v5

--- a/solution.py
+++ b/solution.py
@@ -236,7 +236,7 @@
     return {item: jnp.concatenate(parts, axis=0) for item, parts in got.items()}
 
 
-def second_kernel(ya, yb, right_in, left_in, tiles, strips, xa, xb):
+def second_kernel(yb, ya, right_in, left_in, tiles, strips, xa, xb):
     index = lax.axis_index("gy")
     even = parity("gy")
     has_after = (index < lax.axis_size("gy") - 1).astype(F32)
@@ -471,7 +471,7 @@
 
 
 def outer_kernel(
-    factors, rr, ss, xr, xs, f_in, one_in, qq_in, gg_in, sums, homes, za, zb, sides, rim_a, rim_b,
+    factors, rr, ss, xr, xs, f_in, one_in, qq_in, gg_in, sums, homes, zb, za, sides, rim_b, rim_a,
     f, one, qq, gg, e_rest, h_rest, zeroth, first, second, third, xf, xone,
 ):
     del f_in, one_in, qq_in, gg_in
@@ -569,7 +569,7 @@
         copy.wait()
 
 
-def fold_kernel(sums, first, second, third, kept, sent):
+def fold_kernel(sums, second, first, third, kept, sent):
     upper = lax.rem(lax.axis_index("gz"), 2) == 1
     for i in range(2):
         low, high = (sums[j] + first[j] + second[j] + third[j] for j in (i, i + 2))
@@ -634,7 +634,7 @@
         strip_kernel, [(COMPS,) + block, (2,) + block, (2,) + block, (2, 8, COLS), deep, deep, tall, tall], scalars=2
     )(start_step, pml_cells, f)
     side = (2,) + tall
-    tiles, strips_rim, xa, xb = call(second_kernel, [(COMPS, PLANES, 8, COLS), (COMPS, 8, COLS), side, side])(ya, yb, right, left)
+    tiles, strips_rim, xa, xb = call(second_kernel, [(COMPS, PLANES, 8, COLS), (COMPS, 8, COLS), side, side])(yb, ya, right, left)
     za, zb = call(face_kernel, [(FACE_ROWS, COLS)] * 2)(f, tiles, *loss[:3])
     za = lax.ppermute(za, "gz", swaps("gz", 0))
     zb = lax.ppermute(zb, "gz", swaps("gz", 1))
@@ -654,10 +654,10 @@
     quarter, pair = (LAYERS // 4,) + block, (2,) + block
     *_, e_rest, h_rest, zeroth, first, second, third = call(
         outer_kernel, state + [mid, mid] + [quarter] * 4, side, aliases={5 + i: i for i in range(len(state))}
-    )(*loss, *held, sums, homes, za, zb, sides, rim_a, rim_b)
+    )(*loss, *held, sums, homes, zb, za, sides, rim_b, rim_a)
     e_out, h_out = call(store_kernel, [out, out], [pltpu.SemaphoreType.DMA((6,))], out_space=pltpu.HBM)(e_mid, h_mid, e_rest, h_rest)
     first, second, third = (lax.ppermute(v, "gz", across("gz", m)) for v, m in ((first, 2), (second, 4), (third, 6)))
-    kept, sent = call(fold_kernel, [pair, pair])(zeroth, first, second, third)
+    kept, sent = call(fold_kernel, [pair, pair])(zeroth, second, first, third)
     (gradient,) = call(sum_kernel, [pair])(kept, lax.ppermute(sent, "gz", across("gz", 1)))
     return gradient, e_out, h_out
 

time: 43.3 us -> 42.2 us (0.975)
  waiting for transfers between devices: 8.92 us -> 7.87 us
    ppermute x1, starting transfers between devices: 3.96 us -> 0.01 us  [local(): za = lax.ppermute(za, 'gz', swaps('gz', 0))]
    ppermute x1, starting transfers between devices: 2.54 us -> 6.41 us  [local(): zb = lax.ppermute(zb, 'gz', swaps('gz', 1))]
    ppermute x1, starting transfers between devices: 2.08 us -> 0.01 us  [local(): rim_a = lax.ppermute(rim_a, 'gz', swaps('gz', 0))]
    ppermute x1, starting transfers between devices: 1.71 us -> 3.78 us  [local(): rim_b = lax.ppermute(rim_b, 'gz', swaps('gz', 1))]
    ppermute x1, waiting for transfers between devices: 2.67 us -> 1.69 us  [local(): rim_b = lax.ppermute(rim_b, 'gz', swaps('gz', 1))]
    ppermute x3, starting transfers between devices: 4.78 us -> 4.17 us  [local(): lax.ppermute(v, 'gz', across('gz', m))]
    ppermute x1, waiting for transfers between devices: 0.92 us -> 1.49 us  [local(): rim_a = lax.ppermute(rim_a, 'gz', swaps('gz', 0))]
    ppermute x1, waiting for transfers between devices: 0.7 us -> 0.17 us  [local(): yb = lax.ppermute(yb, ('gy', 'gx'), inner_swaps())]
where the time goes in v6:
time: 42.2 us; the launch traced here: 42.1 us
  starting transfers between devices  23.1 us (55%)
  Pallas kernels  9.03 us (21%)
  waiting for transfers between devices  7.87 us (19%)
  between operations  1.37 us (3%)
  local copies, waits for them, and re-layouts  0.65 us (2%)
    pallas_call x10, Pallas kernels, run(): pl.pallas_call(kernel, out_shape=[jax.ShapeDtypeStruct(s, F32) for s in o...  9.03 us
    ppermute x1, starting transfers between devices, local(): zb = lax.ppermute(zb, 'gz', swaps('gz', 1))  6.41 us
    ppermute x3, starting transfers between devices, local(): lax.ppermute(v, 'gz', across('gz', m))  4.17 us
    ppermute x1, starting transfers between devices, local(): rim_b = lax.ppermute(rim_b, 'gz', swaps('gz', 1))  3.78 us
    ppermute x1, starting transfers between devices, local(): lax.ppermute(sent, 'gz', across('gz', 1))  2.83 us
    ppermute x3, waiting for transfers between devices, local(): lax.ppermute(v, 'gz', across('gz', m))  2.76 us
    ppermute x1, starting transfers between devices, local(): xb = lax.ppermute(xb, 'gx', swaps('gx', 1))  2.1 us
    ppermute x1, waiting for transfers between devices, local(): lax.ppermute(sent, 'gz', across('gz', 1))  1.74 us
  transfers between devices with their start and end apart: 12, of which 6 were waited for; matrix products, arithmetic and copies ran while one was open for 0% of the time, Pallas kernels for 12%

profile of v6, /device:TPU:0, one launch (start us, length us, event | category | flops | bytes accessed | tf_op | source)
XLA Modules:
  0.0 42.1 jit_solution(7688022394711330508)
XLA Ops:
  0.6 1.6 %shard_map.112 = (f32[14,12,40,128]{3,2,1,0:T(8,128)S(1)}, f32[224,128]{1,0:T(8,128)S(1)}, f32[224,128]{1,0:T(8,128)S(1)}) custom-call(f32[3,8,32,128]{3,2,1,0:T(8,128)} %e.1, f32[3,8,32,128]{3,2,1,0:T(8,128)} %h.1, f32[3,8,32,128]{3,2,1,0:T(8,128)} %ae.1, f32[3,8,32,128]{3,2,1,0:T(8,128)} %ah.1, f32[8,32,128]{2,1,0:T(8,128)} %eps.1, f32[8,32,128]{2,1,0:T(8,128)} %cur.1), custom_call_target="tpu_custom_call" | custom-call | flops 1000000 | bytes 5505024 | tf_op jit(solution)/shard_map/pallas_call | solution.py:590
  2.3 1.7 %collective-permute-start = (f32[224,128]{1,0:T(8,128)S(1)}, f32[224,128]{1,0:T(8,128)S(1)}, u32[]{:S(2)}, u32[]{:S(2)}) collective-permute-start(f32[224,128]{1,0:T(8,128)S(1)} %get-tuple-element.47), channel_id=1, source_target_pairs={{4,8},{0,1},{12,13},{5,9},{6,10},{2,3},{14,15},{7,11},{8,4},{1,0},... | collective-permute-start | bytes 344072 | tf_op jit(solution)/shard_map/ppermute | solution.py:631
  3.9 0.5 %collective-permute-start.1 = (f32[224,128]{1,0:T(8,128)S(1)}, f32[224,128]{1,0:T(8,128)S(1)}, u32[]{:S(2)}, u32[]{:S(2)}) collective-permute-start(f32[224,128]{1,0:T(8,128)S(1)} %get-tuple-element.48), channel_id=1, source_target_pairs={{0,4},{8,12},{4,0},{12,8},{1,5},{9,13},{5,1},{13,9},{2,6},{10,14},... | collective-permute-start | bytes 344072 | tf_op jit(solution)/shard_map/ppermute | solution.py:632
  5.1 0.0 copy-start
  5.1 0.6 %copy-done = s32[3]{0:T(128)S(1)} copy-done((s32[3]{0:T(128)S(1)}, s32[3]{0:T(128)}, u32[]{:S(2)}) %copy-start) | copy-done | bytes 36
  5.8 0.0 copy-start.1
  5.8 1.2 %shard_map.113 = (f32[14,32,128]{2,1,0:T(8,128)S(1)}, f32[2,32,128]{2,1,0:T(8,128)S(1)}, f32[2,32,128]{2,1,0:T(8,128)S(1)}, f32[2,8,128]{2,1,0:T(8,128)S(1)}, f3...) custom-call(s32[1]{0:T(128)S(6)} %copy.22.start, ...), custom_call_target="tpu_custom_call" | custom-call | flops 1000000 | bytes 4276240 | tf_op jit(solution)/shard_map/pallas_call | solution.py:590
  7.0 0.2 collective-permute-done.yb
  7.2 0.0 collective-permute-done.1.ya
  7.2 0.3 shard_map.114
  7.4 1.7 %collective-permute-start.2 = (f32[2,40,128]{2,1,0:T(8,128)S(1)}, f32[2,40,128]{2,1,0:T(8,128)S(1)}, u32[]{:S(2)}, u32[]{:S(2)}) collective-permute-start(f32[2,40,128]{2,1,0:T(8,128)S(1)} %get-tuple-element.52), channel_id=1, source_target_pairs={{0,1},{2,3},{1,0},{3,2},{4,5},{6,7},{5,4},{7,6},{8,9},{10,11},{9,8... | collective-permute-start | bytes 122888 | tf_op jit(solution)/shard_map/ppermute | solution.py:641
  9.1 2.1 %collective-permute-start.3 = (f32[2,40,128]{2,1,0:T(8,128)S(1)}, f32[2,40,128]{2,1,0:T(8,128)S(1)}, u32[]{:S(2)}, u32[]{:S(2)}) collective-permute-start(f32[2,40,128]{2,1,0:T(8,128)S(1)} %get-tuple-element.53), channel_id=1, source_target_pairs={{1,2},{3,0},{2,1},{0,3},{5,6},{7,4},{6,5},{4,7},{9,10},{11,8},{10,... | collective-permute-start | bytes 122888 | tf_op jit(solution)/shard_map/ppermute | solution.py:642
  11.2 0.2 shard_map.117
  11.4 6.4 %collective-permute-start.4 = (f32[368,128]{1,0:T(8,128)S(1)}, f32[368,128]{1,0:T(8,128)S(1)}, u32[]{:S(2)}, u32[]{:S(2)}) collective-permute-start(f32[368,128]{1,0:T(8,128)S(1)} %get-tuple-element.63), channel_id=1, source_target_pairs={{16,32},{48,64},{80,96},{112,0},{32,16},{64,48},{96,80},{0,112},{1... | collective-permute-start | bytes 565256 | tf_op jit(solution)/shard_map/ppermute | solution.py:640
  17.8 0.0 collective-permute-start.5
  17.8 0.0 collective-permute-done.2.xa
  17.8 0.0 collective-permute-done.3.xb
  17.8 0.6 %shard_map.115 = (f32[14,40,128]{2,1,0:T(8,128)S(1)}, f32[40,128]{1,0:T(8,128)S(1)}, f32[40,128]{1,0:T(8,128)S(1)}) custom-call(f32[2,40,128]{2,1,0:T(8,128)S(1)} %collective-permute-done.2.xa, f32[2,40,128]{2,1,0:T(8,128)S(1)} %collective-permute-done.3.xb, f32[14,32,128]{2,1,0:T(8,128)S(1)} %get-tuple-element.54.strips, ...), custom_call_target="tpu_custom_call" | custom-call | flops 1000000 | bytes 745472 | tf_op jit(solution)/shard_map/pallas_call | solution.py:590
  18.4 3.8 %collective-permute-start.6 = (f32[40,128]{1,0:T(8,128)S(1)}, f32[40,128]{1,0:T(8,128)S(1)}, u32[]{:S(2)}, u32[]{:S(2)}) collective-permute-start(f32[40,128]{1,0:T(8,128)S(1)} %get-tuple-element.65), channel_id=1, source_target_pairs={{16,32},{48,64},{80,96},{112,0},{32,16},{64,48},{96,80},{0,112},{1... | collective-permute-start | bytes 61448 | tf_op jit(solution)/shard_map/ppermute | solution.py:647
  22.2 0.0 collective-permute-start.7
  22.2 0.0 copy-done.1
  22.2 2.1 %shard_map.116 = (f32[14,12,40,128]{3,2,1,0:T(8,128)S(1)}, f32[6,12,40,128]{3,2,1,0:T(8,128)S(1)}, f32[12,40,128]{2,1,0:T(8,128)S(1)}, f32[12,40,128]{2,1,0:T(8,...) custom-call(s32[8]{0:T(128)S(1)} %copy-done.1, ...), custom_call_target="tpu_custom_call", output_to_operand_aliasing={{0}: (6, {})} | custom-call | flops 99999997952 | bytes 10805280 | tf_op jit(solution)/shard_map/pallas_call | solution.py:590
  24.3 1.7 %collective-permute-done.6.rim_b = f32[40,128]{1,0:T(8,128)S(1)} collective-permute-done((f32[40,128]{1,0:T(8,128)S(1)}, f32[40,128]{1,0:T(8,128)S(1)}, u32[]{:S(2)}, u32[]{:S(2)}) %collective-permute-start.6) | collective-permute-done | bytes 20512 | tf_op jit(solution)/shard_map/ppermute | solution.py:647
  26.0 1.5 %collective-permute-done.7.rim_a = f32[40,128]{1,0:T(8,128)S(1)} collective-permute-done((f32[40,128]{1,0:T(8,128)S(1)}, f32[40,128]{1,0:T(8,128)S(1)}, u32[]{:S(2)}, u32[]{:S(2)}) %collective-permute-start.7) | collective-permute-done | bytes 20512 | tf_op jit(solution)/shard_map/ppermute | solution.py:646
  27.5 0.0 collective-permute-done.4.zb
  27.5 0.0 collective-permute-done.5.za
  27.5 1.5 %shard_map.118 = (f32[14,12,40,128]{3,2,1,0:T(8,128)S(1)}, f32[6,12,40,128]{3,2,1,0:T(8,128)S(1)}, f32[12,40,128]{2,1,0:T(8,128)S(1)}, f32[12,40,128]{2,1,0:T(8,...) custom-call(f32[2,8,128]{2,1,0:T(8,128)S(1)} %get-tuple-element.42.f, ...), custom_call_target="tpu_custom_call", output_to_operand_aliasing={{0}: (5, {}), {1}: (6, {}), {2}: (7, {}), {3}: (8, {})} | custom-call | flops 1000000 | bytes 12992512 | tf_op jit(solution)/shard_map/pallas_call | solution.py:590
  29.0 0.7 %collective-permute-start.8 = (f32[4,32,128]{2,1,0:T(8,128)S(1)}, f32[4,32,128]{2,1,0:T(8,128)S(1)}, u32[]{:S(2)}, u32[]{:S(2)}) collective-permute-start(f32[4,32,128]{2,1,0:T(8,128)S(1)} %get-tuple-element.68), channel_id=1, source_target_pairs={{0,64},{16,80},{32,96},{48,112},{64,0},{80,16},{96,32},{112,48},{1... | collective-permute-start | bytes 196616 | tf_op jit(solution)/shard_map/ppermute | solution.py:659
  29.7 0.8 %collective-permute-start.9 = (f32[4,32,128]{2,1,0:T(8,128)S(1)}, f32[4,32,128]{2,1,0:T(8,128)S(1)}, u32[]{:S(2)}, u32[]{:S(2)}) collective-permute-start(f32[4,32,128]{2,1,0:T(8,128)S(1)} %get-tuple-element.69), channel_id=1, source_target_pairs={{0,32},{16,48},{32,0},{48,16},{64,96},{80,112},{96,64},{112,80},{1... | collective-permute-start | bytes 196616 | tf_op jit(solution)/shard_map/ppermute | solution.py:659
  30.4 2.7 %collective-permute-start.10 = (f32[4,32,128]{2,1,0:T(8,128)S(1)}, f32[4,32,128]{2,1,0:T(8,128)S(1)}, u32[]{:S(2)}, u32[]{:S(2)}) collective-permute-start(f32[4,32,128]{2,1,0:T(8,128)S(1)} %get-tuple-element.70), channel_id=1, source_target_pairs={{0,96},{16,112},{32,64},{48,80},{64,32},{80,48},{96,0},{112,16},{1... | collective-permute-start | bytes 196616 | tf_op jit(solution)/shard_map/ppermute | solution.py:659
  33.2 1.7 %collective-permute-done.8.second = f32[4,32,128]{2,1,0:T(8,128)S(1)} collective-permute-done((f32[4,32,128]{2,1,0:T(8,128)S(1)}, f32[4,32,128]{2,1,0:T(8,128)S(1)}, u32[]{:S(2)}, u32[]{:S(2)}) %collective-permute-start.8) | collective-permute-done | bytes 65568 | tf_op jit(solution)/shard_map/ppermute | solution.py:659
  34.8 0.0 collective-permute-done.9.first
  34.8 1.1 %collective-permute-done.10.third = f32[4,32,128]{2,1,0:T(8,128)S(1)} collective-permute-done((f32[4,32,128]{2,1,0:T(8,128)S(1)}, f32[4,32,128]{2,1,0:T(8,128)S(1)}, u32[]{:S(2)}, u32[]{:S(2)}) %collective-permute-start.10) | collective-permute-done | bytes 65568 | tf_op jit(solution)/shard_map/ppermute | solution.py:659
  35.9 2.8 %collective-permute-start.11 = (f32[2,32,128]{2,1,0:T(8,128)S(1)}, f32[2,32,128]{2,1,0:T(8,128)S(1)}, u32[]{:S(2)}, u32[]{:S(2)}) collective-permute-start(f32[2,32,128]{2,1,0:T(8,128)S(1)} %get-tuple-element.72), channel_id=1, source_target_pairs={{0,16},{16,0},{32,48},{48,32},{64,80},{80,64},{96,112},{112,96},{1... | collective-permute-start | bytes 98312 | tf_op jit(solution)/shard_map/ppermute | solution.py:661
  38.8 0.9 %shard_map.121 = (f32[3,8,32,128]{3,2,1,0:T(8,128)}, f32[3,8,32,128]{3,2,1,0:T(8,128)}) custom-call(f32[3,4,32,128]{3,2,1,0:T(8,128)S(1)} %get-tuple-element.73.e_mid, f32[3,4,32,128]{3,2,1,0:T(8,128)S(1)} %get-tuple-element.74.h_mid, f32[3,4,32,128]{3,2,1,0:T(8,128)S(1)} %get-tuple-element.75.e_rest, f32[3,4,32,128]{3,2,1,0:T(8,128)S(1)} %get-tuple-element.76.h_rest), custom_call_target="tpu_custom_call" | custom-call | flops 1000000 | bytes 1572864 | tf_op jit(solution)/shard_map/pallas_call | solution.py:590
  39.7 1.7 %collective-permute-done.11.got = f32[2,32,128]{2,1,0:T(8,128)S(1)} collective-permute-done((f32[2,32,128]{2,1,0:T(8,128)S(1)}, f32[2,32,128]{2,1,0:T(8,128)S(1)}, u32[]{:S(2)}, u32[]{:S(2)}) %collective-permute-start.11) | collective-permute-done | bytes 32800 | tf_op jit(solution)/shard_map/ppermute | solution.py:661
  41.4 0.6 %shard_map.120 = f32[2,32,128]{2,1,0:T(8,128)} custom-call(f32[2,32,128]{2,1,0:T(8,128)S(1)} %get-tuple-element.71.kept, f32[2,32,128]{2,1,0:T(8,128)S(1)} %collective-permute-done.11.got), custom_call_target="tpu_custom_call" | custom-call | flops 1000000 | bytes 98304 | tf_op jit(solution)/shard_map/pallas_call | solution.py:590
  (1 shorter events, 0.0 us)
Async XLA Ops:
  2.3 4.9 %collective-permute-start = (f32[224,128]{1,0:T(8,128)S(1)}, f32[224,128]{1,0:T(8,128)S(1)}, u32[]{:S(2)}, u32[]{:S(2)}) collective-permute-start(f32[224,128]{1,0:T(8,128)S(1)} %get-tuple-element.47), channel_id=1, source_target_pairs={{4,8},{0,1},{12,13},{5,9},{6,10},{2,3},{14,15},{7,11},{8,4},{1,0},... | collective-permute-start | bytes 344072 | tf_op jit(solution)/shard_map/ppermute | solution.py:631
  3.9 3.2 %collective-permute-start.1 = (f32[224,128]{1,0:T(8,128)S(1)}, f32[224,128]{1,0:T(8,128)S(1)}, u32[]{:S(2)}, u32[]{:S(2)}) collective-permute-start(f32[224,128]{1,0:T(8,128)S(1)} %get-tuple-element.48), channel_id=1, source_target_pairs={{0,4},{8,12},{4,0},{12,8},{1,5},{9,13},{5,1},{13,9},{2,6},{10,14},... | collective-permute-start | bytes 344072 | tf_op jit(solution)/shard_map/ppermute | solution.py:632
  5.1 0.7 %copy-start = (s32[3]{0:T(128)S(1)}, s32[3]{0:T(128)}, u32[]{:S(2)}) copy-start(s32[3]{0:T(128)} %pml.1) | copy-start | bytes 40
  5.8 16.4 %copy-start.1 = (s32[8]{0:T(128)S(1)}, s32[8]{0:T(128)}, u32[]{:S(2)}) copy-start(s32[8]{0:T(128)} %layer.1) | copy-start | bytes 100
  7.4 10.4 %collective-permute-start.2 = (f32[2,40,128]{2,1,0:T(8,128)S(1)}, f32[2,40,128]{2,1,0:T(8,128)S(1)}, u32[]{:S(2)}, u32[]{:S(2)}) collective-permute-start(f32[2,40,128]{2,1,0:T(8,128)S(1)} %get-tuple-element.52), channel_id=1, source_target_pairs={{0,1},{2,3},{1,0},{3,2},{4,5},{6,7},{5,4},{7,6},{8,9},{10,11},{9,8... | collective-permute-start | bytes 122888 | tf_op jit(solution)/shard_map/ppermute | solution.py:641
  9.1 8.8 %collective-permute-start.3 = (f32[2,40,128]{2,1,0:T(8,128)S(1)}, f32[2,40,128]{2,1,0:T(8,128)S(1)}, u32[]{:S(2)}, u32[]{:S(2)}) collective-permute-start(f32[2,40,128]{2,1,0:T(8,128)S(1)} %get-tuple-element.53), channel_id=1, source_target_pairs={{1,2},{3,0},{2,1},{0,3},{5,6},{7,4},{6,5},{4,7},{9,10},{11,8},{10,... | collective-permute-start | bytes 122888 | tf_op jit(solution)/shard_map/ppermute | solution.py:642
  11.4 16.1 %collective-permute-start.4 = (f32[368,128]{1,0:T(8,128)S(1)}, f32[368,128]{1,0:T(8,128)S(1)}, u32[]{:S(2)}, u32[]{:S(2)}) collective-permute-start(f32[368,128]{1,0:T(8,128)S(1)} %get-tuple-element.63), channel_id=1, source_target_pairs={{16,32},{48,64},{80,96},{112,0},{32,16},{64,48},{96,80},{0,112},{1... | collective-permute-start | bytes 565256 | tf_op jit(solution)/shard_map/ppermute | solution.py:640
  17.8 9.7 %collective-permute-start.5 = (f32[368,128]{1,0:T(8,128)S(1)}, f32[368,128]{1,0:T(8,128)S(1)}, u32[]{:S(2)}, u32[]{:S(2)}) collective-permute-start(f32[368,128]{1,0:T(8,128)S(1)} %get-tuple-element.64), channel_id=1, source_target_pairs={{0,16},{32,48},{64,80},{96,112},{16,0},{48,32},{80,64},{112,96},{1... | collective-permute-start | bytes 565256 | tf_op jit(solution)/shard_map/ppermute | solution.py:639
  18.4 7.6 %collective-permute-start.6 = (f32[40,128]{1,0:T(8,128)S(1)}, f32[40,128]{1,0:T(8,128)S(1)}, u32[]{:S(2)}, u32[]{:S(2)}) collective-permute-start(f32[40,128]{1,0:T(8,128)S(1)} %get-tuple-element.65), channel_id=1, source_target_pairs={{16,32},{48,64},{80,96},{112,0},{32,16},{64,48},{96,80},{0,112},{1... | collective-permute-start | bytes 61448 | tf_op jit(solution)/shard_map/ppermute | solution.py:647
  22.2 5.3 %collective-permute-start.7 = (f32[40,128]{1,0:T(8,128)S(1)}, f32[40,128]{1,0:T(8,128)S(1)}, u32[]{:S(2)}, u32[]{:S(2)}) collective-permute-start(f32[40,128]{1,0:T(8,128)S(1)} %get-tuple-element.66), channel_id=1, source_target_pairs={{0,16},{32,48},{64,80},{96,112},{16,0},{48,32},{80,64},{112,96},{1... | collective-permute-start | bytes 61448 | tf_op jit(solution)/shard_map/ppermute | solution.py:646
  29.0 5.8 %collective-permute-start.8 = (f32[4,32,128]{2,1,0:T(8,128)S(1)}, f32[4,32,128]{2,1,0:T(8,128)S(1)}, u32[]{:S(2)}, u32[]{:S(2)}) collective-permute-start(f32[4,32,128]{2,1,0:T(8,128)S(1)} %get-tuple-element.68), channel_id=1, source_target_pairs={{0,64},{16,80},{32,96},{48,112},{64,0},{80,16},{96,32},{112,48},{1... | collective-permute-start | bytes 196616 | tf_op jit(solution)/shard_map/ppermute | solution.py:659
  29.7 5.2 %collective-permute-start.9 = (f32[4,32,128]{2,1,0:T(8,128)S(1)}, f32[4,32,128]{2,1,0:T(8,128)S(1)}, u32[]{:S(2)}, u32[]{:S(2)}) collective-permute-start(f32[4,32,128]{2,1,0:T(8,128)S(1)} %get-tuple-element.69), channel_id=1, source_target_pairs={{0,32},{16,48},{32,0},{48,16},{64,96},{80,112},{96,64},{112,80},{1... | collective-permute-start | bytes 196616 | tf_op jit(solution)/shard_map/ppermute | solution.py:659
  30.4 5.5 %collective-permute-start.10 = (f32[4,32,128]{2,1,0:T(8,128)S(1)}, f32[4,32,128]{2,1,0:T(8,128)S(1)}, u32[]{:S(2)}, u32[]{:S(2)}) collective-permute-start(f32[4,32,128]{2,1,0:T(8,128)S(1)} %get-tuple-element.70), channel_id=1, source_target_pairs={{0,96},{16,112},{32,64},{48,80},{64,32},{80,48},{96,0},{112,16},{1... | collective-permute-start | bytes 196616 | tf_op jit(solution)/shard_map/ppermute | solution.py:659
  35.9 5.5 %collective-permute-start.11 = (f32[2,32,128]{2,1,0:T(8,128)S(1)}, f32[2,32,128]{2,1,0:T(8,128)S(1)}, u32[]{:S(2)}, u32[]{:S(2)}) collective-permute-start(f32[2,32,128]{2,1,0:T(8,128)S(1)} %get-tuple-element.72), channel_id=1, source_target_pairs={{0,16},{16,0},{32,48},{48,32},{64,80},{80,64},{96,112},{112,96},{1... | collective-permute-start | bytes 98312 | tf_op jit(solution)/shard_map/ppermute | solution.py:661

commit v7 on v6

--- a/solution.py
+++ b/solution.py
@@ -14,6 +14,7 @@
 LAYERS = 16
 PERIOD = 64
 COMPS = 14
+LOW, TOP = 1, PLANES + 2
 UP_FACES = [("h", k) for k in (3, 4, 9, 10)] + [("e", k) for k in (0, 1, 2, 6, 7, 8)] + [("f", 12)]
 DOWN_FACES = [("f", k) for k in (0, 1, 6, 7, 12)] + [("e", k) for k in (0, 1, 6, 7)]
 UP_ROWS = [("h", k, 7) for k in (3, 4, 9, 10)] + [("e", 2, 7), ("e", 8, 7), ("f", 12, 7)]
@@ -305,7 +306,7 @@
     zb[...] = jnp.where(even, sent[1], sent[0])
 
 
-def third_kernel(xa, xb, strips, strips_rim, factors, xr, xs, sides, rim_a, rim_b):
+def third_kernel(xb, xa, strips, strips_rim, factors, xr, xs, sides, rim_a, rim_b):
     index = lax.axis_index("gx")
     even = parity("gx")
     has_after = (index < lax.axis_size("gx") - 1).astype(F32)
@@ -470,39 +471,64 @@
     run_steps((xr, xs), factors, f, one, rr, qq, gg, xf, xone, planes, put, put_density)
 
 
+def halo_kernel(rr, ss, sides, f_in, qq_in, gg_in, zb, za, f, qq, gg, below, above):
+    del f_in, qq_in, gg_in
+    index = lax.axis_index("gz")
+    even = parity("gz")
+    lane = lanes(TALL)
+    for pick, faces, rows, out, idx, keep in (
+        (lambda a, b: jnp.where(even, b, a), UP_FACES, UP_ROWS, below, LOW, (index > 0).astype(F32)),
+        (lambda a, b: jnp.where(even, a, b), DOWN_FACES, DOWN_ROWS, above, TOP, (index < lax.axis_size("gz") - 1).astype(F32)),
+    ):
+        planes = face_in(pick(za[...], zb[...]), faces, rows, keep)
+        for i, (kind, k) in enumerate(faces):
+            if kind == "f":
+                f[k, idx] = planes[kind, k]
+            else:
+                out[i] = planes[kind, k]
+        qq[idx], gg[idx] = electric_coefficients(rr[idx], ss[idx], f[12, idx])
+    last = TOP - 1
+    for base in (0, 6):
+
+        def next_x(value, c):
+            return jnp.where(lane == COLS - 1, turn(sides[base + c], 125 - 8 * last, 1), pltpu.roll(value, COLS - 1, 1))
+
+        new = magnetic(
+            *[f[base + c, last] for c in range(3)], f[base, TOP], f[base + 1, TOP],
+            *[f[base + 3 + c, last] for c in range(3)], rr[last], next_x, up_row,
+        )
+        for c in range(3):
+            f[base + 3 + c, last] = new[c]
+
+
 def outer_kernel(
-    factors, rr, ss, xr, xs, f_in, one_in, qq_in, gg_in, sums, homes, zb, za, sides, rim_b, rim_a,
-    f, one, qq, gg, e_rest, h_rest, zeroth, first, second, third, xf, xone,
+    factors, rr, xr, xs, f_in, one_in, qq, gg, sums, homes, below, above, sides, rim_b, rim_a,
+    f, one, e_rest, h_rest, zeroth, first, second, third, xf, xone,
 ):
-    del f_in, one_in, qq_in, gg_in
+    del f_in, one_in
     index = lax.axis_index("gz")
     has_above = (index < lax.axis_size("gz") - 1).astype(F32)
     has_below = (index > 0).astype(F32)
     lane = lanes(TALL)
-    low, top = 1, PLANES + 2
+    low, top = LOW, TOP
     for k in range(COMPS):
         xf[k] = sides[k]
     got = {}
     even = parity("gz")
-    for pick, faces, rows, items, idx, keep in (
-        (lambda a, b: jnp.where(even, b, a), UP_FACES, UP_ROWS, UP_SIDES, low, has_below),
-        (lambda a, b: jnp.where(even, a, b), DOWN_FACES, DOWN_ROWS, DOWN_SIDES, top, has_above),
+    for pick, ref, faces, idx, keep in (
+        (lambda a, b: jnp.where(even, b, a), below, UP_FACES, low, has_below),
+        (lambda a, b: jnp.where(even, a, b), above, DOWN_FACES, top, has_above),
     ):
-        ref = pick(za[...], zb[...])
         packed = pick(rim_a[...], rim_b[...]) * keep
-        planes = face_in(ref, faces, rows, keep)
-        for i, (kind, k) in enumerate(items):
-            if kind != "f":
-                at_last, at_first = turn(packed, 126 - 8 * i, 1), turn(packed, -6 - 8 * i, 1)
-                fixed = jnp.where(lane == COLS - 1, at_last, planes[kind, k])
-                planes[kind, k] = jnp.where(lane == 0, at_first, fixed) if kind == "e" else fixed
-            got[kind, k, idx] = (planes[kind, k], turn(packed, 8 * idx - 8 * i, 1))
-        for k in (0, 1, 6, 7, 12):
-            if ("f", k) in planes:
-                f[k, idx] = planes["f", k]
-                xf[k] = jnp.where((lane >> 3) == idx, got["f", k, idx][1], xf[k])
-    for idx in (low, top):
-        qq[idx], gg[idx] = electric_coefficients(rr[idx], ss[idx], f[12, idx])
+        for i, (kind, k) in enumerate(faces):
+            side = turn(packed, 8 * idx - 8 * i, 1)
+            if kind == "f":
+                xf[k] = jnp.where((lane >> 3) == idx, side, xf[k])
+                continue
+            plane = jnp.where(lane == COLS - 1, turn(packed, 126 - 8 * i, 1), ref[i])
+            if kind == "e":
+                plane = jnp.where(lane == 0, turn(packed, -6 - 8 * i, 1), plane)
+            got[kind, k, idx] = (plane, side)
 
     def add_z(q, x, y, prev_x):
         return q * ((y - prev_x(y)) - (x - down_row(x, 0)))
@@ -546,7 +572,7 @@
     def put_density(idx, density):
         late.append(density)
 
-    planes = [(9,), (2, 9), (1, 2, 8, 9), (2, 3, 8, 9)]
+    planes = [(), (2, 9), (1, 2, 8, 9), (2, 3, 8, 9)]
     run_steps((xr, xs), factors, f, one, rr, qq, gg, xf, xone, planes, put, put_density, halo)
     for i, out in enumerate((zeroth, first, second, third)):
         for j in range(4):
@@ -641,7 +667,7 @@
     xa = lax.ppermute(xa, "gx", swaps("gx", 0))
     xb = lax.ppermute(xb, "gx", swaps("gx", 1))
     sides, rim_a, rim_b = call(third_kernel, [(COMPS,) + tall, tall, tall])(
-        xa, xb, strips, strips_rim, loss[0], *loss[3:]
+        xb, xa, strips, strips_rim, loss[0], *loss[3:]
     )
     rim_a = lax.ppermute(rim_a, "gz", swaps("gz", 0))
     rim_b = lax.ppermute(rim_b, "gz", swaps("gz", 1))
@@ -652,9 +678,16 @@
         layer_of_cell, *loss, f, tiles, sides
     )
     quarter, pair = (LAYERS // 4,) + block, (2,) + block
+    f, one, qq, gg = held
+    factors, rr, ss, xr, xs = loss
+    f, qq, gg, below, above = call(
+        halo_kernel,
+        [(COMPS,) + deep, deep, deep, (len(UP_FACES),) + tall, (len(DOWN_FACES),) + tall],
+        aliases={3: 0, 4: 1, 5: 2},
+    )(rr, ss, sides, f, qq, gg, zb, za)
     *_, e_rest, h_rest, zeroth, first, second, third = call(
-        outer_kernel, state + [mid, mid] + [quarter] * 4, side, aliases={5 + i: i for i in range(len(state))}
-    )(*loss, *held, sums, homes, zb, za, sides, rim_b, rim_a)
+        outer_kernel, [(COMPS,) + deep, (6,) + deep, mid, mid] + [quarter] * 4, side, aliases={4: 0, 5: 1}
+    )(factors, rr, xr, xs, f, one, qq, gg, sums, homes, below, above, sides, rim_b, rim_a)
     e_out, h_out = call(store_kernel, [out, out], [pltpu.SemaphoreType.DMA((6,))], out_space=pltpu.HBM)(e_mid, h_mid, e_rest, h_rest)
     first, second, third = (lax.ppermute(v, "gz", across("gz", m)) for v, m in ((first, 2), (second, 4), (third, 6)))
     kept, sent = call(fold_kernel, [pair, pair])(zeroth, second, first, third)

time: 42.2 us -> 41.8 us (level)
  starting transfers between devices: 23.1 us -> 22.6 us
    ppermute x1, waiting for transfers between devices: 0.01 us -> 2.27 us  [local(): za = lax.ppermute(za, 'gz', swaps('gz', 0))]
    ppermute x1, waiting for transfers between devices: 1.69 us -> 0.01 us  [local(): rim_b = lax.ppermute(rim_b, 'gz', swaps('gz', 1))]
    ppermute x1, starting transfers between devices: 1.65 us -> 0.22 us  [local(): xa = lax.ppermute(xa, 'gx', swaps('gx', 0))]
    ppermute x1, starting transfers between devices: 2.1 us -> 2.92 us  [local(): xb = lax.ppermute(xb, 'gx', swaps('gx', 1))]
    ppermute x1, waiting for transfers between devices: 1.49 us -> 0.73 us  [local(): rim_a = lax.ppermute(rim_a, 'gz', swaps('gz', 0))]
    pallas_call x10 -> x11, Pallas kernels: 9.03 us -> 9.16 us  [run(): pl.pallas_call(kernel, out_shape=[jax.ShapeDtypeStruct(s, F32) for s in o...]
  transfers between devices with their start and end apart: 12 -> 12, of which waited for: 6 -> 6; matrix products, arithmetic and copies ran while one was open for 0% -> 0% of each run, Pallas kernels for 12% -> 13%
where the time goes in v7:
time: 41.8 us; the launch traced here: 41.4 us
  starting transfers between devices  22.6 us (54%)
  Pallas kernels  9.16 us (22%)
  waiting for transfers between devices  7.62 us (18%)
  between operations  1.39 us (3%)
  local copies, waits for them, and re-layouts  0.65 us (2%)
    pallas_call x11, Pallas kernels, run(): pl.pallas_call(kernel, out_shape=[jax.ShapeDtypeStruct(s, F32) for s in o...  9.16 us
    ppermute x1, starting transfers between devices, local(): zb = lax.ppermute(zb, 'gz', swaps('gz', 1))  6.41 us
    ppermute x3, starting transfers between devices, local(): lax.ppermute(v, 'gz', across('gz', m))  4.17 us
    ppermute x1, starting transfers between devices, local(): rim_b = lax.ppermute(rim_b, 'gz', swaps('gz', 1))  3.78 us
    ppermute x1, starting transfers between devices, local(): xb = lax.ppermute(xb, 'gx', swaps('gx', 1))  2.92 us
    ppermute x1, starting transfers between devices, local(): lax.ppermute(sent, 'gz', across('gz', 1))  2.89 us
    ppermute x3, waiting for transfers between devices, local(): lax.ppermute(v, 'gz', across('gz', m))  2.76 us
    ppermute x1, waiting for transfers between devices, local(): za = lax.ppermute(za, 'gz', swaps('gz', 0))  2.27 us
  transfers between devices with their start and end apart: 12, of which 6 were waited for; matrix products, arithmetic and copies ran while one was open for 0% of the time, Pallas kernels for 13%

profile of v7, /device:TPU:0, one launch (start us, length us, event | category | flops | bytes accessed | tf_op | source)
XLA Modules:
  0.0 41.4 jit_solution(16685636251022894706)
XLA Ops:
  0.6 1.6 %shard_map.112 = (f32[14,12,40,128]{3,2,1,0:T(8,128)S(1)}, f32[224,128]{1,0:T(8,128)S(1)}, f32[224,128]{1,0:T(8,128)S(1)}) custom-call(f32[3,8,32,128]{3,2,1,0:T(8,128)} %e.1, f32[3,8,32,128]{3,2,1,0:T(8,128)} %h.1, f32[3,8,32,128]{3,2,1,0:T(8,128)} %ae.1, f32[3,8,32,128]{3,2,1,0:T(8,128)} %ah.1, f32[8,32,128]{2,1,0:T(8,128)} %eps.1, f32[8,32,128]{2,1,0:T(8,128)} %cur.1), custom_call_target="tpu_custom_call" | custom-call | flops 1000000 | bytes 5505024 | tf_op jit(solution)/shard_map/pallas_call | solution.py:616
  2.3 1.7 %collective-permute-start = (f32[224,128]{1,0:T(8,128)S(1)}, f32[224,128]{1,0:T(8,128)S(1)}, u32[]{:S(2)}, u32[]{:S(2)}) collective-permute-start(f32[224,128]{1,0:T(8,128)S(1)} %get-tuple-element.52), channel_id=1, source_target_pairs={{4,8},{0,1},{12,13},{5,9},{6,10},{2,3},{14,15},{7,11},{8,4},{1,0},... | collective-permute-start | bytes 344072 | tf_op jit(solution)/shard_map/ppermute | solution.py:657
  3.9 0.5 %collective-permute-start.1 = (f32[224,128]{1,0:T(8,128)S(1)}, f32[224,128]{1,0:T(8,128)S(1)}, u32[]{:S(2)}, u32[]{:S(2)}) collective-permute-start(f32[224,128]{1,0:T(8,128)S(1)} %get-tuple-element.53), channel_id=1, source_target_pairs={{0,4},{8,12},{4,0},{12,8},{1,5},{9,13},{5,1},{13,9},{2,6},{10,14},... | collective-permute-start | bytes 344072 | tf_op jit(solution)/shard_map/ppermute | solution.py:658
  5.1 0.0 copy-start
  5.1 0.6 %copy-done = s32[3]{0:T(128)S(1)} copy-done((s32[3]{0:T(128)S(1)}, s32[3]{0:T(128)}, u32[]{:S(2)}) %copy-start) | copy-done | bytes 36
  5.8 0.0 copy-start.1
  5.8 1.2 %shard_map.113 = (f32[14,32,128]{2,1,0:T(8,128)S(1)}, f32[2,32,128]{2,1,0:T(8,128)S(1)}, f32[2,32,128]{2,1,0:T(8,128)S(1)}, f32[2,8,128]{2,1,0:T(8,128)S(1)}, f3...) custom-call(s32[1]{0:T(128)S(6)} %copy.24.start, ...), custom_call_target="tpu_custom_call" | custom-call | flops 1000000 | bytes 4276240 | tf_op jit(solution)/shard_map/pallas_call | solution.py:616
  7.0 0.2 collective-permute-done.yb
  7.2 0.0 collective-permute-done.1.ya
  7.2 0.3 shard_map.114
  7.4 2.9 %collective-permute-start.2 = (f32[2,40,128]{2,1,0:T(8,128)S(1)}, f32[2,40,128]{2,1,0:T(8,128)S(1)}, u32[]{:S(2)}, u32[]{:S(2)}) collective-permute-start(f32[2,40,128]{2,1,0:T(8,128)S(1)} %get-tuple-element.56), channel_id=1, source_target_pairs={{1,2},{3,0},{2,1},{0,3},{5,6},{7,4},{6,5},{4,7},{9,10},{11,8},{10,... | collective-permute-start | bytes 122888 | tf_op jit(solution)/shard_map/ppermute | solution.py:668
  10.3 0.2 collective-permute-start.3
  10.6 0.2 shard_map.117
  10.8 6.4 %collective-permute-start.4 = (f32[368,128]{1,0:T(8,128)S(1)}, f32[368,128]{1,0:T(8,128)S(1)}, u32[]{:S(2)}, u32[]{:S(2)}) collective-permute-start(f32[368,128]{1,0:T(8,128)S(1)} %get-tuple-element.65), channel_id=1, source_target_pairs={{16,32},{48,64},{80,96},{112,0},{32,16},{64,48},{96,80},{0,112},{1... | collective-permute-start | bytes 565256 | tf_op jit(solution)/shard_map/ppermute | solution.py:666
  17.2 0.0 collective-permute-start.5
  17.2 0.0 collective-permute-done.2.xb
  17.2 0.0 collective-permute-done.3.xa
  17.2 0.6 %shard_map.115 = (f32[14,40,128]{2,1,0:T(8,128)S(1)}, f32[40,128]{1,0:T(8,128)S(1)}, f32[40,128]{1,0:T(8,128)S(1)}) custom-call(f32[2,40,128]{2,1,0:T(8,128)S(1)} %collective-permute-done.2.xb, f32[2,40,128]{2,1,0:T(8,128)S(1)} %collective-permute-done.3.xa, f32[14,32,128]{2,1,0:T(8,128)S(1)} %get-tuple-element.58.strips, ...), custom_call_target="tpu_custom_call" | custom-call | flops 1000000 | bytes 745472 | tf_op jit(solution)/shard_map/pallas_call | solution.py:616
  17.8 3.8 %collective-permute-start.6 = (f32[40,128]{1,0:T(8,128)S(1)}, f32[40,128]{1,0:T(8,128)S(1)}, u32[]{:S(2)}, u32[]{:S(2)}) collective-permute-start(f32[40,128]{1,0:T(8,128)S(1)} %get-tuple-element.75), channel_id=1, source_target_pairs={{16,32},{48,64},{80,96},{112,0},{32,16},{64,48},{96,80},{0,112},{1... | collective-permute-start | bytes 61448 | tf_op jit(solution)/shard_map/ppermute | solution.py:673
  21.6 0.0 collective-permute-start.7
  21.6 0.0 copy-done.1
  21.6 2.1 %shard_map.116 = (f32[14,12,40,128]{3,2,1,0:T(8,128)S(1)}, f32[6,12,40,128]{3,2,1,0:T(8,128)S(1)}, f32[12,40,128]{2,1,0:T(8,128)S(1)}, f32[12,40,128]{2,1,0:T(8,...) custom-call(s32[8]{0:T(128)S(1)} %copy-done.1, ...), custom_call_target="tpu_custom_call", output_to_operand_aliasing={{0}: (6, {})} | custom-call | flops 99999997952 | bytes 10805280 | tf_op jit(solution)/shard_map/pallas_call | solution.py:616
  23.7 0.0 collective-permute-done.4.zb
  23.8 2.3 %collective-permute-done.5.za = f32[368,128]{1,0:T(8,128)S(1)} collective-permute-done((f32[368,128]{1,0:T(8,128)S(1)}, f32[368,128]{1,0:T(8,128)S(1)}, u32[]{:S(2)}, u32[]{:S(2)}) %collective-permute-start.5) | collective-permute-done | bytes 188448 | tf_op jit(solution)/shard_map/ppermute | solution.py:665
  26.0 0.1 shard_map.118
  26.2 0.0 collective-permute-done.6.rim_b
  26.2 0.7 %collective-permute-done.7.rim_a = f32[40,128]{1,0:T(8,128)S(1)} collective-permute-done((f32[40,128]{1,0:T(8,128)S(1)}, f32[40,128]{1,0:T(8,128)S(1)}, u32[]{:S(2)}, u32[]{:S(2)}) %collective-permute-start.7) | collective-permute-done | bytes 20512 | tf_op jit(solution)/shard_map/ppermute | solution.py:672
  26.9 1.4 %shard_map.119 = (f32[14,12,40,128]{3,2,1,0:T(8,128)S(1)}, f32[6,12,40,128]{3,2,1,0:T(8,128)S(1)}, f32[3,4,32,128]{3,2,1,0:T(8,128)S(1)}, f32[3,4,32,128]{3,2,1,...) custom-call(f32[2,8,128]{2,1,0:T(8,128)S(1)} %get-tuple-element.47.f, ...), custom_call_target="tpu_custom_call", output_to_operand_aliasing={{0}: (4, {}), {1}: (5, {})} | custom-call | flops 1000000 | bytes 12288000 | tf_op jit(solution)/shard_map/pallas_call | solution.py:616
  28.3 0.7 %collective-permute-start.8 = (f32[4,32,128]{2,1,0:T(8,128)S(1)}, f32[4,32,128]{2,1,0:T(8,128)S(1)}, u32[]{:S(2)}, u32[]{:S(2)}) collective-permute-start(f32[4,32,128]{2,1,0:T(8,128)S(1)} %get-tuple-element.78), channel_id=1, source_target_pairs={{0,64},{16,80},{32,96},{48,112},{64,0},{80,16},{96,32},{112,48},{1... | collective-permute-start | bytes 196616 | tf_op jit(solution)/shard_map/ppermute | solution.py:692
  29.1 0.7 %collective-permute-start.9 = (f32[4,32,128]{2,1,0:T(8,128)S(1)}, f32[4,32,128]{2,1,0:T(8,128)S(1)}, u32[]{:S(2)}, u32[]{:S(2)}) collective-permute-start(f32[4,32,128]{2,1,0:T(8,128)S(1)} %get-tuple-element.79), channel_id=1, source_target_pairs={{0,32},{16,48},{32,0},{48,16},{64,96},{80,112},{96,64},{112,80},{1... | collective-permute-start | bytes 196616 | tf_op jit(solution)/shard_map/ppermute | solution.py:692
  29.8 2.7 %collective-permute-start.10 = (f32[4,32,128]{2,1,0:T(8,128)S(1)}, f32[4,32,128]{2,1,0:T(8,128)S(1)}, u32[]{:S(2)}, u32[]{:S(2)}) collective-permute-start(f32[4,32,128]{2,1,0:T(8,128)S(1)} %get-tuple-element.80), channel_id=1, source_target_pairs={{0,96},{16,112},{32,64},{48,80},{64,32},{80,48},{96,0},{112,16},{1... | collective-permute-start | bytes 196616 | tf_op jit(solution)/shard_map/ppermute | solution.py:692
  32.5 1.7 %collective-permute-done.8.second = f32[4,32,128]{2,1,0:T(8,128)S(1)} collective-permute-done((f32[4,32,128]{2,1,0:T(8,128)S(1)}, f32[4,32,128]{2,1,0:T(8,128)S(1)}, u32[]{:S(2)}, u32[]{:S(2)}) %collective-permute-start.8) | collective-permute-done | bytes 65568 | tf_op jit(solution)/shard_map/ppermute | solution.py:692
  34.2 0.0 collective-permute-done.9.first
  34.2 1.1 %collective-permute-done.10.third = f32[4,32,128]{2,1,0:T(8,128)S(1)} collective-permute-done((f32[4,32,128]{2,1,0:T(8,128)S(1)}, f32[4,32,128]{2,1,0:T(8,128)S(1)}, u32[]{:S(2)}, u32[]{:S(2)}) %collective-permute-start.10) | collective-permute-done | bytes 65568 | tf_op jit(solution)/shard_map/ppermute | solution.py:692
  35.3 2.9 %collective-permute-start.11 = (f32[2,32,128]{2,1,0:T(8,128)S(1)}, f32[2,32,128]{2,1,0:T(8,128)S(1)}, u32[]{:S(2)}, u32[]{:S(2)}) collective-permute-start(f32[2,32,128]{2,1,0:T(8,128)S(1)} %get-tuple-element.82), channel_id=1, source_target_pairs={{0,16},{16,0},{32,48},{48,32},{64,80},{80,64},{96,112},{112,96},{1... | collective-permute-start | bytes 98312 | tf_op jit(solution)/shard_map/ppermute | solution.py:694
  38.2 0.9 %shard_map.122 = (f32[3,8,32,128]{3,2,1,0:T(8,128)}, f32[3,8,32,128]{3,2,1,0:T(8,128)}) custom-call(f32[3,4,32,128]{3,2,1,0:T(8,128)S(1)} %get-tuple-element.83.e_mid, f32[3,4,32,128]{3,2,1,0:T(8,128)S(1)} %get-tuple-element.84.h_mid, f32[3,4,32,128]{3,2,1,0:T(8,128)S(1)} %get-tuple-element.85.e_rest, f32[3,4,32,128]{3,2,1,0:T(8,128)S(1)} %get-tuple-element.86.h_rest), custom_call_target="tpu_custom_call" | custom-call | flops 1000000 | bytes 1572864 | tf_op jit(solution)/shard_map/pallas_call | solution.py:616
  39.1 1.7 %collective-permute-done.11.got = f32[2,32,128]{2,1,0:T(8,128)S(1)} collective-permute-done((f32[2,32,128]{2,1,0:T(8,128)S(1)}, f32[2,32,128]{2,1,0:T(8,128)S(1)}, u32[]{:S(2)}, u32[]{:S(2)}) %collective-permute-start.11) | collective-permute-done | bytes 32800 | tf_op jit(solution)/shard_map/ppermute | solution.py:694
  40.8 0.6 %shard_map.121 = f32[2,32,128]{2,1,0:T(8,128)} custom-call(f32[2,32,128]{2,1,0:T(8,128)S(1)} %get-tuple-element.81.kept, f32[2,32,128]{2,1,0:T(8,128)S(1)} %collective-permute-done.11.got), custom_call_target="tpu_custom_call" | custom-call | flops 1000000 | bytes 98304 | tf_op jit(solution)/shard_map/pallas_call | solution.py:616
  (1 shorter events, 0.0 us)
Async XLA Ops:
  2.3 4.9 %collective-permute-start = (f32[224,128]{1,0:T(8,128)S(1)}, f32[224,128]{1,0:T(8,128)S(1)}, u32[]{:S(2)}, u32[]{:S(2)}) collective-permute-start(f32[224,128]{1,0:T(8,128)S(1)} %get-tuple-element.52), channel_id=1, source_target_pairs={{4,8},{0,1},{12,13},{5,9},{6,10},{2,3},{14,15},{7,11},{8,4},{1,0},... | collective-permute-start | bytes 344072 | tf_op jit(solution)/shard_map/ppermute | solution.py:657
  3.9 3.2 %collective-permute-start.1 = (f32[224,128]{1,0:T(8,128)S(1)}, f32[224,128]{1,0:T(8,128)S(1)}, u32[]{:S(2)}, u32[]{:S(2)}) collective-permute-start(f32[224,128]{1,0:T(8,128)S(1)} %get-tuple-element.53), channel_id=1, source_target_pairs={{0,4},{8,12},{4,0},{12,8},{1,5},{9,13},{5,1},{13,9},{2,6},{10,14},... | collective-permute-start | bytes 344072 | tf_op jit(solution)/shard_map/ppermute | solution.py:658
  5.1 0.7 %copy-start = (s32[3]{0:T(128)S(1)}, s32[3]{0:T(128)}, u32[]{:S(2)}) copy-start(s32[3]{0:T(128)} %pml.1) | copy-start | bytes 40
  5.8 15.8 %copy-start.1 = (s32[8]{0:T(128)S(1)}, s32[8]{0:T(128)}, u32[]{:S(2)}) copy-start(s32[8]{0:T(128)} %layer.1) | copy-start | bytes 100
  7.4 9.8 %collective-permute-start.2 = (f32[2,40,128]{2,1,0:T(8,128)S(1)}, f32[2,40,128]{2,1,0:T(8,128)S(1)}, u32[]{:S(2)}, u32[]{:S(2)}) collective-permute-start(f32[2,40,128]{2,1,0:T(8,128)S(1)} %get-tuple-element.56), channel_id=1, source_target_pairs={{1,2},{3,0},{2,1},{0,3},{5,6},{7,4},{6,5},{4,7},{9,10},{11,8},{10,... | collective-permute-start | bytes 122888 | tf_op jit(solution)/shard_map/ppermute | solution.py:668
  10.3 6.9 %collective-permute-start.3 = (f32[2,40,128]{2,1,0:T(8,128)S(1)}, f32[2,40,128]{2,1,0:T(8,128)S(1)}, u32[]{:S(2)}, u32[]{:S(2)}) collective-permute-start(f32[2,40,128]{2,1,0:T(8,128)S(1)} %get-tuple-element.57), channel_id=1, source_target_pairs={{0,1},{2,3},{1,0},{3,2},{4,5},{6,7},{5,4},{7,6},{8,9},{10,11},{9,8... | collective-permute-start | bytes 122888 | tf_op jit(solution)/shard_map/ppermute | solution.py:667
  10.8 12.9 %collective-permute-start.4 = (f32[368,128]{1,0:T(8,128)S(1)}, f32[368,128]{1,0:T(8,128)S(1)}, u32[]{:S(2)}, u32[]{:S(2)}) collective-permute-start(f32[368,128]{1,0:T(8,128)S(1)} %get-tuple-element.65), channel_id=1, source_target_pairs={{16,32},{48,64},{80,96},{112,0},{32,16},{64,48},{96,80},{0,112},{1... | collective-permute-start | bytes 565256 | tf_op jit(solution)/shard_map/ppermute | solution.py:666
  17.2 8.8 %collective-permute-start.5 = (f32[368,128]{1,0:T(8,128)S(1)}, f32[368,128]{1,0:T(8,128)S(1)}, u32[]{:S(2)}, u32[]{:S(2)}) collective-permute-start(f32[368,128]{1,0:T(8,128)S(1)} %get-tuple-element.66), channel_id=1, source_target_pairs={{0,16},{32,48},{64,80},{96,112},{16,0},{48,32},{80,64},{112,96},{1... | collective-permute-start | bytes 565256 | tf_op jit(solution)/shard_map/ppermute | solution.py:665
  17.8 8.3 %collective-permute-start.6 = (f32[40,128]{1,0:T(8,128)S(1)}, f32[40,128]{1,0:T(8,128)S(1)}, u32[]{:S(2)}, u32[]{:S(2)}) collective-permute-start(f32[40,128]{1,0:T(8,128)S(1)} %get-tuple-element.75), channel_id=1, source_target_pairs={{16,32},{48,64},{80,96},{112,0},{32,16},{64,48},{96,80},{0,112},{1... | collective-permute-start | bytes 61448 | tf_op jit(solution)/shard_map/ppermute | solution.py:673
  21.6 5.3 %collective-permute-start.7 = (f32[40,128]{1,0:T(8,128)S(1)}, f32[40,128]{1,0:T(8,128)S(1)}, u32[]{:S(2)}, u32[]{:S(2)}) collective-permute-start(f32[40,128]{1,0:T(8,128)S(1)} %get-tuple-element.76), channel_id=1, source_target_pairs={{0,16},{32,48},{64,80},{96,112},{16,0},{48,32},{80,64},{112,96},{1... | collective-permute-start | bytes 61448 | tf_op jit(solution)/shard_map/ppermute | solution.py:672
  28.3 5.8 %collective-permute-start.8 = (f32[4,32,128]{2,1,0:T(8,128)S(1)}, f32[4,32,128]{2,1,0:T(8,128)S(1)}, u32[]{:S(2)}, u32[]{:S(2)}) collective-permute-start(f32[4,32,128]{2,1,0:T(8,128)S(1)} %get-tuple-element.78), channel_id=1, source_target_pairs={{0,64},{16,80},{32,96},{48,112},{64,0},{80,16},{96,32},{112,48},{1... | collective-permute-start | bytes 196616 | tf_op jit(solution)/shard_map/ppermute | solution.py:692
  29.1 5.1 %collective-permute-start.9 = (f32[4,32,128]{2,1,0:T(8,128)S(1)}, f32[4,32,128]{2,1,0:T(8,128)S(1)}, u32[]{:S(2)}, u32[]{:S(2)}) collective-permute-start(f32[4,32,128]{2,1,0:T(8,128)S(1)} %get-tuple-element.79), channel_id=1, source_target_pairs={{0,32},{16,48},{32,0},{48,16},{64,96},{80,112},{96,64},{112,80},{1... | collective-permute-start | bytes 196616 | tf_op jit(solution)/shard_map/ppermute | solution.py:692
  29.8 5.5 %collective-permute-start.10 = (f32[4,32,128]{2,1,0:T(8,128)S(1)}, f32[4,32,128]{2,1,0:T(8,128)S(1)}, u32[]{:S(2)}, u32[]{:S(2)}) collective-permute-start(f32[4,32,128]{2,1,0:T(8,128)S(1)} %get-tuple-element.80), channel_id=1, source_target_pairs={{0,96},{16,112},{32,64},{48,80},{64,32},{80,48},{96,0},{112,16},{1... | collective-permute-start | bytes 196616 | tf_op jit(solution)/shard_map/ppermute | solution.py:692
  35.3 5.5 %collective-permute-start.11 = (f32[2,32,128]{2,1,0:T(8,128)S(1)}, f32[2,32,128]{2,1,0:T(8,128)S(1)}, u32[]{:S(2)}, u32[]{:S(2)}) collective-permute-start(f32[2,32,128]{2,1,0:T(8,128)S(1)} %get-tuple-element.82), channel_id=1, source_target_pairs={{0,16},{16,0},{32,48},{48,32},{64,80},{80,64},{96,112},{112,96},{1... | collective-permute-start | bytes 98312 | tf_op jit(solution)/shard_map/ppermute | solution.py:694

commit v8 on v7

--- a/solution.py
+++ b/solution.py
@@ -647,6 +647,26 @@
     return pairs + [(b, a) for a, b in pairs]
 
 
+def side_swaps():
+    count, width = lax.axis_size("gy"), lax.axis_size("gx")
+    pairs = []
+    for i in range(count):
+        pairs += [(i * width + j, i * width + j + 1) for j in range(1, width - 1, 2)]
+        if i % 2 == 0:
+            pairs += [(i * width + j, (i + 1) * width + j) for j in (0, width - 1)]
+    return pairs + [(b, a) for a, b in pairs]
+
+
+def depth_swaps():
+    count, width = lax.axis_size("gz"), lax.axis_size("gy")
+    pairs = []
+    for j in range(width):
+        pairs += [(i * width + j, (i + 1) * width + j) for i in range(1, count - 1, 2)]
+        if j % 2 == 0:
+            pairs += [(i * width + j, i * width + j + 1) for i in (0, count - 1)]
+    return pairs + [(b, a) for a, b in pairs]
+
+
 def local(e_start, h_start, adjoint_e, adjoint_h, permittivity, current, layer_of_cell, pml_cells, start_step):
     raw = (e_start, h_start, adjoint_e, adjoint_h, permittivity, current)
     raw = [pltpu.with_memory_space_constraint(a, pltpu.HBM) for a in raw]
@@ -663,14 +683,14 @@
     tiles, strips_rim, xa, xb = call(second_kernel, [(COMPS, PLANES, 8, COLS), (COMPS, 8, COLS), side, side])(yb, ya, right, left)
     za, zb = call(face_kernel, [(FACE_ROWS, COLS)] * 2)(f, tiles, *loss[:3])
     za = lax.ppermute(za, "gz", swaps("gz", 0))
-    zb = lax.ppermute(zb, "gz", swaps("gz", 1))
+    zb = lax.ppermute(zb, ("gz", "gy"), depth_swaps())
     xa = lax.ppermute(xa, "gx", swaps("gx", 0))
-    xb = lax.ppermute(xb, "gx", swaps("gx", 1))
+    xb = lax.ppermute(xb, ("gy", "gx"), side_swaps())
     sides, rim_a, rim_b = call(third_kernel, [(COMPS,) + tall, tall, tall])(
         xb, xa, strips, strips_rim, loss[0], *loss[3:]
     )
     rim_a = lax.ppermute(rim_a, "gz", swaps("gz", 0))
-    rim_b = lax.ppermute(rim_b, "gz", swaps("gz", 1))
+    rim_b = lax.ppermute(rim_b, ("gz", "gy"), depth_swaps())
     state = [(COMPS,) + deep, (6,) + deep, deep, deep]
     mid, out = (3, PLANES // 2) + block, (3, PLANES) + block
     side = [(COMPS,) + tall, (6,) + tall]

time: 41.8 us -> 41.5 us (level)
  starting transfers between devices: 22.6 us -> 22 us
  waiting for transfers between devices: 7.62 us -> 8.19 us
    ppermute x3, starting transfers between devices: 13.1 us -> 0.35 us  [the longest x1 0.18 us: local(): xb = lax.ppermute(xb, ('gy', 'gx'), side_swaps())]
    ppermute x1, starting transfers between devices: 0.01 us -> 4.53 us  [local(): rim_a = lax.ppermute(rim_a, 'gz', swaps('gz', 0))]
    ppermute x1, starting transfers between devices: 0.01 us -> 4.53 us  [local(): za = lax.ppermute(za, 'gz', swaps('gz', 0))]
    ppermute x1, starting transfers between devices: 0.22 us -> 2.97 us  [local(): xa = lax.ppermute(xa, 'gx', swaps('gx', 0))]
    ppermute x3, waiting for transfers between devices: 2.76 us -> 5.14 us  [local(): lax.ppermute(v, 'gz', across('gz', m))]
    ppermute x1, waiting for transfers between devices: 2.27 us -> 0.65 us  [local(): za = lax.ppermute(za, 'gz', swaps('gz', 0))]
    ppermute x3, starting transfers between devices: 4.17 us -> 4.95 us  [local(): lax.ppermute(v, 'gz', across('gz', m))]
    ppermute x1, waiting for transfers between devices: 0.73 us -> 0.07 us  [local(): rim_a = lax.ppermute(rim_a, 'gz', swaps('gz', 0))]
  transfers between devices with their start and end apart: 12 -> 12, of which waited for: 6 -> 7; matrix products, arithmetic and copies ran while one was open for 0% -> 0% of each run, Pallas kernels for 13% -> 13%
where the time goes in v8:
time: 41.5 us; the launch traced here: 41.4 us
  starting transfers between devices  22 us (53%)
  Pallas kernels  9.16 us (22%)
  waiting for transfers between devices  8.19 us (20%)
  between operations  1.4 us (3%)
  local copies, waits for them, and re-layouts  0.65 us (2%)
    pallas_call x11, Pallas kernels, run(): pl.pallas_call(kernel, out_shape=[jax.ShapeDtypeStruct(s, F32) for s in o...  9.16 us
    ppermute x3, waiting for transfers between devices, local(): lax.ppermute(v, 'gz', across('gz', m))  5.14 us
    ppermute x3, starting transfers between devices, local(): lax.ppermute(v, 'gz', across('gz', m))  4.95 us
    ppermute x1, starting transfers between devices, local(): za = lax.ppermute(za, 'gz', swaps('gz', 0))  4.53 us
    ppermute x1, starting transfers between devices, local(): rim_a = lax.ppermute(rim_a, 'gz', swaps('gz', 0))  4.53 us
    ppermute x1, starting transfers between devices, local(): xa = lax.ppermute(xa, 'gx', swaps('gx', 0))  2.97 us
    ppermute x1, starting transfers between devices, local(): lax.ppermute(sent, 'gz', across('gz', 1))  2.43 us
    ppermute x1, waiting for transfers between devices, local(): lax.ppermute(sent, 'gz', across('gz', 1))  2.14 us
  transfers between devices with their start and end apart: 12, of which 7 were waited for; matrix products, arithmetic and copies ran while one was open for 0% of the time, Pallas kernels for 13%

profile of v8, /device:TPU:0, one launch (start us, length us, event | category | flops | bytes accessed | tf_op | source)
XLA Modules:
  0.0 41.4 jit_solution(15518082294900564880)
XLA Ops:
  0.6 1.6 %shard_map.112 = (f32[14,12,40,128]{3,2,1,0:T(8,128)S(1)}, f32[224,128]{1,0:T(8,128)S(1)}, f32[224,128]{1,0:T(8,128)S(1)}) custom-call(f32[3,8,32,128]{3,2,1,0:T(8,128)} %e.1, f32[3,8,32,128]{3,2,1,0:T(8,128)} %h.1, f32[3,8,32,128]{3,2,1,0:T(8,128)} %ae.1, f32[3,8,32,128]{3,2,1,0:T(8,128)} %ah.1, f32[8,32,128]{2,1,0:T(8,128)} %eps.1, f32[8,32,128]{2,1,0:T(8,128)} %cur.1), custom_call_target="tpu_custom_call" | custom-call | flops 1000000 | bytes 5505024 | tf_op jit(solution)/shard_map/pallas_call | solution.py:616
  2.3 1.7 %collective-permute-start = (f32[224,128]{1,0:T(8,128)S(1)}, f32[224,128]{1,0:T(8,128)S(1)}, u32[]{:S(2)}, u32[]{:S(2)}) collective-permute-start(f32[224,128]{1,0:T(8,128)S(1)} %get-tuple-element.52), channel_id=1, source_target_pairs={{4,8},{0,1},{12,13},{5,9},{6,10},{2,3},{14,15},{7,11},{8,4},{1,0},... | collective-permute-start | bytes 344072 | tf_op jit(solution)/shard_map/ppermute | solution.py:677
  3.9 0.5 %collective-permute-start.1 = (f32[224,128]{1,0:T(8,128)S(1)}, f32[224,128]{1,0:T(8,128)S(1)}, u32[]{:S(2)}, u32[]{:S(2)}) collective-permute-start(f32[224,128]{1,0:T(8,128)S(1)} %get-tuple-element.53), channel_id=1, source_target_pairs={{0,4},{8,12},{4,0},{12,8},{1,5},{9,13},{5,1},{13,9},{2,6},{10,14},... | collective-permute-start | bytes 344072 | tf_op jit(solution)/shard_map/ppermute | solution.py:678
  5.1 0.0 copy-start
  5.1 0.6 %copy-done = s32[3]{0:T(128)S(1)} copy-done((s32[3]{0:T(128)S(1)}, s32[3]{0:T(128)}, u32[]{:S(2)}) %copy-start) | copy-done | bytes 36
  5.8 0.0 copy-start.1
  5.8 1.2 %shard_map.113 = (f32[14,32,128]{2,1,0:T(8,128)S(1)}, f32[2,32,128]{2,1,0:T(8,128)S(1)}, f32[2,32,128]{2,1,0:T(8,128)S(1)}, f32[2,8,128]{2,1,0:T(8,128)S(1)}, f3...) custom-call(s32[1]{0:T(128)S(6)} %copy.24.start, ...), custom_call_target="tpu_custom_call" | custom-call | flops 1000000 | bytes 4276240 | tf_op jit(solution)/shard_map/pallas_call | solution.py:616
  7.0 0.2 collective-permute-done.yb
  7.2 0.0 collective-permute-done.1.ya
  7.2 0.3 shard_map.114
  7.4 0.2 collective-permute-start.2
  7.6 3.0 %collective-permute-start.3 = (f32[2,40,128]{2,1,0:T(8,128)S(1)}, f32[2,40,128]{2,1,0:T(8,128)S(1)}, u32[]{:S(2)}, u32[]{:S(2)}) collective-permute-start(f32[2,40,128]{2,1,0:T(8,128)S(1)} %get-tuple-element.57), channel_id=1, source_target_pairs={{0,1},{2,3},{1,0},{3,2},{4,5},{6,7},{5,4},{7,6},{8,9},{10,11},{9,8... | collective-permute-start | bytes 122888 | tf_op jit(solution)/shard_map/ppermute | solution.py:687
  10.6 0.2 shard_map.117
  10.8 0.1 collective-permute-start.4
  10.9 4.5 %collective-permute-start.5 = (f32[368,128]{1,0:T(8,128)S(1)}, f32[368,128]{1,0:T(8,128)S(1)}, u32[]{:S(2)}, u32[]{:S(2)}) collective-permute-start(f32[368,128]{1,0:T(8,128)S(1)} %get-tuple-element.66), channel_id=1, source_target_pairs={{0,16},{32,48},{64,80},{96,112},{16,0},{48,32},{80,64},{112,96},{1... | collective-permute-start | bytes 565256 | tf_op jit(solution)/shard_map/ppermute | solution.py:685
  15.4 0.0 collective-permute-done.2.xb
  15.4 0.0 collective-permute-done.3.xa
  15.4 0.6 %shard_map.115 = (f32[14,40,128]{2,1,0:T(8,128)S(1)}, f32[40,128]{1,0:T(8,128)S(1)}, f32[40,128]{1,0:T(8,128)S(1)}) custom-call(f32[2,40,128]{2,1,0:T(8,128)S(1)} %collective-permute-done.2.xb, f32[2,40,128]{2,1,0:T(8,128)S(1)} %collective-permute-done.3.xa, f32[14,32,128]{2,1,0:T(8,128)S(1)} %get-tuple-element.58.strips, ...), custom_call_target="tpu_custom_call" | custom-call | flops 1000000 | bytes 745472 | tf_op jit(solution)/shard_map/pallas_call | solution.py:616
  16.0 0.1 collective-permute-start.6
  16.1 4.5 %collective-permute-start.7 = (f32[40,128]{1,0:T(8,128)S(1)}, f32[40,128]{1,0:T(8,128)S(1)}, u32[]{:S(2)}, u32[]{:S(2)}) collective-permute-start(f32[40,128]{1,0:T(8,128)S(1)} %get-tuple-element.76), channel_id=1, source_target_pairs={{0,16},{32,48},{64,80},{96,112},{16,0},{48,32},{80,64},{112,96},{1... | collective-permute-start | bytes 61448 | tf_op jit(solution)/shard_map/ppermute | solution.py:692
  20.7 0.0 copy-done.1
  20.7 2.1 %shard_map.116 = (f32[14,12,40,128]{3,2,1,0:T(8,128)S(1)}, f32[6,12,40,128]{3,2,1,0:T(8,128)S(1)}, f32[12,40,128]{2,1,0:T(8,128)S(1)}, f32[12,40,128]{2,1,0:T(8,...) custom-call(s32[8]{0:T(128)S(1)} %copy-done.1, ...), custom_call_target="tpu_custom_call", output_to_operand_aliasing={{0}: (6, {})} | custom-call | flops 99999997952 | bytes 10805280 | tf_op jit(solution)/shard_map/pallas_call | solution.py:616
  22.8 0.0 collective-permute-done.4.zb
  22.8 0.7 %collective-permute-done.5.za = f32[368,128]{1,0:T(8,128)S(1)} collective-permute-done((f32[368,128]{1,0:T(8,128)S(1)}, f32[368,128]{1,0:T(8,128)S(1)}, u32[]{:S(2)}, u32[]{:S(2)}) %collective-permute-start.5) | collective-permute-done | bytes 188448 | tf_op jit(solution)/shard_map/ppermute | solution.py:685
  23.5 0.1 shard_map.118
  23.6 0.0 collective-permute-done.6.rim_b
  23.6 0.1 collective-permute-done.7.rim_a
  23.7 1.4 %shard_map.119 = (f32[14,12,40,128]{3,2,1,0:T(8,128)S(1)}, f32[6,12,40,128]{3,2,1,0:T(8,128)S(1)}, f32[3,4,32,128]{3,2,1,0:T(8,128)S(1)}, f32[3,4,32,128]{3,2,1,...) custom-call(f32[2,8,128]{2,1,0:T(8,128)S(1)} %get-tuple-element.47.f, ...), custom_call_target="tpu_custom_call", output_to_operand_aliasing={{0}: (4, {}), {1}: (5, {})} | custom-call | flops 1000000 | bytes 12288000 | tf_op jit(solution)/shard_map/pallas_call | solution.py:616
  25.1 3.9 %collective-permute-start.8 = (f32[4,32,128]{2,1,0:T(8,128)S(1)}, f32[4,32,128]{2,1,0:T(8,128)S(1)}, u32[]{:S(2)}, u32[]{:S(2)}) collective-permute-start(f32[4,32,128]{2,1,0:T(8,128)S(1)} %get-tuple-element.78), channel_id=1, source_target_pairs={{0,64},{16,80},{32,96},{48,112},{64,0},{80,16},{96,32},{112,48},{1... | collective-permute-start | bytes 196616 | tf_op jit(solution)/shard_map/ppermute | solution.py:712
  29.0 0.7 %collective-permute-start.9 = (f32[4,32,128]{2,1,0:T(8,128)S(1)}, f32[4,32,128]{2,1,0:T(8,128)S(1)}, u32[]{:S(2)}, u32[]{:S(2)}) collective-permute-start(f32[4,32,128]{2,1,0:T(8,128)S(1)} %get-tuple-element.79), channel_id=1, source_target_pairs={{0,32},{16,48},{32,0},{48,16},{64,96},{80,112},{96,64},{112,80},{1... | collective-permute-start | bytes 196616 | tf_op jit(solution)/shard_map/ppermute | solution.py:712
  29.7 0.3 collective-permute-start.10
  30.1 1.2 %collective-permute-done.8.second = f32[4,32,128]{2,1,0:T(8,128)S(1)} collective-permute-done((f32[4,32,128]{2,1,0:T(8,128)S(1)}, f32[4,32,128]{2,1,0:T(8,128)S(1)}, u32[]{:S(2)}, u32[]{:S(2)}) %collective-permute-start.8) | collective-permute-done | bytes 65568 | tf_op jit(solution)/shard_map/ppermute | solution.py:712
  31.3 2.0 %collective-permute-done.9.first = f32[4,32,128]{2,1,0:T(8,128)S(1)} collective-permute-done((f32[4,32,128]{2,1,0:T(8,128)S(1)}, f32[4,32,128]{2,1,0:T(8,128)S(1)}, u32[]{:S(2)}, u32[]{:S(2)}) %collective-permute-start.9) | collective-permute-done | bytes 65568 | tf_op jit(solution)/shard_map/ppermute | solution.py:712
  33.3 1.9 %collective-permute-done.10.third = f32[4,32,128]{2,1,0:T(8,128)S(1)} collective-permute-done((f32[4,32,128]{2,1,0:T(8,128)S(1)}, f32[4,32,128]{2,1,0:T(8,128)S(1)}, u32[]{:S(2)}, u32[]{:S(2)}) %collective-permute-start.10) | collective-permute-done | bytes 65568 | tf_op jit(solution)/shard_map/ppermute | solution.py:712
  35.2 2.4 %collective-permute-start.11 = (f32[2,32,128]{2,1,0:T(8,128)S(1)}, f32[2,32,128]{2,1,0:T(8,128)S(1)}, u32[]{:S(2)}, u32[]{:S(2)}) collective-permute-start(f32[2,32,128]{2,1,0:T(8,128)S(1)} %get-tuple-element.82), channel_id=1, source_target_pairs={{0,16},{16,0},{32,48},{48,32},{64,80},{80,64},{96,112},{112,96},{1... | collective-permute-start | bytes 98312 | tf_op jit(solution)/shard_map/ppermute | solution.py:714
  37.7 0.9 %shard_map.122 = (f32[3,8,32,128]{3,2,1,0:T(8,128)}, f32[3,8,32,128]{3,2,1,0:T(8,128)}) custom-call(f32[3,4,32,128]{3,2,1,0:T(8,128)S(1)} %get-tuple-element.83.e_mid, f32[3,4,32,128]{3,2,1,0:T(8,128)S(1)} %get-tuple-element.84.h_mid, f32[3,4,32,128]{3,2,1,0:T(8,128)S(1)} %get-tuple-element.85.e_rest, f32[3,4,32,128]{3,2,1,0:T(8,128)S(1)} %get-tuple-element.86.h_rest), custom_call_target="tpu_custom_call" | custom-call | flops 1000000 | bytes 1572864 | tf_op jit(solution)/shard_map/pallas_call | solution.py:616
  38.6 2.1 %collective-permute-done.11.got = f32[2,32,128]{2,1,0:T(8,128)S(1)} collective-permute-done((f32[2,32,128]{2,1,0:T(8,128)S(1)}, f32[2,32,128]{2,1,0:T(8,128)S(1)}, u32[]{:S(2)}, u32[]{:S(2)}) %collective-permute-start.11) | collective-permute-done | bytes 32800 | tf_op jit(solution)/shard_map/ppermute | solution.py:714
  40.7 0.6 %shard_map.121 = f32[2,32,128]{2,1,0:T(8,128)} custom-call(f32[2,32,128]{2,1,0:T(8,128)S(1)} %get-tuple-element.81.kept, f32[2,32,128]{2,1,0:T(8,128)S(1)} %collective-permute-done.11.got), custom_call_target="tpu_custom_call" | custom-call | flops 1000000 | bytes 98304 | tf_op jit(solution)/shard_map/pallas_call | solution.py:616
  (1 shorter events, 0.0 us)
Async XLA Ops:
  2.3 4.9 %collective-permute-start = (f32[224,128]{1,0:T(8,128)S(1)}, f32[224,128]{1,0:T(8,128)S(1)}, u32[]{:S(2)}, u32[]{:S(2)}) collective-permute-start(f32[224,128]{1,0:T(8,128)S(1)} %get-tuple-element.52), channel_id=1, source_target_pairs={{4,8},{0,1},{12,13},{5,9},{6,10},{2,3},{14,15},{7,11},{8,4},{1,0},... | collective-permute-start | bytes 344072 | tf_op jit(solution)/shard_map/ppermute | solution.py:677
  3.9 3.2 %collective-permute-start.1 = (f32[224,128]{1,0:T(8,128)S(1)}, f32[224,128]{1,0:T(8,128)S(1)}, u32[]{:S(2)}, u32[]{:S(2)}) collective-permute-start(f32[224,128]{1,0:T(8,128)S(1)} %get-tuple-element.53), channel_id=1, source_target_pairs={{0,4},{8,12},{4,0},{12,8},{1,5},{9,13},{5,1},{13,9},{2,6},{10,14},... | collective-permute-start | bytes 344072 | tf_op jit(solution)/shard_map/ppermute | solution.py:678
  5.1 0.7 %copy-start = (s32[3]{0:T(128)S(1)}, s32[3]{0:T(128)}, u32[]{:S(2)}) copy-start(s32[3]{0:T(128)} %pml.1) | copy-start | bytes 40
  5.8 14.9 %copy-start.1 = (s32[8]{0:T(128)S(1)}, s32[8]{0:T(128)}, u32[]{:S(2)}) copy-start(s32[8]{0:T(128)} %layer.1) | copy-start | bytes 100
  7.4 8.0 %collective-permute-start.2 = (f32[2,40,128]{2,1,0:T(8,128)S(1)}, f32[2,40,128]{2,1,0:T(8,128)S(1)}, u32[]{:S(2)}, u32[]{:S(2)}) collective-permute-start(f32[2,40,128]{2,1,0:T(8,128)S(1)} %get-tuple-element.56), channel_id=1, source_target_pairs={{1,2},{0,4},{3,7},{5,6},{9,10},{8,12},{11,15},{13,14},{2,1},{4,0},... | collective-permute-start | bytes 122888 | tf_op jit(solution)/shard_map/ppermute | solution.py:688
  7.6 7.8 %collective-permute-start.3 = (f32[2,40,128]{2,1,0:T(8,128)S(1)}, f32[2,40,128]{2,1,0:T(8,128)S(1)}, u32[]{:S(2)}, u32[]{:S(2)}) collective-permute-start(f32[2,40,128]{2,1,0:T(8,128)S(1)} %get-tuple-element.57), channel_id=1, source_target_pairs={{0,1},{2,3},{1,0},{3,2},{4,5},{6,7},{5,4},{7,6},{8,9},{10,11},{9,8... | collective-permute-start | bytes 122888 | tf_op jit(solution)/shard_map/ppermute | solution.py:687
  10.8 12.0 %collective-permute-start.4 = (f32[368,128]{1,0:T(8,128)S(1)}, f32[368,128]{1,0:T(8,128)S(1)}, u32[]{:S(2)}, u32[]{:S(2)}) collective-permute-start(f32[368,128]{1,0:T(8,128)S(1)} %get-tuple-element.65), channel_id=1, source_target_pairs={{16,32},{48,64},{80,96},{0,4},{112,116},{20,36},{52,68},{84,100},{... | collective-permute-start | bytes 565256 | tf_op jit(solution)/shard_map/ppermute | solution.py:686
  10.9 12.5 %collective-permute-start.5 = (f32[368,128]{1,0:T(8,128)S(1)}, f32[368,128]{1,0:T(8,128)S(1)}, u32[]{:S(2)}, u32[]{:S(2)}) collective-permute-start(f32[368,128]{1,0:T(8,128)S(1)} %get-tuple-element.66), channel_id=1, source_target_pairs={{0,16},{32,48},{64,80},{96,112},{16,0},{48,32},{80,64},{112,96},{1... | collective-permute-start | bytes 565256 | tf_op jit(solution)/shard_map/ppermute | solution.py:685
  16.0 7.6 %collective-permute-start.6 = (f32[40,128]{1,0:T(8,128)S(1)}, f32[40,128]{1,0:T(8,128)S(1)}, u32[]{:S(2)}, u32[]{:S(2)}) collective-permute-start(f32[40,128]{1,0:T(8,128)S(1)} %get-tuple-element.75), channel_id=1, source_target_pairs={{16,32},{48,64},{80,96},{0,4},{112,116},{20,36},{52,68},{84,100},{... | collective-permute-start | bytes 61448 | tf_op jit(solution)/shard_map/ppermute | solution.py:693
  16.1 7.5 %collective-permute-start.7 = (f32[40,128]{1,0:T(8,128)S(1)}, f32[40,128]{1,0:T(8,128)S(1)}, u32[]{:S(2)}, u32[]{:S(2)}) collective-permute-start(f32[40,128]{1,0:T(8,128)S(1)} %get-tuple-element.76), channel_id=1, source_target_pairs={{0,16},{32,48},{64,80},{96,112},{16,0},{48,32},{80,64},{112,96},{1... | collective-permute-start | bytes 61448 | tf_op jit(solution)/shard_map/ppermute | solution.py:692
  25.1 6.1 %collective-permute-start.8 = (f32[4,32,128]{2,1,0:T(8,128)S(1)}, f32[4,32,128]{2,1,0:T(8,128)S(1)}, u32[]{:S(2)}, u32[]{:S(2)}) collective-permute-start(f32[4,32,128]{2,1,0:T(8,128)S(1)} %get-tuple-element.78), channel_id=1, source_target_pairs={{0,64},{16,80},{32,96},{48,112},{64,0},{80,16},{96,32},{112,48},{1... | collective-permute-start | bytes 196616 | tf_op jit(solution)/shard_map/ppermute | solution.py:712
  29.0 4.3 %collective-permute-start.9 = (f32[4,32,128]{2,1,0:T(8,128)S(1)}, f32[4,32,128]{2,1,0:T(8,128)S(1)}, u32[]{:S(2)}, u32[]{:S(2)}) collective-permute-start(f32[4,32,128]{2,1,0:T(8,128)S(1)} %get-tuple-element.79), channel_id=1, source_target_pairs={{0,32},{16,48},{32,0},{48,16},{64,96},{80,112},{96,64},{112,80},{1... | collective-permute-start | bytes 196616 | tf_op jit(solution)/shard_map/ppermute | solution.py:712
  29.7 5.5 %collective-permute-start.10 = (f32[4,32,128]{2,1,0:T(8,128)S(1)}, f32[4,32,128]{2,1,0:T(8,128)S(1)}, u32[]{:S(2)}, u32[]{:S(2)}) collective-permute-start(f32[4,32,128]{2,1,0:T(8,128)S(1)} %get-tuple-element.80), channel_id=1, source_target_pairs={{0,96},{16,112},{32,64},{48,80},{64,32},{80,48},{96,0},{112,16},{1... | collective-permute-start | bytes 196616 | tf_op jit(solution)/shard_map/ppermute | solution.py:712
  35.2 5.5 %collective-permute-start.11 = (f32[2,32,128]{2,1,0:T(8,128)S(1)}, f32[2,32,128]{2,1,0:T(8,128)S(1)}, u32[]{:S(2)}, u32[]{:S(2)}) collective-permute-start(f32[2,32,128]{2,1,0:T(8,128)S(1)} %get-tuple-element.82), channel_id=1, source_target_pairs={{0,16},{16,0},{32,48},{48,32},{64,80},{80,64},{96,112},{112,96},{1... | collective-permute-start | bytes 98312 | tf_op jit(solution)/shard_map/ppermute | solution.py:714

commit v9 on v8

--- a/solution.py
+++ b/solution.py
@@ -306,7 +306,7 @@
     zb[...] = jnp.where(even, sent[1], sent[0])
 
 
-def third_kernel(xb, xa, strips, strips_rim, factors, xr, xs, sides, rim_a, rim_b):
+def third_kernel(xa, xb, strips, strips_rim, factors, xr, xs, sides, rim_a, rim_b):
     index = lax.axis_index("gx")
     even = parity("gx")
     has_after = (index < lax.axis_size("gx") - 1).astype(F32)
@@ -687,7 +687,7 @@
     xa = lax.ppermute(xa, "gx", swaps("gx", 0))
     xb = lax.ppermute(xb, ("gy", "gx"), side_swaps())
     sides, rim_a, rim_b = call(third_kernel, [(COMPS,) + tall, tall, tall])(
-        xb, xa, strips, strips_rim, loss[0], *loss[3:]
+        xa, xb, strips, strips_rim, loss[0], *loss[3:]
     )
     rim_a = lax.ppermute(rim_a, "gz", swaps("gz", 0))
     rim_b = lax.ppermute(rim_b, ("gz", "gy"), depth_swaps())

time: 41.5 us -> 41.1 us (level)
  starting transfers between devices: 22 us -> 20.5 us
  waiting for transfers between devices: 8.19 us -> 9.15 us
    ppermute x1, starting transfers between devices: 2.97 us -> 1.65 us  [local(): xa = lax.ppermute(xa, 'gx', swaps('gx', 0))]
    ppermute x1, waiting for transfers between devices: 0.65 us -> 1.71 us  [local(): za = lax.ppermute(za, 'gz', swaps('gz', 0))]
    ppermute x1, starting transfers between devices: 0.09 us -> 0.59 us  [local(): zb = lax.ppermute(zb, ('gz', 'gy'), depth_swaps())]
    ppermute x1, starting transfers between devices: 4.53 us -> 4.04 us  [local(): za = lax.ppermute(za, 'gz', swaps('gz', 0))]
where the time goes in v9:
time: 41.1 us; the launch traced here: 40.9 us
  starting transfers between devices  20.5 us (50%)
  Pallas kernels  9.16 us (22%)
  waiting for transfers between devices  9.15 us (22%)
  between operations  1.39 us (3%)
  local copies, waits for them, and re-layouts  0.65 us (2%)
    pallas_call x11, Pallas kernels, run(): pl.pallas_call(kernel, out_shape=[jax.ShapeDtypeStruct(s, F32) for s in o...  9.16 us
    ppermute x3, waiting for transfers between devices, local(): lax.ppermute(v, 'gz', across('gz', m))  5.09 us
    ppermute x3, starting transfers between devices, local(): lax.ppermute(v, 'gz', across('gz', m))  4.95 us
    ppermute x1, starting transfers between devices, local(): rim_a = lax.ppermute(rim_a, 'gz', swaps('gz', 0))  4.53 us
    ppermute x1, starting transfers between devices, local(): za = lax.ppermute(za, 'gz', swaps('gz', 0))  4.04 us
    ppermute x1, starting transfers between devices, local(): lax.ppermute(sent, 'gz', across('gz', 1))  2.48 us
    ppermute x1, waiting for transfers between devices, local(): lax.ppermute(sent, 'gz', across('gz', 1))  2.1 us
    ppermute x1, waiting for transfers between devices, local(): za = lax.ppermute(za, 'gz', swaps('gz', 0))  1.71 us
  transfers between devices with their start and end apart: 12, of which 7 were waited for; matrix products, arithmetic and copies ran while one was open for 0% of the time, Pallas kernels for 13%

profile of v9, /device:TPU:0, one launch (start us, length us, event | category | flops | bytes accessed | tf_op | source)
XLA Modules:
  0.0 40.9 jit_solution(1593322423640832595)
XLA Ops:
  0.6 1.6 %shard_map.112 = (f32[14,12,40,128]{3,2,1,0:T(8,128)S(1)}, f32[224,128]{1,0:T(8,128)S(1)}, f32[224,128]{1,0:T(8,128)S(1)}) custom-call(f32[3,8,32,128]{3,2,1,0:T(8,128)} %e.1, f32[3,8,32,128]{3,2,1,0:T(8,128)} %h.1, f32[3,8,32,128]{3,2,1,0:T(8,128)} %ae.1, f32[3,8,32,128]{3,2,1,0:T(8,128)} %ah.1, f32[8,32,128]{2,1,0:T(8,128)} %eps.1, f32[8,32,128]{2,1,0:T(8,128)} %cur.1), custom_call_target="tpu_custom_call" | custom-call | flops 1000000 | bytes 5505024 | tf_op jit(solution)/shard_map/pallas_call | solution.py:616
  2.3 1.7 %collective-permute-start = (f32[224,128]{1,0:T(8,128)S(1)}, f32[224,128]{1,0:T(8,128)S(1)}, u32[]{:S(2)}, u32[]{:S(2)}) collective-permute-start(f32[224,128]{1,0:T(8,128)S(1)} %get-tuple-element.52), channel_id=1, source_target_pairs={{4,8},{0,1},{12,13},{5,9},{6,10},{2,3},{14,15},{7,11},{8,4},{1,0},... | collective-permute-start | bytes 344072 | tf_op jit(solution)/shard_map/ppermute | solution.py:677
  3.9 0.5 %collective-permute-start.1 = (f32[224,128]{1,0:T(8,128)S(1)}, f32[224,128]{1,0:T(8,128)S(1)}, u32[]{:S(2)}, u32[]{:S(2)}) collective-permute-start(f32[224,128]{1,0:T(8,128)S(1)} %get-tuple-element.53), channel_id=1, source_target_pairs={{0,4},{8,12},{4,0},{12,8},{1,5},{9,13},{5,1},{13,9},{2,6},{10,14},... | collective-permute-start | bytes 344072 | tf_op jit(solution)/shard_map/ppermute | solution.py:678
  5.1 0.0 copy-start
  5.1 0.6 %copy-done = s32[3]{0:T(128)S(1)} copy-done((s32[3]{0:T(128)S(1)}, s32[3]{0:T(128)}, u32[]{:S(2)}) %copy-start) | copy-done | bytes 36
  5.8 0.0 copy-start.1
  5.8 1.2 %shard_map.113 = (f32[14,32,128]{2,1,0:T(8,128)S(1)}, f32[2,32,128]{2,1,0:T(8,128)S(1)}, f32[2,32,128]{2,1,0:T(8,128)S(1)}, f32[2,8,128]{2,1,0:T(8,128)S(1)}, f3...) custom-call(s32[1]{0:T(128)S(6)} %copy.24.start, ...), custom_call_target="tpu_custom_call" | custom-call | flops 1000000 | bytes 4276240 | tf_op jit(solution)/shard_map/pallas_call | solution.py:616
  7.0 0.2 collective-permute-done.yb
  7.2 0.0 collective-permute-done.1.ya
  7.2 0.3 shard_map.114
  7.4 1.7 %collective-permute-start.2 = (f32[2,40,128]{2,1,0:T(8,128)S(1)}, f32[2,40,128]{2,1,0:T(8,128)S(1)}, u32[]{:S(2)}, u32[]{:S(2)}) collective-permute-start(f32[2,40,128]{2,1,0:T(8,128)S(1)} %get-tuple-element.56), channel_id=1, source_target_pairs={{0,1},{2,3},{1,0},{3,2},{4,5},{6,7},{5,4},{7,6},{8,9},{10,11},{9,8... | collective-permute-start | bytes 122888 | tf_op jit(solution)/shard_map/ppermute | solution.py:687
  9.1 0.0 collective-permute-start.3
  9.1 0.2 shard_map.117
  9.3 0.6 %collective-permute-start.4 = (f32[368,128]{1,0:T(8,128)S(1)}, f32[368,128]{1,0:T(8,128)S(1)}, u32[]{:S(2)}, u32[]{:S(2)}) collective-permute-start(f32[368,128]{1,0:T(8,128)S(1)} %get-tuple-element.65), channel_id=1, source_target_pairs={{16,32},{48,64},{80,96},{0,4},{112,116},{20,36},{52,68},{84,100},{... | collective-permute-start | bytes 565256 | tf_op jit(solution)/shard_map/ppermute | solution.py:686
  9.9 4.0 %collective-permute-start.5 = (f32[368,128]{1,0:T(8,128)S(1)}, f32[368,128]{1,0:T(8,128)S(1)}, u32[]{:S(2)}, u32[]{:S(2)}) collective-permute-start(f32[368,128]{1,0:T(8,128)S(1)} %get-tuple-element.66), channel_id=1, source_target_pairs={{0,16},{32,48},{64,80},{96,112},{16,0},{48,32},{80,64},{112,96},{1... | collective-permute-start | bytes 565256 | tf_op jit(solution)/shard_map/ppermute | solution.py:685
  13.9 0.0 collective-permute-done.2.xa
  14.0 0.0 collective-permute-done.3.xb
  14.0 0.6 %shard_map.115 = (f32[14,40,128]{2,1,0:T(8,128)S(1)}, f32[40,128]{1,0:T(8,128)S(1)}, f32[40,128]{1,0:T(8,128)S(1)}) custom-call(f32[2,40,128]{2,1,0:T(8,128)S(1)} %collective-permute-done.2.xa, f32[2,40,128]{2,1,0:T(8,128)S(1)} %collective-permute-done.3.xb, f32[14,32,128]{2,1,0:T(8,128)S(1)} %get-tuple-element.58.strips, ...), custom_call_target="tpu_custom_call" | custom-call | flops 1000000 | bytes 745472 | tf_op jit(solution)/shard_map/pallas_call | solution.py:616
  14.6 0.1 collective-permute-start.6
  14.6 4.5 %collective-permute-start.7 = (f32[40,128]{1,0:T(8,128)S(1)}, f32[40,128]{1,0:T(8,128)S(1)}, u32[]{:S(2)}, u32[]{:S(2)}) collective-permute-start(f32[40,128]{1,0:T(8,128)S(1)} %get-tuple-element.76), channel_id=1, source_target_pairs={{0,16},{32,48},{64,80},{96,112},{16,0},{48,32},{80,64},{112,96},{1... | collective-permute-start | bytes 61448 | tf_op jit(solution)/shard_map/ppermute | solution.py:692
  19.2 0.0 copy-done.1
  19.2 2.1 %shard_map.116 = (f32[14,12,40,128]{3,2,1,0:T(8,128)S(1)}, f32[6,12,40,128]{3,2,1,0:T(8,128)S(1)}, f32[12,40,128]{2,1,0:T(8,128)S(1)}, f32[12,40,128]{2,1,0:T(8,...) custom-call(s32[8]{0:T(128)S(1)} %copy-done.1, ...), custom_call_target="tpu_custom_call", output_to_operand_aliasing={{0}: (6, {})} | custom-call | flops 99999997952 | bytes 10805280 | tf_op jit(solution)/shard_map/pallas_call | solution.py:616
  21.3 0.0 collective-permute-done.4.zb
  21.3 1.7 %collective-permute-done.5.za = f32[368,128]{1,0:T(8,128)S(1)} collective-permute-done((f32[368,128]{1,0:T(8,128)S(1)}, f32[368,128]{1,0:T(8,128)S(1)}, u32[]{:S(2)}, u32[]{:S(2)}) %collective-permute-start.5) | collective-permute-done | bytes 188448 | tf_op jit(solution)/shard_map/ppermute | solution.py:685
  23.0 0.1 shard_map.118
  23.2 0.0 collective-permute-done.6.rim_b
  23.2 0.1 collective-permute-done.7.rim_a
  23.2 1.4 %shard_map.119 = (f32[14,12,40,128]{3,2,1,0:T(8,128)S(1)}, f32[6,12,40,128]{3,2,1,0:T(8,128)S(1)}, f32[3,4,32,128]{3,2,1,0:T(8,128)S(1)}, f32[3,4,32,128]{3,2,1,...) custom-call(f32[2,8,128]{2,1,0:T(8,128)S(1)} %get-tuple-element.47.f, ...), custom_call_target="tpu_custom_call", output_to_operand_aliasing={{0}: (4, {}), {1}: (5, {})} | custom-call | flops 1000000 | bytes 12288000 | tf_op jit(solution)/shard_map/pallas_call | solution.py:616
  24.7 3.9 %collective-permute-start.8 = (f32[4,32,128]{2,1,0:T(8,128)S(1)}, f32[4,32,128]{2,1,0:T(8,128)S(1)}, u32[]{:S(2)}, u32[]{:S(2)}) collective-permute-start(f32[4,32,128]{2,1,0:T(8,128)S(1)} %get-tuple-element.78), channel_id=1, source_target_pairs={{0,64},{16,80},{32,96},{48,112},{64,0},{80,16},{96,32},{112,48},{1... | collective-permute-start | bytes 196616 | tf_op jit(solution)/shard_map/ppermute | solution.py:712
  28.6 0.7 %collective-permute-start.9 = (f32[4,32,128]{2,1,0:T(8,128)S(1)}, f32[4,32,128]{2,1,0:T(8,128)S(1)}, u32[]{:S(2)}, u32[]{:S(2)}) collective-permute-start(f32[4,32,128]{2,1,0:T(8,128)S(1)} %get-tuple-element.79), channel_id=1, source_target_pairs={{0,32},{16,48},{32,0},{48,16},{64,96},{80,112},{96,64},{112,80},{1... | collective-permute-start | bytes 196616 | tf_op jit(solution)/shard_map/ppermute | solution.py:712
  29.3 0.4 collective-permute-start.10
  29.6 1.2 %collective-permute-done.8.second = f32[4,32,128]{2,1,0:T(8,128)S(1)} collective-permute-done((f32[4,32,128]{2,1,0:T(8,128)S(1)}, f32[4,32,128]{2,1,0:T(8,128)S(1)}, u32[]{:S(2)}, u32[]{:S(2)}) %collective-permute-start.8) | collective-permute-done | bytes 65568 | tf_op jit(solution)/shard_map/ppermute | solution.py:712
  30.9 2.0 %collective-permute-done.9.first = f32[4,32,128]{2,1,0:T(8,128)S(1)} collective-permute-done((f32[4,32,128]{2,1,0:T(8,128)S(1)}, f32[4,32,128]{2,1,0:T(8,128)S(1)}, u32[]{:S(2)}, u32[]{:S(2)}) %collective-permute-start.9) | collective-permute-done | bytes 65568 | tf_op jit(solution)/shard_map/ppermute | solution.py:712
  32.9 1.8 %collective-permute-done.10.third = f32[4,32,128]{2,1,0:T(8,128)S(1)} collective-permute-done((f32[4,32,128]{2,1,0:T(8,128)S(1)}, f32[4,32,128]{2,1,0:T(8,128)S(1)}, u32[]{:S(2)}, u32[]{:S(2)}) %collective-permute-start.10) | collective-permute-done | bytes 65568 | tf_op jit(solution)/shard_map/ppermute | solution.py:712
  34.8 2.5 %collective-permute-start.11 = (f32[2,32,128]{2,1,0:T(8,128)S(1)}, f32[2,32,128]{2,1,0:T(8,128)S(1)}, u32[]{:S(2)}, u32[]{:S(2)}) collective-permute-start(f32[2,32,128]{2,1,0:T(8,128)S(1)} %get-tuple-element.82), channel_id=1, source_target_pairs={{0,16},{16,0},{32,48},{48,32},{64,80},{80,64},{96,112},{112,96},{1... | collective-permute-start | bytes 98312 | tf_op jit(solution)/shard_map/ppermute | solution.py:714
  37.2 0.9 %shard_map.122 = (f32[3,8,32,128]{3,2,1,0:T(8,128)}, f32[3,8,32,128]{3,2,1,0:T(8,128)}) custom-call(f32[3,4,32,128]{3,2,1,0:T(8,128)S(1)} %get-tuple-element.83.e_mid, f32[3,4,32,128]{3,2,1,0:T(8,128)S(1)} %get-tuple-element.84.h_mid, f32[3,4,32,128]{3,2,1,0:T(8,128)S(1)} %get-tuple-element.85.e_rest, f32[3,4,32,128]{3,2,1,0:T(8,128)S(1)} %get-tuple-element.86.h_rest), custom_call_target="tpu_custom_call" | custom-call | flops 1000000 | bytes 1572864 | tf_op jit(solution)/shard_map/pallas_call | solution.py:616
  38.2 2.1 %collective-permute-done.11.got = f32[2,32,128]{2,1,0:T(8,128)S(1)} collective-permute-done((f32[2,32,128]{2,1,0:T(8,128)S(1)}, f32[2,32,128]{2,1,0:T(8,128)S(1)}, u32[]{:S(2)}, u32[]{:S(2)}) %collective-permute-start.11) | collective-permute-done | bytes 32800 | tf_op jit(solution)/shard_map/ppermute | solution.py:714
  40.3 0.6 %shard_map.121 = f32[2,32,128]{2,1,0:T(8,128)} custom-call(f32[2,32,128]{2,1,0:T(8,128)S(1)} %get-tuple-element.81.kept, f32[2,32,128]{2,1,0:T(8,128)S(1)} %collective-permute-done.11.got), custom_call_target="tpu_custom_call" | custom-call | flops 1000000 | bytes 98304 | tf_op jit(solution)/shard_map/pallas_call | solution.py:616
  (1 shorter events, 0.0 us)
Async XLA Ops:
  2.3 4.9 %collective-permute-start = (f32[224,128]{1,0:T(8,128)S(1)}, f32[224,128]{1,0:T(8,128)S(1)}, u32[]{:S(2)}, u32[]{:S(2)}) collective-permute-start(f32[224,128]{1,0:T(8,128)S(1)} %get-tuple-element.52), channel_id=1, source_target_pairs={{4,8},{0,1},{12,13},{5,9},{6,10},{2,3},{14,15},{7,11},{8,4},{1,0},... | collective-permute-start | bytes 344072 | tf_op jit(solution)/shard_map/ppermute | solution.py:677
  3.9 3.2 %collective-permute-start.1 = (f32[224,128]{1,0:T(8,128)S(1)}, f32[224,128]{1,0:T(8,128)S(1)}, u32[]{:S(2)}, u32[]{:S(2)}) collective-permute-start(f32[224,128]{1,0:T(8,128)S(1)} %get-tuple-element.53), channel_id=1, source_target_pairs={{0,4},{8,12},{4,0},{12,8},{1,5},{9,13},{5,1},{13,9},{2,6},{10,14},... | collective-permute-start | bytes 344072 | tf_op jit(solution)/shard_map/ppermute | solution.py:678
  5.1 0.7 %copy-start = (s32[3]{0:T(128)S(1)}, s32[3]{0:T(128)}, u32[]{:S(2)}) copy-start(s32[3]{0:T(128)} %pml.1) | copy-start | bytes 40
  5.8 13.4 %copy-start.1 = (s32[8]{0:T(128)S(1)}, s32[8]{0:T(128)}, u32[]{:S(2)}) copy-start(s32[8]{0:T(128)} %layer.1) | copy-start | bytes 100
  7.4 6.5 %collective-permute-start.2 = (f32[2,40,128]{2,1,0:T(8,128)S(1)}, f32[2,40,128]{2,1,0:T(8,128)S(1)}, u32[]{:S(2)}, u32[]{:S(2)}) collective-permute-start(f32[2,40,128]{2,1,0:T(8,128)S(1)} %get-tuple-element.56), channel_id=1, source_target_pairs={{0,1},{2,3},{1,0},{3,2},{4,5},{6,7},{5,4},{7,6},{8,9},{10,11},{9,8... | collective-permute-start | bytes 122888 | tf_op jit(solution)/shard_map/ppermute | solution.py:687
  9.1 4.9 %collective-permute-start.3 = (f32[2,40,128]{2,1,0:T(8,128)S(1)}, f32[2,40,128]{2,1,0:T(8,128)S(1)}, u32[]{:S(2)}, u32[]{:S(2)}) collective-permute-start(f32[2,40,128]{2,1,0:T(8,128)S(1)} %get-tuple-element.57), channel_id=1, source_target_pairs={{1,2},{0,4},{3,7},{5,6},{9,10},{8,12},{11,15},{13,14},{2,1},{4,0},... | collective-permute-start | bytes 122888 | tf_op jit(solution)/shard_map/ppermute | solution.py:688
  9.3 12.0 %collective-permute-start.4 = (f32[368,128]{1,0:T(8,128)S(1)}, f32[368,128]{1,0:T(8,128)S(1)}, u32[]{:S(2)}, u32[]{:S(2)}) collective-permute-start(f32[368,128]{1,0:T(8,128)S(1)} %get-tuple-element.65), channel_id=1, source_target_pairs={{16,32},{48,64},{80,96},{0,4},{112,116},{20,36},{52,68},{84,100},{... | collective-permute-start | bytes 565256 | tf_op jit(solution)/shard_map/ppermute | solution.py:686
  9.9 13.1 %collective-permute-start.5 = (f32[368,128]{1,0:T(8,128)S(1)}, f32[368,128]{1,0:T(8,128)S(1)}, u32[]{:S(2)}, u32[]{:S(2)}) collective-permute-start(f32[368,128]{1,0:T(8,128)S(1)} %get-tuple-element.66), channel_id=1, source_target_pairs={{0,16},{32,48},{64,80},{96,112},{16,0},{48,32},{80,64},{112,96},{1... | collective-permute-start | bytes 565256 | tf_op jit(solution)/shard_map/ppermute | solution.py:685
  14.6 8.6 %collective-permute-start.6 = (f32[40,128]{1,0:T(8,128)S(1)}, f32[40,128]{1,0:T(8,128)S(1)}, u32[]{:S(2)}, u32[]{:S(2)}) collective-permute-start(f32[40,128]{1,0:T(8,128)S(1)} %get-tuple-element.75), channel_id=1, source_target_pairs={{16,32},{48,64},{80,96},{0,4},{112,116},{20,36},{52,68},{84,100},{... | collective-permute-start | bytes 61448 | tf_op jit(solution)/shard_map/ppermute | solution.py:693
  14.6 8.6 %collective-permute-start.7 = (f32[40,128]{1,0:T(8,128)S(1)}, f32[40,128]{1,0:T(8,128)S(1)}, u32[]{:S(2)}, u32[]{:S(2)}) collective-permute-start(f32[40,128]{1,0:T(8,128)S(1)} %get-tuple-element.76), channel_id=1, source_target_pairs={{0,16},{32,48},{64,80},{96,112},{16,0},{48,32},{80,64},{112,96},{1... | collective-permute-start | bytes 61448 | tf_op jit(solution)/shard_map/ppermute | solution.py:692
  24.7 6.2 %collective-permute-start.8 = (f32[4,32,128]{2,1,0:T(8,128)S(1)}, f32[4,32,128]{2,1,0:T(8,128)S(1)}, u32[]{:S(2)}, u32[]{:S(2)}) collective-permute-start(f32[4,32,128]{2,1,0:T(8,128)S(1)} %get-tuple-element.78), channel_id=1, source_target_pairs={{0,64},{16,80},{32,96},{48,112},{64,0},{80,16},{96,32},{112,48},{1... | collective-permute-start | bytes 196616 | tf_op jit(solution)/shard_map/ppermute | solution.py:712
  28.6 4.3 %collective-permute-start.9 = (f32[4,32,128]{2,1,0:T(8,128)S(1)}, f32[4,32,128]{2,1,0:T(8,128)S(1)}, u32[]{:S(2)}, u32[]{:S(2)}) collective-permute-start(f32[4,32,128]{2,1,0:T(8,128)S(1)} %get-tuple-element.79), channel_id=1, source_target_pairs={{0,32},{16,48},{32,0},{48,16},{64,96},{80,112},{96,64},{112,80},{1... | collective-permute-start | bytes 196616 | tf_op jit(solution)/shard_map/ppermute | solution.py:712
  29.3 5.5 %collective-permute-start.10 = (f32[4,32,128]{2,1,0:T(8,128)S(1)}, f32[4,32,128]{2,1,0:T(8,128)S(1)}, u32[]{:S(2)}, u32[]{:S(2)}) collective-permute-start(f32[4,32,128]{2,1,0:T(8,128)S(1)} %get-tuple-element.80), channel_id=1, source_target_pairs={{0,96},{16,112},{32,64},{48,80},{64,32},{80,48},{96,0},{112,16},{1... | collective-permute-start | bytes 196616 | tf_op jit(solution)/shard_map/ppermute | solution.py:712
  34.8 5.5 %collective-permute-start.11 = (f32[2,32,128]{2,1,0:T(8,128)S(1)}, f32[2,32,128]{2,1,0:T(8,128)S(1)}, u32[]{:S(2)}, u32[]{:S(2)}) collective-permute-start(f32[2,32,128]{2,1,0:T(8,128)S(1)} %get-tuple-element.82), channel_id=1, source_target_pairs={{0,16},{16,0},{32,48},{48,32},{64,80},{80,64},{96,112},{112,96},{1... | collective-permute-start | bytes 98312 | tf_op jit(solution)/shard_map/ppermute | solution.py:714
